TPU v7x, 32 devices: a whole 2x2x4 slice. The times are simulated.
32 devices in a mesh: patch: 4 (over z), uly: 2 (over y), rep: 4 (over x, core).
Axes of the slice: x: 2, y: 2, z: 4, core: 2. Of those that a mesh axis runs over, the one named last changes fastest.
Arguments:
- queries: bfloat16 [512, 3072], P(('rep', 'patch', 'uly')), parts along dimension 0, may hold values from -130 to 130
- stale_kv: bfloat16 [512, 2, 3072], P('rep', None, 'uly'), parts along dimension 0, may hold values from -10 to 10
- codes: int32 [512, 2, 3072], P(('rep', 'patch', 'uly')), parts along dimension 0, may hold values from -127 to 127
- exps: int32 [512, 2, 24], P(('rep', 'patch', 'uly')), parts along dimension 0, may hold values from -10 to -6
Outputs:
- mixed: bfloat16 [512, 3072], P(('rep', 'patch', 'uly')), parts along dimension 0
There are 4 independent parts, one for each index of `rep`. A program takes and returns all parts, laid end to end along the dimension named above; each array names one. Nothing has to cross between parts.
All inputs are finite; a program needn't handle non-finite values.
Results may differ from a plain program's by a relative error of at most 0.0076.
Values may be sent and summed in bfloat16 or wider, within the bound.
No kernel may reach another device: no remote copies, remote signals or barrier semaphores. Data moves between devices by JAX's collectives and lax.ppermute only.
A program may use at most 128 MiB of HBM per device.

v0:
```python
import math

import jax
import jax.numpy as jnp
from jax import lax
from jax.sharding import PartitionSpec as P

HEAD_DIM = 128
SCALE_BLOCK = 128


def decode(codes, exps):
    num_rows = codes.shape[0]
    num_blocks = exps.shape[2]
    scaled = (
        codes.astype(jnp.float32).reshape(num_rows, 2, num_blocks, SCALE_BLOCK)
        * jnp.exp2(exps.astype(jnp.float32))[..., None]
    )
    return scaled.reshape(num_rows, 2, num_blocks * SCALE_BLOCK).astype(jnp.bfloat16)


def refresh(stale_part, resid_part):
    return (stale_part.astype(jnp.float32) + resid_part.astype(jnp.float32)).astype(jnp.bfloat16)


def column_block(rows, head):
    return rows[:, head * HEAD_DIM : (head + 1) * HEAD_DIM]


def head_scores(query_rows, key_rows, head):
    scores = lax.dot_general(
        column_block(query_rows, head),
        column_block(key_rows, head),
        (((1,), (1,)), ((), ())),
        preferred_element_type=jnp.float32,
    )
    return scores * (1.0 / math.sqrt(HEAD_DIM))


def weigh_values(weights, value_rows, head):
    return jnp.dot(
        weights.astype(jnp.bfloat16),
        column_block(value_rows, head),
        preferred_element_type=jnp.float32,
    )


def attend_whole(query_rows, kv_rows):
    head_count = query_rows.shape[1] // HEAD_DIM
    key_rows = kv_rows[:, 0]
    value_rows = kv_rows[:, 1]
    outputs = []
    for head in range(head_count):
        scores = head_scores(query_rows, key_rows, head)
        row_max = jnp.max(scores, axis=1, keepdims=True)
        weights = jnp.exp(scores - row_max)
        totals = jnp.sum(weights, axis=1, keepdims=True)
        outputs.append(weigh_values(weights, value_rows, head) / totals)
    return jnp.concatenate(outputs, axis=1).astype(jnp.bfloat16)


def on_device(queries, stale_kv, codes, exps):
    residual = decode(codes, exps)
    query_rows = lax.all_to_all(queries, "uly", split_axis=1, concat_axis=0, tiled=True)
    gathered = lax.all_gather(residual, "patch", axis=0, tiled=True)
    patch_count = lax.axis_size("patch")
    blocked = gathered.reshape(patch_count, residual.shape[0], 2, residual.shape[2])
    spread = lax.all_to_all(blocked, "uly", split_axis=3, concat_axis=1, tiled=True)
    all_resid = spread.reshape(stale_kv.shape)
    result = attend_whole(query_rows, refresh(stale_kv, all_resid))
    return lax.all_to_all(result, "uly", split_axis=0, concat_axis=1, tiled=True)


def solution(mesh):
    return jax.shard_map(
        on_device,
        mesh=mesh,
        in_specs=(
            P(("rep", "patch", "uly"), None),
            P("rep", None, "uly"),
            P(("rep", "patch", "uly"), None, None),
            P(("rep", "patch", "uly"), None, None),
        ),
        out_specs=P(("rep", "patch", "uly"), None),
        check_vma=False,
    )
```

profile of v0, /device:TPU:0, one launch (start us, length us, event | category | flops | bytes accessed | tf_op | source)
XLA Modules:
  0.0 95.3 jit_solution(12198869564282904742)
XLA Ops:
  0.0 0.7 multiply_exponential_fusion
  0.9 0.2 mul.60
  1.1 1.2 %multiply_convert_fusion = bf16[16,2,3072]{2,1,0:T(2,128)(2,1)S(1)} fusion(f32[16,2,3072]{2,1,0:T(2,128)S(1)} %mul.60, s32[16,2,3072]{2,1,0:T(2,128)} %param.6), kind=kLoop, calls=%fused_computation.40 | loop fusion | flops 294912 | bytes 983040 | tf_op jit(solution)/shard_map/convert_element_type | solution.py:19
  2.3 21.3 %all_gather.3 = bf16[64,2,3072]{2,1,0:T(2,128)(2,1)S(1)} all-gather(bf16[16,2,3072]{2,1,0:T(2,128)(2,1)S(1)} %multiply_convert_fusion), channel_id=1, replica_groups=mesh['patch'=4,'uly'=2,'rep'=4] {'patch'}, dimensions={0}, use_global_device_ids=true | all-gather | bytes 983040 | tf_op jit(solution)/shard_map/all_gather | solution.py:65
  23.6 10.4 %copy.25 = bf16[4,16,2,3072]{1,2,0,3:T(2,128)(2,1)} copy(bf16[4,16,2,3072]{3,2,1,0:T(2,128)(2,1)S(1)} %bitcast.43) | data formatting | bytes 1572864 | tf_op jit(solution)/shard_map/reshape | solution.py:67
  34.0 9.1 %reshape.70 = bf16[2,2,98304]{2,1,0:T(2,128)(2,1)} reshape(bf16[3072,4,2,16]{3,2,1,0:T(2,128)(2,1)} %bitcast.40) | data formatting | bytes 1572864
  43.2 3.7 %all-to-all-start = ((bf16[2,2,98304]{2,1,0:T(2,128)(2,1)}), bf16[2,2,98304]{2,1,0:T(2,128)(2,1)S(1)}, u32[]{:S(2)}, u32[]{:S(2)}) async-start(bf16[2,2,98304]{2,1,0:T(2,128)(2,1)} %reshape.70), calls=%async_computation | async-start | bytes 1572864 | tf_op jit(solution)/shard_map/all_to_all | solution.py:68
  46.9 0.6 copy.34
  47.5 7.7 %all-to-all-done = bf16[2,2,98304]{2,1,0:T(2,128)(2,1)S(1)} async-done(((bf16[2,2,98304]{2,1,0:T(2,128)(2,1)}), bf16[2,2,98304]{2,1,0:T(2,128)(2,1)S(1)}, u32[]{:S(2)}, u32[]{:S(2)}) %all-to-all-start) | async-done | bytes 786464 | tf_op jit(solution)/shard_map/all_to_all | solution.py:68
  55.3 3.3 %all-to-all-start.1 = ((bf16[16,2,1536]{2,0,1:T(8,128)(2,1)}), bf16[16,2,1536]{2,0,1:T(8,128)(2,1)S(1)}, u32[]{:S(2)}, u32[]{:S(2)}) async-start(bf16[16,2,1536]{2,0,1:T(8,128)(2,1)} %bitcast.39), calls=%async_computation.1 | async-start | bytes 196608 | tf_op jit(solution)/shard_map/all_to_all | solution.py:64
  58.6 5.9 %reshape.71 = bf16[3072,4,2,16]{3,2,1,0:T(2,128)(2,1)} reshape(bf16[2,2,98304]{2,1,0:T(2,128)(2,1)S(1)} %all-to-all-done) | data formatting | bytes 1572864
  64.5 11.9 %copy.26 = bf16[4,16,2,3072]{3,1,2,0:T(8,128)(2,1)S(1)} copy(bf16[4,16,2,3072]{1,2,0,3:T(2,128)(2,1)} %bitcast.41) | data formatting | bytes 1572864 | tf_op jit(solution)/shard_map/all_to_all | solution.py:68
  76.4 1.5 %reshape.69 = f32[4,16,2,2,1536]{4,3,1,2,0:T(2,128)S(1)} reshape(bf16[4,16,2,3072]{3,1,2,0:T(8,128)(2,1)S(1)} %copy.26) | data formatting | bytes 2359296 | tf_op jit(solution)/shard_map/convert_element_type | solution.py:23
  78.0 0.3 copy.27
  78.2 0.8 copy-done
  79.3 0.2 fusion.98
  79.6 0.3 fusion.97
  79.8 0.3 fusion.99
  80.1 0.3 fusion.100
  80.4 0.3 fusion.101
  80.6 0.3 fusion.102
  80.9 0.3 fusion.103
  81.1 0.3 fusion.104
  81.4 0.3 fusion.105
  81.7 0.3 fusion.106
  81.9 0.3 fusion.107
  82.2 0.3 fusion.108
  82.5 0.2 fusion.39
  82.7 0.2 fusion.2
  82.9 0.2 fusion.37
  83.0 0.2 fusion.1
  83.3 0.2 fusion.41
  83.4 0.2 fusion.3
  83.8 0.2 fusion.4
  84.2 0.2 fusion.5
  84.4 0.2 fusion.47
  84.6 0.2 fusion.6
  85.0 0.2 fusion.7
  85.2 0.2 fusion.51
  85.4 0.2 fusion.8
  85.6 0.2 fusion.53
  85.8 0.2 fusion.9
  86.0 0.2 fusion.55
  86.2 0.2 fusion.10
  86.6 0.2 fusion.11
  87.0 0.2 fusion.12
  87.3 7.4 %all_to_all.44 = bf16[2,16,1536]{2,1,0:T(8,128)(2,1)S(1)} all-to-all(bf16[2,16,1536]{2,1,0:T(8,128)(2,1)S(1)} %constant_dynamic-update-slice_fusion), channel_id=1, replica_groups=mesh['patch'=4,'uly'=2,'rep'=4] {'uly'}, dimensions={0} | all-to-all | bytes 196608 | tf_op jit(solution)/shard_map/all_to_all | solution.py:71
  94.7 0.6 copy.31
  (24 shorter events, 1.4 us)
Async XLA Ops:
  43.2 3.7 %copy-start.1 = (bf16[16,3072]{1,0:T(8,128)(2,1)S(1)}, bf16[16,3072]{1,0:T(8,128)(2,1)}, u32[]{:S(2)}) copy-start(bf16[16,3072]{1,0:T(8,128)(2,1)} %param.4) | copy-start | bytes 294916
  43.2 12.1 %all-to-all-start = ((bf16[2,2,98304]{2,1,0:T(2,128)(2,1)}), bf16[2,2,98304]{2,1,0:T(2,128)(2,1)S(1)}, u32[]{:S(2)}, u32[]{:S(2)}) async-start(bf16[2,2,98304]{2,1,0:T(2,128)(2,1)} %reshape.70), calls=%async_computation | async-start | bytes 1572864 | tf_op jit(solution)/shard_map/all_to_all | solution.py:68
  55.3 24.0 %all-to-all-start.1 = ((bf16[16,2,1536]{2,0,1:T(8,128)(2,1)}), bf16[16,2,1536]{2,0,1:T(8,128)(2,1)S(1)}, u32[]{:S(2)}, u32[]{:S(2)}) async-start(bf16[16,2,1536]{2,0,1:T(8,128)(2,1)} %bitcast.39), calls=%async_computation.1 | async-start | bytes 196608 | tf_op jit(solution)/shard_map/all_to_all | solution.py:64
  77.9 1.1 %copy-start = (bf16[128,2,1536]{2,1,0:T(2,128)(2,1)S(1)}, bf16[128,2,1536]{2,1,0:T(2,128)(2,1)}, u32[]{:S(2)}) copy-start(bf16[128,2,1536]{2,1,0:T(2,128)(2,1)} %param.5) | copy-start | bytes 2359300
where the time goes:
time: 96 us; the launch traced here: 95.3 us
  local copies, waits for them, and re-layouts  41.8 us (44%)
  blocking collectives  28.6 us (30%)
  waiting for transfers between devices  7.75 us (8%)
  starting transfers between devices  7 us (7%)
  matrix products  5.54 us (6%)
  other arithmetic  4.29 us (4%)
    all_gather x1, blocking collectives, on_device(): gathered = lax.all_gather(residual, 'patch', axis=0, tiled=True)  21.3 us
    unnamed x17, local copies, waits for them, and re-layouts  16 us
    all_to_all x1, local copies, waits for them, and re-layouts, on_device(): lax.all_to_all(blocked, 'uly', split_axis=3, concat_axis=1, tiled=True)  11.9 us
    reshape x1, local copies, waits for them, and re-layouts, on_device(): gathered.reshape(patch_count, residual.shape[0], 2, residual.shape[2])  10.4 us
    all_to_all x1, waiting for transfers between devices, on_device(): lax.all_to_all(blocked, 'uly', split_axis=3, concat_axis=1, tiled=True)  7.74 us
    all_to_all x1, blocking collectives, on_device(): lax.all_to_all(result, 'uly', split_axis=0, concat_axis=1, tiled=True)  7.35 us
    all_to_all x1, starting transfers between devices, on_device(): lax.all_to_all(blocked, 'uly', split_axis=3, concat_axis=1, tiled=True)  3.67 us
    all_to_all x1, starting transfers between devices, on_device(): lax.all_to_all(queries, 'uly', split_axis=1, concat_axis=0, tiled=True)  3.34 us
  transfers between devices with their start and end apart: 2, of which 1 were waited for; matrix products, arithmetic and copies ran while one was open for 21% of the time, Pallas kernels for 0%

commit v1 on v0

--- a/solution.py
+++ b/solution.py
@@ -1,8 +1,10 @@
+import functools
 import math
 
 import jax
 import jax.numpy as jnp
 from jax import lax
+from jax.experimental import pallas as pl
 from jax.sharding import PartitionSpec as P
 
 HEAD_DIM = 128
@@ -59,7 +61,7 @@
     return jnp.concatenate(outputs, axis=1).astype(jnp.bfloat16)
 
 
-def on_device(queries, stale_kv, codes, exps):
+def attend_gathered(queries, stale_kv, codes, exps):
     residual = decode(codes, exps)
     query_rows = lax.all_to_all(queries, "uly", split_axis=1, concat_axis=0, tiled=True)
     gathered = lax.all_gather(residual, "patch", axis=0, tiled=True)
@@ -69,6 +71,79 @@
     all_resid = spread.reshape(stale_kv.shape)
     result = attend_whole(query_rows, refresh(stale_kv, all_resid))
     return lax.all_to_all(result, "uly", split_axis=0, concat_axis=1, tiled=True)
+
+
+def pack_kernel(queries_ref, codes_ref, exps_ref, packed_ref, *, patch_count, uly_count):
+    width = packed_ref.shape[2]
+    rows = queries_ref.shape[0]
+    for patch in range(patch_count):
+        for uly in range(uly_count):
+            dest = patch * uly_count + uly
+            start = (uly * patch_count + patch) * width
+            packed_ref[dest, 0:rows, :] = queries_ref[:, start : start + width]
+    for kind in range(2):
+        scale = jnp.exp2(exps_ref[:, kind, :].astype(jnp.float32))
+        for patch in range(patch_count):
+            for uly in range(uly_count):
+                dest = patch * uly_count + uly
+                start = (uly * patch_count + patch) * width
+                for offset in range(0, width, SCALE_BLOCK):
+                    block = (start + offset) // SCALE_BLOCK
+                    values = codes_ref[:, kind, start + offset : start + offset + SCALE_BLOCK].astype(jnp.float32)
+                    decoded = values * scale[:, block : block + 1]
+                    packed_ref[dest, (kind + 1) * rows : (kind + 2) * rows, offset : offset + SCALE_BLOCK] = decoded.astype(
+                        jnp.bfloat16
+                    )
+
+
+def attend_kernel(blocks_ref, stale_ref, mixed_ref):
+    sources, rows, width = mixed_ref.shape
+    tokens = sources * rows
+
+    def received(kind):
+        return blocks_ref[:, kind * rows : (kind + 1) * rows, :].reshape(tokens, width)
+
+    query_rows = received(0)
+    key_rows = refresh(stale_ref[0], received(1))
+    value_rows = refresh(stale_ref[1], received(2))
+    for head in range(width // HEAD_DIM):
+        scores = head_scores(query_rows, key_rows, head)
+        weights = jnp.exp(scores - jnp.max(scores, axis=1, keepdims=True))
+        totals = jnp.sum(weights, axis=1, keepdims=True)
+        result = weigh_values(weights, value_rows, head) / totals
+        mixed_ref[:, :, head * HEAD_DIM : (head + 1) * HEAD_DIM] = result.astype(jnp.bfloat16).reshape(sources, rows, HEAD_DIM)
+
+
+def attend_split_heads(queries, stale_kv, codes, exps):
+    patch_count = lax.axis_size("patch")
+    uly_count = lax.axis_size("uly")
+    peers = patch_count * uly_count
+    rows, model_width = queries.shape
+    tokens = stale_kv.shape[0]
+    width = model_width // peers
+    both = ("patch", "uly")
+    packed = pl.pallas_call(
+        functools.partial(pack_kernel, patch_count=patch_count, uly_count=uly_count),
+        out_shape=jax.ShapeDtypeStruct((peers, 3 * rows, width), jnp.bfloat16),
+    )(queries, codes, exps)
+    blocks = lax.all_to_all(packed, both, split_axis=0, concat_axis=0, tiled=True)
+    own_stale = lax.dynamic_slice(stale_kv, (0, 0, lax.axis_index("patch") * width), (tokens, 2, width))
+    own_stale = jnp.swapaxes(own_stale, 0, 1)
+    mixed = pl.pallas_call(
+        attend_kernel,
+        out_shape=jax.ShapeDtypeStruct((peers, rows, width), jnp.bfloat16),
+    )(blocks, own_stale)
+    back = lax.all_to_all(mixed, both, split_axis=0, concat_axis=0, tiled=True)
+    return jnp.concatenate(
+        [back[patch * uly_count + uly] for uly in range(uly_count) for patch in range(patch_count)], axis=1
+    )
+
+
+def on_device(queries, stale_kv, codes, exps):
+    own_heads = stale_kv.shape[2] // HEAD_DIM
+    if own_heads % lax.axis_size("patch") == 0:
+        return attend_split_heads(queries, stale_kv, codes, exps)
+    return attend_gathered(queries, stale_kv, codes, exps)
 
 
 def solution(mesh):

time: 96 us -> 35.2 us (0.37)
  local copies, waits for them, and re-layouts: 41.8 us -> 2.84 us
  blocking collectives: 28.6 us -> 10.7 us
  matrix products: 5.54 us -> 0 us
  Pallas kernels: 0 us -> 5.27 us
  other arithmetic: 4.29 us -> 0 us
  waiting for transfers between devices: 7.75 us -> 8.77 us
    all_gather x1 -> x0, blocking collectives: 21.3 us -> none  [on_device(): gathered = lax.all_gather(residual, 'patch', axis=0, tiled=True)]
    unnamed x17 -> x14, local copies, waits for them, and re-layouts: 16 us -> 2.1 us
    all_to_all x3 -> x0, local copies, waits for them, and re-layouts: 13.2 us -> none  [the longest x1 11.9 us: on_device(): lax.all_to_all(blocked, 'uly', split_axis=3, concat_axis=1, tiled=True)]
    reshape x1 -> x0, local copies, waits for them, and re-layouts: 10.4 us -> none  [on_device(): gathered.reshape(patch_count, residual.shape[0], 2, residual.shape[2])]
    dot_general x24 -> x0, matrix products: 5.54 us -> none  [the longest x12 3.09 us: head_scores(): lax.dot_general(column_block(query_rows, head), column_block(key_rows, he...]
    pallas_call x0 -> x2, Pallas kernels: none -> 5.27 us  [the longest x1 2.77 us: attend_split_heads(): pl.pallas_call(functools.partial(pack_kernel, patch_count=patch_count, ul...]
    all_to_all x1, blocking collectives: 7.35 us -> 10.7 us  [attend_split_heads(): back = lax.all_to_all(mixed, both, split_axis=0, concat_axis=0, tiled=True)]
    reduce_sum x12 -> x0, other arithmetic: 2.19 us -> none  [attend_whole(): totals = jnp.sum(weights, axis=1, keepdims=True)]
  transfers between devices with their start and end apart: 2 -> 1, of which waited for: 1 -> 1; matrix products, arithmetic and copies ran while one was open for 21% -> 2% of each run, Pallas kernels for 0% -> 0%
where the time goes in v1:
time: 35.2 us; the launch traced here: 34.9 us
  blocking collectives  10.7 us (30%)
  waiting for transfers between devices  8.77 us (25%)
  starting transfers between devices  7.28 us (21%)
  Pallas kernels  5.27 us (15%)
  local copies, waits for them, and re-layouts  2.84 us (8%)
    all_to_all x1, blocking collectives, attend_split_heads(): back = lax.all_to_all(mixed, both, split_axis=0, concat_axis=0, tiled=True)  10.7 us
    all_to_all x1, waiting for transfers between devices, attend_split_heads(): lax.all_to_all(packed, both, split_axis=0, concat_axis=0, tiled=True)  8.77 us
    all_to_all x1, starting transfers between devices, attend_split_heads(): lax.all_to_all(packed, both, split_axis=0, concat_axis=0, tiled=True)  7.28 us
    pallas_call x1, Pallas kernels, attend_split_heads(): pl.pallas_call(functools.partial(pack_kernel, patch_count=patch_count, ul...  2.77 us
    pallas_call x1, Pallas kernels, attend_split_heads(): pl.pallas_call(attend_kernel, out_shape=jax.ShapeDtypeStruct((peers, rows...  2.5 us
    unnamed x14, local copies, waits for them, and re-layouts  2.1 us
  transfers between devices with their start and end apart: 1, of which 1 were waited for; matrix products, arithmetic and copies ran while one was open for 2% of the time, Pallas kernels for 0%

profile of v1, /device:TPU:0, one launch (start us, length us, event | category | flops | bytes accessed | tf_op | source)
XLA Modules:
  0.0 34.9 jit_solution(1486319500254923795)
XLA Ops:
  0.0 0.0 copy-start
  0.0 2.8 %shard_map.46 = bf16[8,48,384]{2,1,0:T(8,128)(2,1)} custom-call(bf16[16,3072]{1,0:T(8,128)(2,1)} %queries_ref.1, s32[16,2,3072]{2,1,0:T(2,128)} %codes_ref.1, s32[16,2,24]{2,1,0:T(2,128)} %exps_ref.1), custom_call_target="tpu_custom_call" | custom-call | tf_op jit(solution)/shard_map/pallas_call | solution.py:125
  2.8 7.3 %all-to-all-start = ((bf16[8,48,384]{2,1,0:T(8,128)(2,1)}), bf16[8,48,384]{2,1,0:T(8,128)(2,1)S(1)}, u32[]{:S(2)}, u32[]{:S(2)}) async-start(bf16[8,48,384]{2,1,0:T(8,128)(2,1)} %shard_map.46), calls=%async_computation | async-start | bytes 589824 | tf_op jit(solution)/shard_map/all_to_all | solution.py:129
  10.1 0.0 copy-done
  10.1 0.1 constant_dynamic-slice_fusion
  10.2 0.7 %copy.8 = bf16[128,2,384]{2,0,1:T(8,128)(2,1)} copy(bf16[128,2,384]{2,1,0:T(2,128)(2,1)S(1)} %constant_dynamic-slice_fusion) | data formatting | bytes 393216
  10.9 8.8 %all-to-all-done.blocks_ref = bf16[8,48,384]{2,1,0:T(8,128)(2,1)S(1)} async-done(((bf16[8,48,384]{2,1,0:T(8,128)(2,1)}), bf16[8,48,384]{2,1,0:T(8,128)(2,1)S(1)}, u32[]{:S(2)}, u32[]{:S(2)}) %all-to-all-start) | async-done | bytes 294944 | tf_op jit(solution)/shard_map/all_to_all | solution.py:129
  19.7 0.0 copy-start.1
  19.7 0.7 %copy-done.1 = bf16[8,48,384]{2,1,0:T(8,128)(2,1)} copy-done((bf16[8,48,384]{2,1,0:T(8,128)(2,1)}, bf16[8,48,384]{2,1,0:T(8,128)(2,1)S(1)}, u32[]{:S(2)}) %copy-start.1) | copy-done | bytes 294936
  20.4 2.5 %shard_map.47 = bf16[8,16,384]{2,1,0:T(8,128)(2,1)} custom-call(bf16[8,48,384]{2,1,0:T(8,128)(2,1)} %copy-done.1, bf16[2,128,384]{2,1,0:T(8,128)(2,1)} %bitcast.35), custom_call_target="tpu_custom_call" | custom-call | tf_op jit(solution)/shard_map/pallas_call | solution.py:132
  22.9 10.7 %all_to_all.10 = bf16[8,16,384]{2,1,0:T(8,128)(2,1)S(1)} all-to-all(bf16[8,16,384]{2,1,0:T(8,128)(2,1)} %shard_map.47), channel_id=1, replica_groups=mesh['patch'=4,'uly'=2,'rep'=4] {'patch','uly'}, dimensions={0} | all-to-all | bytes 196608 | tf_op jit(solution)/shard_map/all_to_all | solution.py:136
  33.7 0.0 copy-start.2
  33.7 0.6 %copy-done.2 = bf16[16,3072]{1,0:T(8,128)(2,1)} copy-done((bf16[16,3072]{1,0:T(8,128)(2,1)}, bf16[16,3072]{1,0:T(8,128)(2,1)S(1)}, u32[]{:S(2)}) %copy-start.2) | copy-done | bytes 98328
  34.3 0.6 %constant_dynamic-update-slice_fusion = bf16[16,3072]{1,0:T(8,128)(2,1)} fusion(bf16[16,3072]{1,0:T(8,128)(2,1)} %copy-done.2, bf16[8,16,384]{2,1,0:T(8,128)(2,1)S(1)} %all_to_all.10), kind=kLoop, calls=%fused_computation.1 | loop fusion | bytes 24576 | tf_op jit(solution)/shard_map/concatenate | solution.py:137
  (7 shorter events, 0.1 us)
Async XLA Ops:
  0.0 10.1 %copy-start = (bf16[128,2,1536]{2,1,0:T(2,128)(2,1)S(1)}, bf16[128,2,1536]{2,1,0:T(2,128)(2,1)}, u32[]{:S(2)}) copy-start(bf16[128,2,1536]{2,1,0:T(2,128)(2,1)} %param.5) | copy-start | bytes 2359300
  2.8 16.9 %all-to-all-start = ((bf16[8,48,384]{2,1,0:T(8,128)(2,1)}), bf16[8,48,384]{2,1,0:T(8,128)(2,1)S(1)}, u32[]{:S(2)}, u32[]{:S(2)}) async-start(bf16[8,48,384]{2,1,0:T(8,128)(2,1)} %shard_map.46), calls=%async_computation | async-start | bytes 589824 | tf_op jit(solution)/shard_map/all_to_all | solution.py:129
  19.7 0.7 %copy-start.1 = (bf16[8,48,384]{2,1,0:T(8,128)(2,1)}, bf16[8,48,384]{2,1,0:T(8,128)(2,1)S(1)}, u32[]{:S(2)}) copy-start(bf16[8,48,384]{2,1,0:T(8,128)(2,1)S(1)} %all-to-all-done.blocks_ref) | copy-start | bytes 884740
  33.7 0.6 %copy-start.2 = (bf16[16,3072]{1,0:T(8,128)(2,1)}, bf16[16,3072]{1,0:T(8,128)(2,1)S(1)}, u32[]{:S(2)}) copy-start(bf16[16,3072]{1,0:T(8,128)(2,1)S(1)} %constant_dynamic-update-slice_fusion.1) | copy-start | bytes 294916

commit v2 on v0

--- a/solution.py
+++ b/solution.py
@@ -1,12 +1,18 @@
+import functools
 import math
 
 import jax
 import jax.numpy as jnp
 from jax import lax
+from jax.experimental import pallas as pl
+from jax.experimental.pallas import tpu as pltpu
 from jax.sharding import PartitionSpec as P
 
 HEAD_DIM = 128
 SCALE_BLOCK = 128
+CODE_CHUNKS = 4
+KERNEL_VMEM = 8 << 20
+PACK_VMEM = 8 << 20
 
 
 def decode(codes, exps):
@@ -59,7 +65,7 @@
     return jnp.concatenate(outputs, axis=1).astype(jnp.bfloat16)
 
 
-def on_device(queries, stale_kv, codes, exps):
+def attend_gathered(queries, stale_kv, codes, exps):
     residual = decode(codes, exps)
     query_rows = lax.all_to_all(queries, "uly", split_axis=1, concat_axis=0, tiled=True)
     gathered = lax.all_gather(residual, "patch", axis=0, tiled=True)
@@ -69,6 +75,146 @@
     all_resid = spread.reshape(stale_kv.shape)
     result = attend_whole(query_rows, refresh(stale_kv, all_resid))
     return lax.all_to_all(result, "uly", split_axis=0, concat_axis=1, tiled=True)
+
+
+def home_column(peer, patch_count, uly_count, width):
+    return ((peer % uly_count) * patch_count + peer // uly_count) * width
+
+
+def pack_kernel(queries_hbm, codes_hbm, exps_hbm, packed_ref, queries_ref, codes_ref, exps_ref, sems, *, patch_count, uly_count):
+    width = packed_ref.shape[2]
+    rows = queries_ref.shape[0]
+    peers = patch_count * uly_count
+    fetch_exps = pltpu.make_async_copy(exps_hbm, exps_ref, sems.at[0])
+    fetch_exps.start()
+    fetch_codes = []
+    half = codes_ref.shape[2] // CODE_CHUNKS
+    for part in range(CODE_CHUNKS):
+        columns = pl.ds(part * half, half)
+        copies = [
+            pltpu.make_async_copy(codes_hbm.at[:, kind, columns], codes_ref.at[kind, :, columns], sems.at[2 + 2 * part + kind])
+            for kind in range(2)
+        ]
+        for copy in copies:
+            copy.start()
+        fetch_codes.append(copies)
+    fetch_queries = pltpu.make_async_copy(queries_hbm, queries_ref, sems.at[1])
+    fetch_queries.start()
+
+    fetch_exps.wait()
+    scales = [jnp.exp2(exps_ref[:, kind, :].astype(jnp.float32)) for kind in range(2)]
+    ready = 0
+    for peer in sorted(range(peers), key=lambda peer: home_column(peer, patch_count, uly_count, width)):
+        start = home_column(peer, patch_count, uly_count, width)
+        while ready * half < start + width:
+            for copy in fetch_codes[ready]:
+                copy.wait()
+            ready += 1
+        for kind in range(2):
+            for offset in range(0, width, SCALE_BLOCK):
+                block = (start + offset) // SCALE_BLOCK
+                values = codes_ref[kind, :, start + offset : start + offset + SCALE_BLOCK].astype(jnp.float32)
+                decoded = values * scales[kind][:, block : block + 1]
+                packed_ref[peer, (kind + 1) * rows : (kind + 2) * rows, offset : offset + SCALE_BLOCK] = decoded.astype(
+                    jnp.bfloat16
+                )
+    fetch_queries.wait()
+    for peer in range(peers):
+        start = home_column(peer, patch_count, uly_count, width)
+        packed_ref[peer, 0:rows, :] = queries_ref[:, start : start + width]
+
+
+def pack(queries, codes, exps, patch_count, uly_count):
+    rows, model_width = queries.shape
+    peers = patch_count * uly_count
+    return pl.pallas_call(
+        functools.partial(pack_kernel, patch_count=patch_count, uly_count=uly_count),
+        out_shape=jax.ShapeDtypeStruct((peers, 3 * rows, model_width // peers), jnp.bfloat16),
+        in_specs=[pl.BlockSpec(memory_space=pltpu.HBM)] * 3,
+        out_specs=pl.BlockSpec(memory_space=pltpu.VMEM),
+        scratch_shapes=[
+            pltpu.VMEM(queries.shape, queries.dtype),
+            pltpu.VMEM((2, rows, model_width), codes.dtype),
+            pltpu.VMEM(exps.shape, exps.dtype),
+            pltpu.SemaphoreType.DMA((2 + 2 * CODE_CHUNKS,)),
+        ],
+        compiler_params=pltpu.CompilerParams(vmem_limit_bytes=PACK_VMEM),
+    )(*(pltpu.with_memory_space_constraint(each, pltpu.HBM) for each in (queries, codes, exps)))
+
+
+def attend_kernel(blocks_ref, stale_ref, mixed_ref):
+    sources, rows, width = mixed_ref.shape
+    tokens = sources * rows
+    heads = range(width // HEAD_DIM)
+
+    def received(kind):
+        return blocks_ref[:, kind * rows : (kind + 1) * rows, :].reshape(tokens, width)
+
+    query_rows = received(0)
+    key_rows = refresh(stale_ref[0], received(1))
+    scores = [head_scores(query_rows, key_rows, head) for head in heads]
+    value_rows = refresh(stale_ref[1], received(2))
+    weights = [jnp.exp(each - jnp.max(each, axis=1, keepdims=True)) for each in scores]
+    sums = [weigh_values(weights[head], value_rows, head) for head in heads]
+    for head in heads:
+        result = sums[head] / jnp.sum(weights[head], axis=1, keepdims=True)
+        mixed_ref[:, :, head * HEAD_DIM : (head + 1) * HEAD_DIM] = result.astype(jnp.bfloat16).reshape(sources, rows, HEAD_DIM)
+
+
+def attend(blocks, own_stale):
+    peers, packed_rows, width = blocks.shape
+    return pl.pallas_call(
+        attend_kernel,
+        out_shape=jax.ShapeDtypeStruct((peers, packed_rows // 3, width), jnp.bfloat16),
+        in_specs=[pl.BlockSpec(memory_space=pltpu.VMEM)] * 2,
+        out_specs=pl.BlockSpec(memory_space=pltpu.VMEM),
+        compiler_params=pltpu.CompilerParams(vmem_limit_bytes=KERNEL_VMEM),
+    )(blocks, own_stale)
+
+
+def place_kernel(back_ref, mixed_hbm, sems, *, patch_count, uly_count):
+    peers, _, width = back_ref.shape
+    copies = []
+    for peer in range(peers):
+        columns = pl.ds(home_column(peer, patch_count, uly_count, width), width)
+        copies.append(pltpu.make_async_copy(back_ref.at[peer], mixed_hbm.at[:, columns], sems.at[peer]))
+        copies[-1].start()
+    for copy in copies:
+        copy.wait()
+
+
+def place(back, patch_count, uly_count):
+    peers, rows, width = back.shape
+    return pl.pallas_call(
+        functools.partial(place_kernel, patch_count=patch_count, uly_count=uly_count),
+        out_shape=jax.ShapeDtypeStruct((rows, peers * width), jnp.bfloat16),
+        in_specs=[pl.BlockSpec(memory_space=pltpu.VMEM)],
+        out_specs=pl.BlockSpec(memory_space=pltpu.HBM),
+        scratch_shapes=[pltpu.SemaphoreType.DMA((peers,))],
+        compiler_params=pltpu.CompilerParams(vmem_limit_bytes=KERNEL_VMEM),
+    )(back)
+
+
+def attend_split_heads(queries, stale_kv, codes, exps):
+    patch_count = lax.axis_size("patch")
+    uly_count = lax.axis_size("uly")
+    tokens = stale_kv.shape[0]
+    width = queries.shape[1] // (patch_count * uly_count)
+    both = ("patch", "uly")
+    packed = pack(queries, codes, exps, patch_count, uly_count)
+    own_stale = lax.dynamic_slice(stale_kv, (0, 0, lax.axis_index("patch") * width), (tokens, 2, width))
+    packed, own_stale = lax.optimization_barrier((packed, jnp.swapaxes(own_stale, 0, 1)))
+    blocks = lax.all_to_all(packed, both, split_axis=0, concat_axis=0, tiled=True)
+    mixed = attend(blocks, own_stale)
+    back = lax.all_to_all(mixed, both, split_axis=0, concat_axis=0, tiled=True)
+    return place(back, patch_count, uly_count)
+
+
+def on_device(queries, stale_kv, codes, exps):
+    own_heads = stale_kv.shape[2] // HEAD_DIM
+    if own_heads % lax.axis_size("patch") == 0:
+        return attend_split_heads(queries, stale_kv, codes, exps)
+    return attend_gathered(queries, stale_kv, codes, exps)
 
 
 def solution(mesh):

time: 96 us -> 32.1 us (0.33)
  local copies, waits for them, and re-layouts: 41.8 us -> 1.3 us
  waiting for transfers between devices: 7.75 us -> 0 us
  starting transfers between devices: 7 us -> 0 us
  matrix products: 5.54 us -> 0 us
  other arithmetic: 4.29 us -> 0 us
  Pallas kernels: 0 us -> 3.25 us
  blocking collectives: 28.6 us -> 27.2 us
    all_gather x1 -> x0, blocking collectives: 21.3 us -> none  [on_device(): gathered = lax.all_gather(residual, 'patch', axis=0, tiled=True)]
    all_to_all x1 -> x2, blocking collectives: 7.35 us -> 27.2 us  [the longest x1 17.4 us: attend_split_heads(): lax.all_to_all(packed, both, split_axis=0, concat_axis=0, tiled=True)]
    unnamed x17 -> x3, local copies, waits for them, and re-layouts: 16 us -> 1.16 us
    all_to_all x3 -> x0, local copies, waits for them, and re-layouts: 13.2 us -> none  [the longest x1 11.9 us: on_device(): lax.all_to_all(blocked, 'uly', split_axis=3, concat_axis=1, tiled=True)]
    reshape x1 -> x0, local copies, waits for them, and re-layouts: 10.4 us -> none  [on_device(): gathered.reshape(patch_count, residual.shape[0], 2, residual.shape[2])]
    all_to_all x2 -> x0, waiting for transfers between devices: 7.75 us -> none  [the longest x1 7.74 us: on_device(): lax.all_to_all(blocked, 'uly', split_axis=3, concat_axis=1, tiled=True)]
    all_to_all x2 -> x0, starting transfers between devices: 7 us -> none  [the longest x1 3.67 us: on_device(): lax.all_to_all(blocked, 'uly', split_axis=3, concat_axis=1, tiled=True)]
    dot_general x24 -> x0, matrix products: 5.54 us -> none  [the longest x12 3.09 us: head_scores(): lax.dot_general(column_block(query_rows, head), column_block(key_rows, he...]
  transfers between devices with their start and end apart: 2 -> 0, of which waited for: 1 -> 0; matrix products, arithmetic and copies ran while one was open for 21% -> 0% of each run, Pallas kernels for 0% -> 0%
where the time goes in v2:
time: 32.1 us; the launch traced here: 31.8 us
  blocking collectives  27.2 us (85%)
  Pallas kernels  3.25 us (10%)
  local copies, waits for them, and re-layouts  1.3 us (4%)
    all_to_all x1, blocking collectives, attend_split_heads(): lax.all_to_all(packed, both, split_axis=0, concat_axis=0, tiled=True)  17.4 us
    all_to_all x1, blocking collectives, attend_split_heads(): back = lax.all_to_all(mixed, both, split_axis=0, concat_axis=0, tiled=True)  9.79 us
    pallas_call x1, Pallas kernels, pack(): pl.pallas_call(functools.partial(pack_kernel, patch_count=patch_count, ul...  2.13 us
    unnamed x3, local copies, waits for them, and re-layouts  1.16 us
    pallas_call x1, Pallas kernels, place(): pl.pallas_call(functools.partial(place_kernel, patch_count=patch_count, u...  0.7 us

profile of v2, /device:TPU:0, one launch (start us, length us, event | category | flops | bytes accessed | tf_op | source)
XLA Modules:
  0.0 31.8 jit_solution(18029409347714125726)
XLA Ops:
  0.0 0.0 copy-start
  0.0 1.1 %copy-done = bf16[128,2,1536]{2,1,0:T(2,128)(2,1)S(1)} copy-done((bf16[128,2,1536]{2,1,0:T(2,128)(2,1)S(1)}, bf16[128,2,1536]{2,1,0:T(2,128)(2,1)}, u32[]{:S(2)}) %copy-start) | copy-done | bytes 786456
  1.1 0.1 constant_dynamic-slice_fusion
  1.3 2.1 %shard_map.46 = bf16[8,48,384]{2,1,0:T(8,128)(2,1)S(1)} custom-call(bf16[16,3072]{1,0:T(8,128)(2,1)} %queries_hbm.1, s32[16,2,3072]{2,1,0:T(2,128)} %codes_hbm.1, s32[16,2,24]{2,1,0:T(2,128)} %exps_hbm.1), custom_call_target="tpu_custom_call" | custom-call | tf_op jit(solution)/shard_map/pallas_call | solution.py:130
  3.5 17.4 %all_to_all.10.blocks_ref = bf16[8,48,384]{2,1,0:T(8,128)(2,1)S(1)} all-to-all(bf16[8,48,384]{2,1,0:T(8,128)(2,1)S(1)} %shard_map.46), channel_id=1, replica_groups=mesh['patch'=4,'uly'=2,'rep'=4] {'patch','uly'}, dimensions={0} | all-to-all | bytes 589824 | tf_op jit(solution)/shard_map/all_to_all | solution.py:207
  20.9 0.4 %shard_map.47 = bf16[8,16,384]{2,1,0:T(8,128)(2,1)S(1)} custom-call(bf16[8,48,384]{2,1,0:T(8,128)(2,1)S(1)} %all_to_all.10.blocks_ref, bf16[2,128,384]{2,1,0:T(8,128)(2,1)S(1)} %bitcast.3), custom_call_target="tpu_custom_call" | custom-call | tf_op jit(solution)/shard_map/pallas_call | solution.py:166
  21.3 9.8 %all_to_all.11.back_ref = bf16[8,16,384]{2,1,0:T(8,128)(2,1)S(1)} all-to-all(bf16[8,16,384]{2,1,0:T(8,128)(2,1)S(1)} %shard_map.47), channel_id=1, replica_groups=mesh['patch'=4,'uly'=2,'rep'=4] {'patch','uly'}, dimensions={0} | all-to-all | bytes 196608 | tf_op jit(solution)/shard_map/all_to_all | solution.py:209
  31.1 0.7 %shard_map.48 = bf16[16,3072]{1,0:T(8,128)(2,1)} custom-call(bf16[8,16,384]{2,1,0:T(8,128)(2,1)S(1)} %all_to_all.11.back_ref), custom_call_target="tpu_custom_call" | custom-call | tf_op jit(solution)/shard_map/pallas_call | solution.py:188
  (1 shorter events, 0.0 us)
Async XLA Ops:
  0.0 1.1 %copy-start = (bf16[128,2,1536]{2,1,0:T(2,128)(2,1)S(1)}, bf16[128,2,1536]{2,1,0:T(2,128)(2,1)}, u32[]{:S(2)}) copy-start(bf16[128,2,1536]{2,1,0:T(2,128)(2,1)} %param.5) | copy-start | bytes 2359300

commit v3 on v0

--- a/solution.py
+++ b/solution.py
@@ -1,12 +1,17 @@
+import functools
 import math
 
 import jax
 import jax.numpy as jnp
 from jax import lax
+from jax.experimental import pallas as pl
+from jax.experimental.pallas import tpu as pltpu
 from jax.sharding import PartitionSpec as P
 
 HEAD_DIM = 128
 SCALE_BLOCK = 128
+KERNEL_VMEM = 8 << 20
+BOTH = ("patch", "uly")
 
 
 def decode(codes, exps):
@@ -59,7 +64,7 @@
     return jnp.concatenate(outputs, axis=1).astype(jnp.bfloat16)
 
 
-def on_device(queries, stale_kv, codes, exps):
+def attend_gathered(queries, stale_kv, codes, exps):
     residual = decode(codes, exps)
     query_rows = lax.all_to_all(queries, "uly", split_axis=1, concat_axis=0, tiled=True)
     gathered = lax.all_gather(residual, "patch", axis=0, tiled=True)
@@ -69,6 +74,186 @@
     all_resid = spread.reshape(stale_kv.shape)
     result = attend_whole(query_rows, refresh(stale_kv, all_resid))
     return lax.all_to_all(result, "uly", split_axis=0, concat_axis=1, tiled=True)
+
+
+def aligned(start, size):
+    return pl.ds(pl.multiple_of(start, HEAD_DIM), size)
+
+
+def kernel_call(body, outputs, operands, spaces, scratch=(), out_space=pltpu.VMEM):
+    operands = [
+        pltpu.with_memory_space_constraint(each, pltpu.HBM) if space is pltpu.HBM else each
+        for each, space in zip(operands, spaces)
+    ]
+    return pl.pallas_call(
+        body,
+        out_shape=[jax.ShapeDtypeStruct(shape, jnp.bfloat16) for shape in outputs],
+        in_specs=[pl.BlockSpec(memory_space=space) for space in spaces],
+        out_specs=[pl.BlockSpec(memory_space=out_space)] * len(outputs),
+        scratch_shapes=list(scratch),
+        compiler_params=pltpu.CompilerParams(vmem_limit_bytes=KERNEL_VMEM),
+    )(*operands)
+
+
+def decode_kernel(queries_hbm, codes_hbm, exps_hbm, away_ref, home_ref, codes_ref, exps_ref, sems):
+    _, packed_rows, width = home_ref.shape
+    rows = packed_rows // 3
+    uly = lax.axis_index("uly")
+    letter = lax.rem(lax.axis_index("patch"), 2)
+    fetch_exps = pltpu.make_async_copy(exps_hbm, exps_ref, sems.at[0])
+    fetch_exps.start()
+    starts = []
+    fetch_codes = []
+    for side in range(2):
+        for turn in range(2):
+            start = (((1 - uly) if side == 0 else uly) * 2 + (letter ^ turn)) * width
+            starts.append(start)
+            for kind in range(2):
+                slot = len(fetch_codes)
+                fetch_codes.append(
+                    pltpu.make_async_copy(
+                        codes_hbm.at[:, kind, aligned(start, width)], codes_ref.at[slot], sems.at[1 + slot]
+                    )
+                )
+                fetch_codes[slot].start()
+    fetch_queries = []
+    for part, start in enumerate(starts):
+        out_ref = (away_ref, home_ref)[part // 2]
+        fetch_queries.append(
+            pltpu.make_async_copy(
+                queries_hbm.at[:, aligned(start, width)], out_ref.at[part % 2, pl.ds(2 * rows, rows)], sems.at[9 + part]
+            )
+        )
+        fetch_queries[-1].start()
+    blocks = exps_ref.shape[2]
+    block_of = lax.broadcasted_iota(jnp.int32, (blocks, width), 1) // SCALE_BLOCK
+    row_of = lax.broadcasted_iota(jnp.int32, (blocks, width), 0)
+    fetch_exps.wait()
+    scales = [jnp.exp2(exps_ref[:, kind, :].astype(jnp.float32)).astype(jnp.bfloat16) for kind in range(2)]
+    for part, start in enumerate(starts):
+        out_ref = (away_ref, home_ref)[part // 2]
+        spread = (row_of == block_of + start // SCALE_BLOCK).astype(jnp.float32).astype(jnp.bfloat16)
+        for kind in range(2):
+            scale = jnp.dot(scales[kind], spread, preferred_element_type=jnp.float32)
+            fetch_codes[2 * part + kind].wait()
+            decoded = codes_ref[2 * part + kind].astype(jnp.float32) * scale
+            out_ref[part % 2, kind * rows : (kind + 1) * rows, :] = decoded.astype(jnp.bfloat16)
+    for fetch in fetch_queries:
+        fetch.wait()
+
+
+def decode_halves(queries, codes, exps):
+    rows, model_width = queries.shape
+    quarter = model_width // lax.axis_size("uly") // 2
+    return kernel_call(
+        decode_kernel,
+        [(2, 3 * rows, quarter)] * 2,
+        [queries, codes, exps],
+        [pltpu.HBM] * 3,
+        [
+            pltpu.VMEM((8, rows, quarter), codes.dtype),
+            pltpu.VMEM(exps.shape, exps.dtype),
+            pltpu.SemaphoreType.DMA((13,)),
+        ],
+    )
+
+
+def attend_kernel(home_ref, received_ref, near_ref, far_refs, cross_refs, stale_ref, *out_refs):
+    rows, width = out_refs[0].shape
+    patch = lax.axis_index("patch")
+    uly = lax.axis_index("uly")
+    heads = range(width // HEAD_DIM)
+    sources = (
+        (home_ref.at[0], received_ref.at[0]),
+        (near_ref.at[0], near_ref.at[1]),
+        far_refs,
+        cross_refs,
+    )
+
+    def refreshed(kind):
+        parts = []
+        for step, pair in enumerate(sources):
+            for side, source_ref in enumerate(pair):
+                block = (patch ^ step) * 2 + (uly ^ side)
+                stale = stale_ref[kind, pl.ds(pl.multiple_of(block * rows, rows), rows), :]
+                parts.append(refresh(stale, source_ref[kind * rows : (kind + 1) * rows, :]))
+        return jnp.concatenate(parts, axis=0)
+
+    query_rows = jnp.concatenate(
+        [source_ref[2 * rows : 3 * rows, :] for pair in sources[:2] for source_ref in pair], axis=0
+    )
+    key_rows = refreshed(0)
+    scores = [head_scores(query_rows, key_rows, head) for head in heads]
+    value_rows = refreshed(1)
+    weights = [jnp.exp(each - jnp.max(each, axis=1, keepdims=True)) for each in scores]
+    sums = [weigh_values(weights[head], value_rows, head) for head in heads]
+    for head in heads:
+        result = (sums[head] / jnp.sum(weights[head], axis=1, keepdims=True)).astype(jnp.bfloat16)
+        for block, out_ref in enumerate(out_refs):
+            out_ref[:, head * HEAD_DIM : (head + 1) * HEAD_DIM] = result[block * rows : (block + 1) * rows]
+
+
+def attend_quarter(home, received, near, far, cross, own_stale):
+    rows, width = home.shape[1] // 3, home.shape[2]
+
+    def body(home_ref, received_ref, near_ref, far_a, far_b, cross_a, cross_b, stale_ref, *out_refs):
+        attend_kernel(home_ref, received_ref, near_ref, (far_a, far_b), (cross_a, cross_b), stale_ref, *out_refs)
+
+    return kernel_call(body, [(rows, width)] * 4, [home, received, near, *far, *cross, own_stale], [pltpu.VMEM] * 8)
+
+
+def place_kernel(*refs):
+    *part_refs, mixed_hbm, sems = refs
+    width = part_refs[0].shape[1]
+    uly = lax.axis_index("uly")
+    letter = lax.rem(lax.axis_index("patch"), 2)
+    copies = []
+    for block, part_ref in enumerate(part_refs):
+        start = ((uly ^ (block & 1)) * 2 + (letter ^ (block >> 1))) * width
+        copies.append(pltpu.make_async_copy(part_ref, mixed_hbm.at[:, aligned(start, width)], sems.at[block]))
+        copies[-1].start()
+    for copy in copies:
+        copy.wait()
+
+
+def place(parts):
+    rows, width = parts[0].shape
+    (mixed,) = kernel_call(
+        place_kernel,
+        [(rows, 4 * width)],
+        parts,
+        [pltpu.VMEM] * 4,
+        [pltpu.SemaphoreType.DMA((4,))],
+        out_space=pltpu.HBM,
+    )
+    return mixed
+
+
+def swap(array, distance):
+    count = lax.axis_size(BOTH)
+    return lax.ppermute(array, BOTH, [(peer, peer ^ distance) for peer in range(count)])
+
+
+def attend_paired(queries, stale_kv, codes, exps):
+    tokens = stale_kv.shape[0]
+    quarter = stale_kv.shape[2] // 2
+    kv_rows = 2 * queries.shape[0]
+    away, home = decode_halves(queries, codes, exps)
+    received = swap(away, 1)
+    home, stale_kv = lax.optimization_barrier((home, stale_kv))
+    letter = lax.rem(lax.axis_index("patch"), 2)
+    own_stale = jnp.swapaxes(lax.dynamic_slice(stale_kv, (0, 0, letter * quarter), (tokens, 2, quarter)), 0, 1)
+    cross = [swap(each[1, :kv_rows], 6) for each in (home, received)]
+    far = [swap(each[0, :kv_rows], 4) for each in (home, received)]
+    near = swap(jnp.stack([home[1], received[1]]), 2)
+    parts = attend_quarter(home, received, near, far, cross, own_stale)
+    return place([parts[0]] + [swap(parts[block], block) for block in (1, 2, 3)])
+
+
+def on_device(queries, stale_kv, codes, exps):
+    if lax.axis_size("patch") == 4 and lax.axis_size("uly") == 2:
+        return attend_paired(queries, stale_kv, codes, exps)
+    return attend_gathered(queries, stale_kv, codes, exps)
 
 
 def solution(mesh):

time: 96 us -> 26.9 us (0.28)
  local copies, waits for them, and re-layouts: 41.8 us -> 0.14 us
  blocking collectives: 28.6 us -> 0 us
  starting transfers between devices: 7 us -> 15.1 us
  matrix products: 5.54 us -> 0 us
  other arithmetic: 4.29 us -> 0.02 us
  Pallas kernels: 0 us -> 3.1 us
    all_gather x1 -> x0, blocking collectives: 21.3 us -> none  [on_device(): gathered = lax.all_gather(residual, 'patch', axis=0, tiled=True)]
    unnamed x17 -> x2, local copies, waits for them, and re-layouts: 16 us -> 0.01 us
    ppermute x0 -> x9, starting transfers between devices: none -> 15.1 us  [swap(): lax.ppermute(array, BOTH, [(peer, peer ^ distance) for peer in range(coun...]
    all_to_all x3 -> x0, local copies, waits for them, and re-layouts: 13.2 us -> none  [the longest x1 11.9 us: on_device(): lax.all_to_all(blocked, 'uly', split_axis=3, concat_axis=1, tiled=True)]
    reshape x1 -> x0, local copies, waits for them, and re-layouts: 10.4 us -> none  [on_device(): gathered.reshape(patch_count, residual.shape[0], 2, residual.shape[2])]
    ppermute x0 -> x9, waiting for transfers between devices: none -> 8.33 us  [swap(): lax.ppermute(array, BOTH, [(peer, peer ^ distance) for peer in range(coun...]
    all_to_all x2 -> x0, waiting for transfers between devices: 7.75 us -> none  [the longest x1 7.74 us: on_device(): lax.all_to_all(blocked, 'uly', split_axis=3, concat_axis=1, tiled=True)]
    all_to_all x1 -> x0, blocking collectives: 7.35 us -> none  [on_device(): lax.all_to_all(result, 'uly', split_axis=0, concat_axis=1, tiled=True)]
  transfers between devices with their start and end apart: 2 -> 9, of which waited for: 1 -> 6; matrix products, arithmetic and copies ran while one was open for 21% -> 1% of each run, Pallas kernels for 0% -> 0%
where the time goes in v3:
time: 26.9 us; the launch traced here: 26.8 us
  starting transfers between devices  15.1 us (56%)
  waiting for transfers between devices  8.33 us (31%)
  Pallas kernels  3.1 us (12%)
    ppermute x9, starting transfers between devices, swap(): lax.ppermute(array, BOTH, [(peer, peer ^ distance) for peer in range(coun...  15.1 us
    ppermute x9, waiting for transfers between devices, swap(): lax.ppermute(array, BOTH, [(peer, peer ^ distance) for peer in range(coun...  8.33 us
    pallas_call x3, Pallas kernels, kernel_call(): pl.pallas_call(body, out_shape=[jax.ShapeDtypeStruct(shape, jnp.bfloat16)...  3.1 us
  transfers between devices with their start and end apart: 9, of which 6 were waited for; matrix products, arithmetic and copies ran while one was open for 1% of the time, Pallas kernels for 0%

profile of v3, /device:TPU:0, one launch (start us, length us, event | category | flops | bytes accessed | tf_op | source)
XLA Modules:
  0.0 26.8 jit_solution(2053870795748460147)
XLA Ops:
  0.0 0.0 copy-start
  0.0 2.0 %shard_map.46 = (bf16[2,48,768]{2,1,0:T(8,128)(2,1)S(1)}, bf16[2,48,768]{2,1,0:T(8,128)(2,1)S(1)}) custom-call(bf16[16,3072]{1,0:T(8,128)(2,1)} %queries_hbm.1, s32[16,2,3072]{2,1,0:T(2,128)} %codes_hbm.1, s32[16,2,24]{2,1,0:T(2,128)} %exps_hbm.1), custom_call_target="tpu_custom_call" | custom-call | tf_op jit(solution)/shard_map/pallas_call | solution.py:88
  2.0 3.0 %collective-permute-start = (bf16[2,48,768]{2,1,0:T(8,128)(2,1)S(1)}, bf16[2,48,768]{2,1,0:T(8,128)(2,1)S(1)}, u32[]{:S(2)}, u32[]{:S(2)}) collective-permute-start(bf16[2,48,768]{2,1,0:T(8,128)(2,1)S(1)} %get-tuple-element.15), channel_id=1, source_target_pairs={{0,4},{4,0},{8,12},{12,8},{16,20},{20,16},{24,28},{28,24},{1,5},{5... | collective-permute-start | bytes 442376 | tf_op jit(solution)/shard_map/ppermute | solution.py:234
  5.0 2.6 %collective-permute-start.2 = (bf16[32,768]{1,0:T(8,128)(2,1)S(1)}, bf16[32,768]{1,0:T(8,128)(2,1)S(1)}, u32[]{:S(2)}, u32[]{:S(2)}) collective-permute-start(bf16[32,768]{1,0:T(8,128)(2,1)S(1)} %get-tuple-element.24), channel_id=1, source_target_pairs={{0,16},{4,20},{8,24},{12,28},{16,0},{20,4},{24,8},{28,12},{1,17},{... | collective-permute-start | bytes 147464 | tf_op jit(solution)/shard_map/ppermute | solution.py:234
  7.7 1.3 %collective-permute-start.4 = (bf16[32,768]{1,0:T(8,128)(2,1)S(1)}, bf16[32,768]{1,0:T(8,128)(2,1)S(1)}, u32[]{:S(2)}, u32[]{:S(2)}) collective-permute-start(bf16[32,768]{1,0:T(8,128)(2,1)S(1)} %get-tuple-element.23), channel_id=1, source_target_pairs={{0,24},{4,28},{8,16},{12,20},{16,8},{20,12},{24,0},{28,4},{1,25},{... | collective-permute-start | bytes 147464 | tf_op jit(solution)/shard_map/ppermute | solution.py:234
  9.0 0.0 copy-done
  9.0 0.1 copy.5
  9.1 0.0 collective-permute-done.received_ref
  9.2 1.6 %collective-permute-start.1 = (bf16[2,48,768]{2,1,0:T(8,128)(2,1)S(1)}, bf16[2,48,768]{2,1,0:T(8,128)(2,1)S(1)}, u32[]{:S(2)}, u32[]{:S(2)}) collective-permute-start(bf16[2,48,768]{2,1,0:T(8,128)(2,1)S(1)} %pad_maximum_fusion), channel_id=1, source_target_pairs={{0,8},{4,12},{8,0},{12,4},{16,24},{20,28},{24,16},{28,20},{1,9},{5... | collective-permute-start | bytes 442376 | tf_op jit(solution)/shard_map/ppermute | solution.py:234
  10.8 2.6 %collective-permute-start.3 = (bf16[32,768]{1,0:T(8,128)(2,1)S(1)}, bf16[32,768]{1,0:T(8,128)(2,1)S(1)}, u32[]{:S(2)}, u32[]{:S(2)}) collective-permute-start(bf16[32,768]{1,0:T(8,128)(2,1)S(1)} %get-tuple-element.22), channel_id=1, source_target_pairs={{0,16},{4,20},{8,24},{12,28},{16,0},{20,4},{24,8},{28,12},{1,17},{... | collective-permute-start | bytes 147464 | tf_op jit(solution)/shard_map/ppermute | solution.py:234
  13.4 0.3 %collective-permute-start.5 = (bf16[32,768]{1,0:T(8,128)(2,1)S(1)}, bf16[32,768]{1,0:T(8,128)(2,1)S(1)}, u32[]{:S(2)}, u32[]{:S(2)}) collective-permute-start(bf16[32,768]{1,0:T(8,128)(2,1)S(1)} %get-tuple-element.21), channel_id=1, source_target_pairs={{0,24},{4,28},{8,16},{12,20},{16,8},{20,12},{24,0},{28,4},{1,25},{... | collective-permute-start | bytes 147464 | tf_op jit(solution)/shard_map/ppermute | solution.py:234
  13.7 0.0 collective-permute-done.2.far_a
  13.7 0.4 %collective-permute-done.4.cross_a = bf16[32,768]{1,0:T(8,128)(2,1)S(1)} collective-permute-done((bf16[32,768]{1,0:T(8,128)(2,1)S(1)}, bf16[32,768]{1,0:T(8,128)(2,1)S(1)}, u32[]{:S(2)}, u32[]{:S(2)}) %collective-permute-start.4) | collective-permute-done | bytes 49184 | tf_op jit(solution)/shard_map/ppermute | solution.py:234
  14.2 2.0 %collective-permute-done.3.far_b = bf16[32,768]{1,0:T(8,128)(2,1)S(1)} collective-permute-done((bf16[32,768]{1,0:T(8,128)(2,1)S(1)}, bf16[32,768]{1,0:T(8,128)(2,1)S(1)}, u32[]{:S(2)}, u32[]{:S(2)}) %collective-permute-start.3) | collective-permute-done | bytes 49184 | tf_op jit(solution)/shard_map/ppermute | solution.py:234
  16.1 3.2 %collective-permute-done.5.cross_b = bf16[32,768]{1,0:T(8,128)(2,1)S(1)} collective-permute-done((bf16[32,768]{1,0:T(8,128)(2,1)S(1)}, bf16[32,768]{1,0:T(8,128)(2,1)S(1)}, u32[]{:S(2)}, u32[]{:S(2)}) %collective-permute-start.5) | collective-permute-done | bytes 49184 | tf_op jit(solution)/shard_map/ppermute | solution.py:234
  19.3 0.0 collective-permute-done.1.near_ref
  19.3 0.5 %shard_map.47 = (bf16[16,768]{1,0:T(8,128)(2,1)S(1)}, bf16[16,768]{1,0:T(8,128)(2,1)S(1)}, bf16[16,768]{1,0:T(8,128)(2,1)S(1)}, bf16[16,768]{1,0:T(8,128)(2,1)S(1)}) custom-call(bf16[2,48,768]{2,1,0:T(8,128)(2,1)S(1)} %get-tuple-element.14.home_ref, bf16[2,48,768]{2,1,0:T(8,128)(2,1)S(1)} %collective-permute-done.received_ref, ...), custom_call_target="tpu_custom_call" | custom-call | tf_op jit(solution)/shard_map/pallas_call | solution.py:88
  19.8 1.6 %collective-permute-start.6 = (bf16[16,768]{1,0:T(8,128)(2,1)S(1)}, bf16[16,768]{1,0:T(8,128)(2,1)S(1)}, u32[]{:S(2)}, u32[]{:S(2)}) collective-permute-start(bf16[16,768]{1,0:T(8,128)(2,1)S(1)} %get-tuple-element.18), channel_id=1, source_target_pairs={{0,4},{4,0},{8,12},{12,8},{16,20},{20,16},{24,28},{28,24},{1,5},{5... | collective-permute-start | bytes 73736 | tf_op jit(solution)/shard_map/ppermute | solution.py:234
  21.4 0.0 collective-permute-start.7
  21.4 2.0 %collective-permute-start.8 = (bf16[16,768]{1,0:T(8,128)(2,1)S(1)}, bf16[16,768]{1,0:T(8,128)(2,1)S(1)}, u32[]{:S(2)}, u32[]{:S(2)}) collective-permute-start(bf16[16,768]{1,0:T(8,128)(2,1)S(1)} %get-tuple-element.20), channel_id=1, source_target_pairs={{0,12},{4,8},{8,4},{12,0},{16,28},{20,24},{24,20},{28,16},{1,13},{... | collective-permute-start | bytes 73736 | tf_op jit(solution)/shard_map/ppermute | solution.py:234
  23.3 0.3 %collective-permute-done.6.refs_1_ = bf16[16,768]{1,0:T(8,128)(2,1)S(1)} collective-permute-done((bf16[16,768]{1,0:T(8,128)(2,1)S(1)}, bf16[16,768]{1,0:T(8,128)(2,1)S(1)}, u32[]{:S(2)}, u32[]{:S(2)}) %collective-permute-start.6) | collective-permute-done | bytes 24608 | tf_op jit(solution)/shard_map/ppermute | solution.py:234
  23.7 1.5 %collective-permute-done.7.refs_2_ = bf16[16,768]{1,0:T(8,128)(2,1)S(1)} collective-permute-done((bf16[16,768]{1,0:T(8,128)(2,1)S(1)}, bf16[16,768]{1,0:T(8,128)(2,1)S(1)}, u32[]{:S(2)}, u32[]{:S(2)}) %collective-permute-start.7) | collective-permute-done | bytes 24608 | tf_op jit(solution)/shard_map/ppermute | solution.py:234
  25.2 0.9 %collective-permute-done.8.refs_3_ = bf16[16,768]{1,0:T(8,128)(2,1)S(1)} collective-permute-done((bf16[16,768]{1,0:T(8,128)(2,1)S(1)}, bf16[16,768]{1,0:T(8,128)(2,1)S(1)}, u32[]{:S(2)}, u32[]{:S(2)}) %collective-permute-start.8) | collective-permute-done | bytes 24608 | tf_op jit(solution)/shard_map/ppermute | solution.py:234
  26.1 0.7 %shard_map.48 = bf16[16,3072]{1,0:T(8,128)(2,1)} custom-call(bf16[16,768]{1,0:T(8,128)(2,1)S(1)} %get-tuple-element.17.refs_0_, bf16[16,768]{1,0:T(8,128)(2,1)S(1)} %collective-permute-done.6.refs_1_, bf16[16,768]{1,0:T(8,128)(2,1)S(1)} %collective-permute-done.7.refs_2_, bf16[16,768]{1,0:T(8,128)(2,1)S(1)} %collective-permute-done.8.refs_3_), custom_call_target="tpu_custom_call" | custom-call | tf_op jit(solution)/shard_map/pallas_call | solution.py:88
  (6 shorter events, 0.1 us)
Async XLA Ops:
  0.0 9.0 %copy-start = (bf16[128,2,1536]{2,1,0:T(2,128)(2,1)S(1)}, bf16[128,2,1536]{2,1,0:T(2,128)(2,1)}, u32[]{:S(2)}) copy-start(bf16[128,2,1536]{2,1,0:T(2,128)(2,1)} %param.5) | copy-start | bytes 2359300
  2.0 7.1 %collective-permute-start = (bf16[2,48,768]{2,1,0:T(8,128)(2,1)S(1)}, bf16[2,48,768]{2,1,0:T(8,128)(2,1)S(1)}, u32[]{:S(2)}, u32[]{:S(2)}) collective-permute-start(bf16[2,48,768]{2,1,0:T(8,128)(2,1)S(1)} %get-tuple-element.15), channel_id=1, source_target_pairs={{0,4},{4,0},{8,12},{12,8},{16,20},{20,16},{24,28},{28,24},{1,5},{5... | collective-permute-start | bytes 442376 | tf_op jit(solution)/shard_map/ppermute | solution.py:234
  5.0 8.7 %collective-permute-start.2 = (bf16[32,768]{1,0:T(8,128)(2,1)S(1)}, bf16[32,768]{1,0:T(8,128)(2,1)S(1)}, u32[]{:S(2)}, u32[]{:S(2)}) collective-permute-start(bf16[32,768]{1,0:T(8,128)(2,1)S(1)} %get-tuple-element.24), channel_id=1, source_target_pairs={{0,16},{4,20},{8,24},{12,28},{16,0},{20,4},{24,8},{28,12},{1,17},{... | collective-permute-start | bytes 147464 | tf_op jit(solution)/shard_map/ppermute | solution.py:234
  7.7 6.5 %collective-permute-start.4 = (bf16[32,768]{1,0:T(8,128)(2,1)S(1)}, bf16[32,768]{1,0:T(8,128)(2,1)S(1)}, u32[]{:S(2)}, u32[]{:S(2)}) collective-permute-start(bf16[32,768]{1,0:T(8,128)(2,1)S(1)} %get-tuple-element.23), channel_id=1, source_target_pairs={{0,24},{4,28},{8,16},{12,20},{16,8},{20,12},{24,0},{28,4},{1,25},{... | collective-permute-start | bytes 147464 | tf_op jit(solution)/shard_map/ppermute | solution.py:234
  9.2 10.1 %collective-permute-start.1 = (bf16[2,48,768]{2,1,0:T(8,128)(2,1)S(1)}, bf16[2,48,768]{2,1,0:T(8,128)(2,1)S(1)}, u32[]{:S(2)}, u32[]{:S(2)}) collective-permute-start(bf16[2,48,768]{2,1,0:T(8,128)(2,1)S(1)} %pad_maximum_fusion), channel_id=1, source_target_pairs={{0,8},{4,12},{8,0},{12,4},{16,24},{20,28},{24,16},{28,20},{1,9},{5... | collective-permute-start | bytes 442376 | tf_op jit(solution)/shard_map/ppermute | solution.py:234
  10.8 5.4 %collective-permute-start.3 = (bf16[32,768]{1,0:T(8,128)(2,1)S(1)}, bf16[32,768]{1,0:T(8,128)(2,1)S(1)}, u32[]{:S(2)}, u32[]{:S(2)}) collective-permute-start(bf16[32,768]{1,0:T(8,128)(2,1)S(1)} %get-tuple-element.22), channel_id=1, source_target_pairs={{0,16},{4,20},{8,24},{12,28},{16,0},{20,4},{24,8},{28,12},{1,17},{... | collective-permute-start | bytes 147464 | tf_op jit(solution)/shard_map/ppermute | solution.py:234
  13.4 5.9 %collective-permute-start.5 = (bf16[32,768]{1,0:T(8,128)(2,1)S(1)}, bf16[32,768]{1,0:T(8,128)(2,1)S(1)}, u32[]{:S(2)}, u32[]{:S(2)}) collective-permute-start(bf16[32,768]{1,0:T(8,128)(2,1)S(1)} %get-tuple-element.21), channel_id=1, source_target_pairs={{0,24},{4,28},{8,16},{12,20},{16,8},{20,12},{24,0},{28,4},{1,25},{... | collective-permute-start | bytes 147464 | tf_op jit(solution)/shard_map/ppermute | solution.py:234
  19.8 3.9 %collective-permute-start.6 = (bf16[16,768]{1,0:T(8,128)(2,1)S(1)}, bf16[16,768]{1,0:T(8,128)(2,1)S(1)}, u32[]{:S(2)}, u32[]{:S(2)}) collective-permute-start(bf16[16,768]{1,0:T(8,128)(2,1)S(1)} %get-tuple-element.18), channel_id=1, source_target_pairs={{0,4},{4,0},{8,12},{12,8},{16,20},{20,16},{24,28},{28,24},{1,5},{5... | collective-permute-start | bytes 73736 | tf_op jit(solution)/shard_map/ppermute | solution.py:234
  21.4 3.8 %collective-permute-start.7 = (bf16[16,768]{1,0:T(8,128)(2,1)S(1)}, bf16[16,768]{1,0:T(8,128)(2,1)S(1)}, u32[]{:S(2)}, u32[]{:S(2)}) collective-permute-start(bf16[16,768]{1,0:T(8,128)(2,1)S(1)} %get-tuple-element.19), channel_id=1, source_target_pairs={{0,8},{4,12},{8,0},{12,4},{16,24},{20,28},{24,16},{28,20},{1,9},{5... | collective-permute-start | bytes 73736 | tf_op jit(solution)/shard_map/ppermute | solution.py:234
  21.4 4.7 %collective-permute-start.8 = (bf16[16,768]{1,0:T(8,128)(2,1)S(1)}, bf16[16,768]{1,0:T(8,128)(2,1)S(1)}, u32[]{:S(2)}, u32[]{:S(2)}) collective-permute-start(bf16[16,768]{1,0:T(8,128)(2,1)S(1)} %get-tuple-element.20), channel_id=1, source_target_pairs={{0,12},{4,8},{8,4},{12,0},{16,28},{20,24},{24,20},{28,16},{1,13},{... | collective-permute-start | bytes 73736 | tf_op jit(solution)/shard_map/ppermute | solution.py:234

commit v4 on v3

--- a/solution.py
+++ b/solution.py
@@ -12,6 +12,7 @@
 SCALE_BLOCK = 128
 KERNEL_VMEM = 8 << 20
 BOTH = ("patch", "uly")
+RETURN_ORDER = (3, 1, 2)
 
 
 def decode(codes, exps):
@@ -129,15 +130,17 @@
     block_of = lax.broadcasted_iota(jnp.int32, (blocks, width), 1) // SCALE_BLOCK
     row_of = lax.broadcasted_iota(jnp.int32, (blocks, width), 0)
     fetch_exps.wait()
-    scales = [jnp.exp2(exps_ref[:, kind, :].astype(jnp.float32)).astype(jnp.bfloat16) for kind in range(2)]
-    for part, start in enumerate(starts):
+    scales = jnp.concatenate([jnp.exp2(exps_ref[:, kind, :].astype(jnp.float32)) for kind in range(2)], axis=0)
+    scales = scales.astype(jnp.bfloat16)
+    spreads = [(row_of == block_of + start // SCALE_BLOCK).astype(jnp.float32).astype(jnp.bfloat16) for start in starts]
+    wide_scales = [jnp.dot(scales, spread, preferred_element_type=jnp.float32) for spread in spreads]
+    for part, wide_scale in enumerate(wide_scales):
         out_ref = (away_ref, home_ref)[part // 2]
-        spread = (row_of == block_of + start // SCALE_BLOCK).astype(jnp.float32).astype(jnp.bfloat16)
         for kind in range(2):
-            scale = jnp.dot(scales[kind], spread, preferred_element_type=jnp.float32)
             fetch_codes[2 * part + kind].wait()
-            decoded = codes_ref[2 * part + kind].astype(jnp.float32) * scale
-            out_ref[part % 2, kind * rows : (kind + 1) * rows, :] = decoded.astype(jnp.bfloat16)
+            own_rows = slice(kind * rows, (kind + 1) * rows)
+            decoded = codes_ref[2 * part + kind].astype(jnp.float32) * wide_scale[own_rows]
+            out_ref[part % 2, own_rows, :] = decoded.astype(jnp.bfloat16)
     for fetch in fetch_queries:
         fetch.wait()
 
@@ -196,10 +199,10 @@
 def attend_quarter(home, received, near, far, cross, own_stale):
     rows, width = home.shape[1] // 3, home.shape[2]
 
-    def body(home_ref, received_ref, near_ref, far_a, far_b, cross_a, cross_b, stale_ref, *out_refs):
+    def body(home_ref, received_ref, cross_a, far_a, cross_b, far_b, near_ref, stale_ref, *out_refs):
         attend_kernel(home_ref, received_ref, near_ref, (far_a, far_b), (cross_a, cross_b), stale_ref, *out_refs)
 
-    return kernel_call(body, [(rows, width)] * 4, [home, received, near, *far, *cross, own_stale], [pltpu.VMEM] * 8)
+    return kernel_call(body, [(rows, width)] * 4, [home, received, cross[0], far[0], cross[1], far[1], near, own_stale], [pltpu.VMEM] * 8)
 
 
 def place_kernel(*refs):
@@ -208,7 +211,7 @@
     uly = lax.axis_index("uly")
     letter = lax.rem(lax.axis_index("patch"), 2)
     copies = []
-    for block, part_ref in enumerate(part_refs):
+    for block, part_ref in zip((0, *RETURN_ORDER), part_refs):
         start = ((uly ^ (block & 1)) * 2 + (letter ^ (block >> 1))) * width
         copies.append(pltpu.make_async_copy(part_ref, mixed_hbm.at[:, aligned(start, width)], sems.at[block]))
         copies[-1].start()
@@ -247,7 +250,7 @@
     far = [swap(each[0, :kv_rows], 4) for each in (home, received)]
     near = swap(jnp.stack([home[1], received[1]]), 2)
     parts = attend_quarter(home, received, near, far, cross, own_stale)
-    return place([parts[0]] + [swap(parts[block], block) for block in (1, 2, 3)])
+    return place([parts[0]] + [swap(parts[block], block) for block in RETURN_ORDER])
 
 
 def on_device(queries, stale_kv, codes, exps):

time: 26.9 us -> 25 us (0.929)
  waiting for transfers between devices: 8.33 us -> 7.39 us
  Pallas kernels: 3.1 us -> 2.37 us
  starting transfers between devices: 15.1 us -> 14.8 us
    ppermute x9, waiting for transfers between devices: 8.33 us -> 7.39 us  [swap(): lax.ppermute(array, BOTH, [(peer, peer ^ distance) for peer in range(coun...]
    pallas_call x3, Pallas kernels: 3.1 us -> 2.37 us  [kernel_call(): pl.pallas_call(body, out_shape=[jax.ShapeDtypeStruct(shape, jnp.bfloat16)...]
  transfers between devices with their start and end apart: 9 -> 9, of which waited for: 6 -> 7; matrix products, arithmetic and copies ran while one was open for 1% -> 1% of each run, Pallas kernels for 0% -> 0%
where the time goes in v4:
time: 25 us; the launch traced here: 24.8 us
  starting transfers between devices  14.8 us (59%)
  waiting for transfers between devices  7.39 us (30%)
  Pallas kernels  2.37 us (9%)
    ppermute x9, starting transfers between devices, swap(): lax.ppermute(array, BOTH, [(peer, peer ^ distance) for peer in range(coun...  14.8 us
    ppermute x9, waiting for transfers between devices, swap(): lax.ppermute(array, BOTH, [(peer, peer ^ distance) for peer in range(coun...  7.39 us
    pallas_call x3, Pallas kernels, kernel_call(): pl.pallas_call(body, out_shape=[jax.ShapeDtypeStruct(shape, jnp.bfloat16)...  2.37 us
  transfers between devices with their start and end apart: 9, of which 7 were waited for; matrix products, arithmetic and copies ran while one was open for 1% of the time, Pallas kernels for 0%

profile of v4, /device:TPU:0, one launch (start us, length us, event | category | flops | bytes accessed | tf_op | source)
XLA Modules:
  0.0 24.8 jit_solution(10199942485619994127)
XLA Ops:
  0.0 0.0 copy-start
  0.0 1.2 %shard_map.46 = (bf16[2,48,768]{2,1,0:T(8,128)(2,1)S(1)}, bf16[2,48,768]{2,1,0:T(8,128)(2,1)S(1)}) custom-call(bf16[16,3072]{1,0:T(8,128)(2,1)} %queries_hbm.1, s32[16,2,3072]{2,1,0:T(2,128)} %codes_hbm.1, s32[16,2,24]{2,1,0:T(2,128)} %exps_hbm.1), custom_call_target="tpu_custom_call" | custom-call | tf_op jit(solution)/shard_map/pallas_call | solution.py:89
  1.2 3.0 %collective-permute-start = (bf16[2,48,768]{2,1,0:T(8,128)(2,1)S(1)}, bf16[2,48,768]{2,1,0:T(8,128)(2,1)S(1)}, u32[]{:S(2)}, u32[]{:S(2)}) collective-permute-start(bf16[2,48,768]{2,1,0:T(8,128)(2,1)S(1)} %get-tuple-element.15), channel_id=1, source_target_pairs={{0,4},{4,0},{8,12},{12,8},{16,20},{20,16},{24,28},{28,24},{1,5},{5... | collective-permute-start | bytes 442376 | tf_op jit(solution)/shard_map/ppermute | solution.py:237
  4.3 3.7 %collective-permute-start.1 = (bf16[32,768]{1,0:T(8,128)(2,1)S(1)}, bf16[32,768]{1,0:T(8,128)(2,1)S(1)}, u32[]{:S(2)}, u32[]{:S(2)}) collective-permute-start(bf16[32,768]{1,0:T(8,128)(2,1)S(1)} %get-tuple-element.24), channel_id=1, source_target_pairs={{0,24},{4,28},{8,16},{12,20},{16,8},{20,12},{24,0},{28,4},{1,25},{... | collective-permute-start | bytes 147464 | tf_op jit(solution)/shard_map/ppermute | solution.py:237
  8.0 0.0 collective-permute-start.2
  8.0 0.0 copy-done
  8.0 0.1 copy.5
  8.1 0.1 collective-permute-done.received_ref
  8.2 1.9 %collective-permute-start.5 = (bf16[2,48,768]{2,1,0:T(8,128)(2,1)S(1)}, bf16[2,48,768]{2,1,0:T(8,128)(2,1)S(1)}, u32[]{:S(2)}, u32[]{:S(2)}) collective-permute-start(bf16[2,48,768]{2,1,0:T(8,128)(2,1)S(1)} %pad_maximum_fusion), channel_id=1, source_target_pairs={{0,8},{4,12},{8,0},{12,4},{16,24},{20,28},{24,16},{28,20},{1,9},{5... | collective-permute-start | bytes 442376 | tf_op jit(solution)/shard_map/ppermute | solution.py:237
  10.0 2.6 %collective-permute-start.3 = (bf16[32,768]{1,0:T(8,128)(2,1)S(1)}, bf16[32,768]{1,0:T(8,128)(2,1)S(1)}, u32[]{:S(2)}, u32[]{:S(2)}) collective-permute-start(bf16[32,768]{1,0:T(8,128)(2,1)S(1)} %get-tuple-element.22), channel_id=1, source_target_pairs={{0,24},{4,28},{8,16},{12,20},{16,8},{20,12},{24,0},{28,4},{1,25},{... | collective-permute-start | bytes 147464 | tf_op jit(solution)/shard_map/ppermute | solution.py:237
  12.6 0.1 collective-permute-start.4
  12.8 0.0 collective-permute-done.1.cross_a
  12.8 0.6 %collective-permute-done.2.far_a = bf16[32,768]{1,0:T(8,128)(2,1)S(1)} collective-permute-done((bf16[32,768]{1,0:T(8,128)(2,1)S(1)}, bf16[32,768]{1,0:T(8,128)(2,1)S(1)}, u32[]{:S(2)}, u32[]{:S(2)}) %collective-permute-start.2) | collective-permute-done | bytes 49184 | tf_op jit(solution)/shard_map/ppermute | solution.py:237
  13.4 3.5 %collective-permute-done.3.cross_b = bf16[32,768]{1,0:T(8,128)(2,1)S(1)} collective-permute-done((bf16[32,768]{1,0:T(8,128)(2,1)S(1)}, bf16[32,768]{1,0:T(8,128)(2,1)S(1)}, u32[]{:S(2)}, u32[]{:S(2)}) %collective-permute-start.3) | collective-permute-done | bytes 49184 | tf_op jit(solution)/shard_map/ppermute | solution.py:237
  16.9 1.3 %collective-permute-done.4.far_b = bf16[32,768]{1,0:T(8,128)(2,1)S(1)} collective-permute-done((bf16[32,768]{1,0:T(8,128)(2,1)S(1)}, bf16[32,768]{1,0:T(8,128)(2,1)S(1)}, u32[]{:S(2)}, u32[]{:S(2)}) %collective-permute-start.4) | collective-permute-done | bytes 49184 | tf_op jit(solution)/shard_map/ppermute | solution.py:237
  18.1 0.0 collective-permute-done.5.near_ref
  18.1 0.5 %shard_map.47 = (bf16[16,768]{1,0:T(8,128)(2,1)S(1)}, bf16[16,768]{1,0:T(8,128)(2,1)S(1)}, bf16[16,768]{1,0:T(8,128)(2,1)S(1)}, bf16[16,768]{1,0:T(8,128)(2,1)S(1)}) custom-call(bf16[2,48,768]{2,1,0:T(8,128)(2,1)S(1)} %get-tuple-element.14.home_ref, bf16[2,48,768]{2,1,0:T(8,128)(2,1)S(1)} %collective-permute-done.received_ref, ...), custom_call_target="tpu_custom_call" | custom-call | tf_op jit(solution)/shard_map/pallas_call | solution.py:89
  18.6 1.2 %collective-permute-start.6 = (bf16[16,768]{1,0:T(8,128)(2,1)S(1)}, bf16[16,768]{1,0:T(8,128)(2,1)S(1)}, u32[]{:S(2)}, u32[]{:S(2)}) collective-permute-start(bf16[16,768]{1,0:T(8,128)(2,1)S(1)} %get-tuple-element.18), channel_id=1, source_target_pairs={{0,12},{4,8},{8,4},{12,0},{16,28},{20,24},{24,20},{28,16},{1,13},{... | collective-permute-start | bytes 73736 | tf_op jit(solution)/shard_map/ppermute | solution.py:237
  19.8 0.5 %collective-permute-start.7 = (bf16[16,768]{1,0:T(8,128)(2,1)S(1)}, bf16[16,768]{1,0:T(8,128)(2,1)S(1)}, u32[]{:S(2)}, u32[]{:S(2)}) collective-permute-start(bf16[16,768]{1,0:T(8,128)(2,1)S(1)} %get-tuple-element.19), channel_id=1, source_target_pairs={{0,4},{4,0},{8,12},{12,8},{16,20},{20,16},{24,28},{28,24},{1,5},{5... | collective-permute-start | bytes 73736 | tf_op jit(solution)/shard_map/ppermute | solution.py:237
  20.3 1.8 %collective-permute-start.8 = (bf16[16,768]{1,0:T(8,128)(2,1)S(1)}, bf16[16,768]{1,0:T(8,128)(2,1)S(1)}, u32[]{:S(2)}, u32[]{:S(2)}) collective-permute-start(bf16[16,768]{1,0:T(8,128)(2,1)S(1)} %get-tuple-element.20), channel_id=1, source_target_pairs={{0,8},{4,12},{8,0},{12,4},{16,24},{20,28},{24,16},{28,20},{1,9},{5... | collective-permute-start | bytes 73736 | tf_op jit(solution)/shard_map/ppermute | solution.py:237
  22.2 1.2 %collective-permute-done.6.refs_1_ = bf16[16,768]{1,0:T(8,128)(2,1)S(1)} collective-permute-done((bf16[16,768]{1,0:T(8,128)(2,1)S(1)}, bf16[16,768]{1,0:T(8,128)(2,1)S(1)}, u32[]{:S(2)}, u32[]{:S(2)}) %collective-permute-start.6) | collective-permute-done | bytes 24608 | tf_op jit(solution)/shard_map/ppermute | solution.py:237
  23.4 0.3 %collective-permute-done.7.refs_2_ = bf16[16,768]{1,0:T(8,128)(2,1)S(1)} collective-permute-done((bf16[16,768]{1,0:T(8,128)(2,1)S(1)}, bf16[16,768]{1,0:T(8,128)(2,1)S(1)}, u32[]{:S(2)}, u32[]{:S(2)}) %collective-permute-start.7) | collective-permute-done | bytes 24608 | tf_op jit(solution)/shard_map/ppermute | solution.py:237
  23.7 0.5 %collective-permute-done.8.refs_3_ = bf16[16,768]{1,0:T(8,128)(2,1)S(1)} collective-permute-done((bf16[16,768]{1,0:T(8,128)(2,1)S(1)}, bf16[16,768]{1,0:T(8,128)(2,1)S(1)}, u32[]{:S(2)}, u32[]{:S(2)}) %collective-permute-start.8) | collective-permute-done | bytes 24608 | tf_op jit(solution)/shard_map/ppermute | solution.py:237
  24.2 0.7 %shard_map.48 = bf16[16,3072]{1,0:T(8,128)(2,1)} custom-call(bf16[16,768]{1,0:T(8,128)(2,1)S(1)} %get-tuple-element.17.refs_0_, bf16[16,768]{1,0:T(8,128)(2,1)S(1)} %collective-permute-done.6.refs_1_, bf16[16,768]{1,0:T(8,128)(2,1)S(1)} %collective-permute-done.7.refs_2_, bf16[16,768]{1,0:T(8,128)(2,1)S(1)} %collective-permute-done.8.refs_3_), custom_call_target="tpu_custom_call" | custom-call | tf_op jit(solution)/shard_map/pallas_call | solution.py:89
  (6 shorter events, 0.1 us)
Async XLA Ops:
  0.0 8.0 %copy-start = (bf16[128,2,1536]{2,1,0:T(2,128)(2,1)S(1)}, bf16[128,2,1536]{2,1,0:T(2,128)(2,1)}, u32[]{:S(2)}) copy-start(bf16[128,2,1536]{2,1,0:T(2,128)(2,1)} %param.5) | copy-start | bytes 2359300
  1.2 6.9 %collective-permute-start = (bf16[2,48,768]{2,1,0:T(8,128)(2,1)S(1)}, bf16[2,48,768]{2,1,0:T(8,128)(2,1)S(1)}, u32[]{:S(2)}, u32[]{:S(2)}) collective-permute-start(bf16[2,48,768]{2,1,0:T(8,128)(2,1)S(1)} %get-tuple-element.15), channel_id=1, source_target_pairs={{0,4},{4,0},{8,12},{12,8},{16,20},{20,16},{24,28},{28,24},{1,5},{5... | collective-permute-start | bytes 442376 | tf_op jit(solution)/shard_map/ppermute | solution.py:237
  4.3 8.5 %collective-permute-start.1 = (bf16[32,768]{1,0:T(8,128)(2,1)S(1)}, bf16[32,768]{1,0:T(8,128)(2,1)S(1)}, u32[]{:S(2)}, u32[]{:S(2)}) collective-permute-start(bf16[32,768]{1,0:T(8,128)(2,1)S(1)} %get-tuple-element.24), channel_id=1, source_target_pairs={{0,24},{4,28},{8,16},{12,20},{16,8},{20,12},{24,0},{28,4},{1,25},{... | collective-permute-start | bytes 147464 | tf_op jit(solution)/shard_map/ppermute | solution.py:237
  8.0 5.4 %collective-permute-start.2 = (bf16[32,768]{1,0:T(8,128)(2,1)S(1)}, bf16[32,768]{1,0:T(8,128)(2,1)S(1)}, u32[]{:S(2)}, u32[]{:S(2)}) collective-permute-start(bf16[32,768]{1,0:T(8,128)(2,1)S(1)} %get-tuple-element.23), channel_id=1, source_target_pairs={{0,16},{4,20},{8,24},{12,28},{16,0},{20,4},{24,8},{28,12},{1,17},{... | collective-permute-start | bytes 147464 | tf_op jit(solution)/shard_map/ppermute | solution.py:237
  8.2 10.0 %collective-permute-start.5 = (bf16[2,48,768]{2,1,0:T(8,128)(2,1)S(1)}, bf16[2,48,768]{2,1,0:T(8,128)(2,1)S(1)}, u32[]{:S(2)}, u32[]{:S(2)}) collective-permute-start(bf16[2,48,768]{2,1,0:T(8,128)(2,1)S(1)} %pad_maximum_fusion), channel_id=1, source_target_pairs={{0,8},{4,12},{8,0},{12,4},{16,24},{20,28},{24,16},{28,20},{1,9},{5... | collective-permute-start | bytes 442376 | tf_op jit(solution)/shard_map/ppermute | solution.py:237
  10.0 6.8 %collective-permute-start.3 = (bf16[32,768]{1,0:T(8,128)(2,1)S(1)}, bf16[32,768]{1,0:T(8,128)(2,1)S(1)}, u32[]{:S(2)}, u32[]{:S(2)}) collective-permute-start(bf16[32,768]{1,0:T(8,128)(2,1)S(1)} %get-tuple-element.22), channel_id=1, source_target_pairs={{0,24},{4,28},{8,16},{12,20},{16,8},{20,12},{24,0},{28,4},{1,25},{... | collective-permute-start | bytes 147464 | tf_op jit(solution)/shard_map/ppermute | solution.py:237
  12.6 5.5 %collective-permute-start.4 = (bf16[32,768]{1,0:T(8,128)(2,1)S(1)}, bf16[32,768]{1,0:T(8,128)(2,1)S(1)}, u32[]{:S(2)}, u32[]{:S(2)}) collective-permute-start(bf16[32,768]{1,0:T(8,128)(2,1)S(1)} %get-tuple-element.21), channel_id=1, source_target_pairs={{0,16},{4,20},{8,24},{12,28},{16,0},{20,4},{24,8},{28,12},{1,17},{... | collective-permute-start | bytes 147464 | tf_op jit(solution)/shard_map/ppermute | solution.py:237
  18.6 4.8 %collective-permute-start.6 = (bf16[16,768]{1,0:T(8,128)(2,1)S(1)}, bf16[16,768]{1,0:T(8,128)(2,1)S(1)}, u32[]{:S(2)}, u32[]{:S(2)}) collective-permute-start(bf16[16,768]{1,0:T(8,128)(2,1)S(1)} %get-tuple-element.18), channel_id=1, source_target_pairs={{0,12},{4,8},{8,4},{12,0},{16,28},{20,24},{24,20},{28,16},{1,13},{... | collective-permute-start | bytes 73736 | tf_op jit(solution)/shard_map/ppermute | solution.py:237
  19.8 3.8 %collective-permute-start.7 = (bf16[16,768]{1,0:T(8,128)(2,1)S(1)}, bf16[16,768]{1,0:T(8,128)(2,1)S(1)}, u32[]{:S(2)}, u32[]{:S(2)}) collective-permute-start(bf16[16,768]{1,0:T(8,128)(2,1)S(1)} %get-tuple-element.19), channel_id=1, source_target_pairs={{0,4},{4,0},{8,12},{12,8},{16,20},{20,16},{24,28},{28,24},{1,5},{5... | collective-permute-start | bytes 73736 | tf_op jit(solution)/shard_map/ppermute | solution.py:237
  20.3 3.8 %collective-permute-start.8 = (bf16[16,768]{1,0:T(8,128)(2,1)S(1)}, bf16[16,768]{1,0:T(8,128)(2,1)S(1)}, u32[]{:S(2)}, u32[]{:S(2)}) collective-permute-start(bf16[16,768]{1,0:T(8,128)(2,1)S(1)} %get-tuple-element.20), channel_id=1, source_target_pairs={{0,8},{4,12},{8,0},{12,4},{16,24},{20,28},{24,16},{28,20},{1,9},{5... | collective-permute-start | bytes 73736 | tf_op jit(solution)/shard_map/ppermute | solution.py:237

commit v5 on v0

--- a/solution.py
+++ b/solution.py
@@ -1,12 +1,20 @@
+import functools
 import math
 
 import jax
 import jax.numpy as jnp
 from jax import lax
+from jax.experimental import pallas as pl
+from jax.experimental.pallas import tpu as pltpu
 from jax.sharding import PartitionSpec as P
 
 HEAD_DIM = 128
 SCALE_BLOCK = 128
+KERNEL_VMEM = 8 << 20
+BOTH = ("patch", "uly")
+START_ORDER = (5, 4, 1, 3, 2)
+RETURN_ORDER = (3, 1, 2)
+SPLIT_TERMS = 3
 
 
 def decode(codes, exps):
@@ -59,7 +67,7 @@
     return jnp.concatenate(outputs, axis=1).astype(jnp.bfloat16)
 
 
-def on_device(queries, stale_kv, codes, exps):
+def attend_gathered(queries, stale_kv, codes, exps):
     residual = decode(codes, exps)
     query_rows = lax.all_to_all(queries, "uly", split_axis=1, concat_axis=0, tiled=True)
     gathered = lax.all_gather(residual, "patch", axis=0, tiled=True)
@@ -69,6 +77,226 @@
     all_resid = spread.reshape(stale_kv.shape)
     result = attend_whole(query_rows, refresh(stale_kv, all_resid))
     return lax.all_to_all(result, "uly", split_axis=0, concat_axis=1, tiled=True)
+
+
+def aligned(start, size):
+    return pl.ds(pl.multiple_of(start, HEAD_DIM), size)
+
+
+def kernel_call(body, outputs, operands, spaces, scratch=(), out_space=pltpu.VMEM):
+    operands = [
+        pltpu.with_memory_space_constraint(each, pltpu.HBM) if space is pltpu.HBM else each
+        for each, space in zip(operands, spaces)
+    ]
+    return pl.pallas_call(
+        body,
+        out_shape=[jax.ShapeDtypeStruct(shape, jnp.bfloat16) for shape in outputs],
+        in_specs=[pl.BlockSpec(memory_space=space) for space in spaces],
+        out_specs=[pl.BlockSpec(memory_space=out_space)] * len(outputs),
+        scratch_shapes=list(scratch),
+        compiler_params=pltpu.CompilerParams(vmem_limit_bytes=KERNEL_VMEM),
+    )(*operands)
+
+
+def decode_kernel(queries_hbm, codes_hbm, exps_hbm, away_ref, home_ref, home_queries_ref, codes_ref, exps_ref, sems):
+    rows, half = home_queries_ref.shape
+    uly = lax.axis_index("uly")
+    starts = ((1 - uly) * half, uly * half)
+    fetch_exps = pltpu.make_async_copy(exps_hbm, exps_ref, sems.at[0])
+    fetch_exps.start()
+    fetch_codes = []
+    for start in starts:
+        for kind in range(2):
+            slot = len(fetch_codes)
+            fetch_codes.append(
+                pltpu.make_async_copy(codes_hbm.at[:, kind, aligned(start, half)], codes_ref.at[slot], sems.at[1 + slot])
+            )
+            fetch_codes[slot].start()
+    fetch_queries = []
+    for side, target in enumerate((away_ref.at[pl.ds(2 * rows, rows)], home_queries_ref)):
+        fetch_queries.append(pltpu.make_async_copy(queries_hbm.at[:, aligned(starts[side], half)], target, sems.at[5 + side]))
+        fetch_queries[side].start()
+    blocks = exps_ref.shape[2]
+    block_of = lax.broadcasted_iota(jnp.int32, (blocks, half), 1) // SCALE_BLOCK
+    row_of = lax.broadcasted_iota(jnp.int32, (blocks, half), 0)
+    fetch_exps.wait()
+    scales = jnp.concatenate([jnp.exp2(exps_ref[:, kind, :].astype(jnp.float32)) for kind in range(2)], axis=0)
+    scales = scales.astype(jnp.bfloat16)
+    spreads = [(row_of == block_of + start // SCALE_BLOCK).astype(jnp.float32).astype(jnp.bfloat16) for start in starts]
+    wide_scales = [jnp.dot(scales, spread, preferred_element_type=jnp.float32) for spread in spreads]
+    for side, out_ref in enumerate((away_ref, home_ref)):
+        for kind in range(2):
+            fetch_codes[2 * side + kind].wait()
+            own_rows = slice(kind * rows, (kind + 1) * rows)
+            decoded = codes_ref[2 * side + kind].astype(jnp.float32) * wide_scales[side][own_rows]
+            out_ref[own_rows, :] = decoded.astype(jnp.bfloat16)
+    for fetch in fetch_queries:
+        fetch.wait()
+
+
+def decode_halves(queries, codes, exps):
+    rows, model_width = queries.shape
+    half = model_width // lax.axis_size("uly")
+    return kernel_call(
+        decode_kernel,
+        [(3 * rows, half), (2 * rows, half), (rows, half)],
+        [queries, codes, exps],
+        [pltpu.HBM] * 3,
+        [
+            pltpu.VMEM((4, rows, half), codes.dtype),
+            pltpu.VMEM(exps.shape, exps.dtype),
+            pltpu.SemaphoreType.DMA((7,)),
+        ],
+    )
+
+
+def lane_groups(heads):
+    lane = lax.broadcasted_iota(jnp.int32, (1, HEAD_DIM), 1)
+    return [(lane >= group * heads) & (lane < (group + 1) * heads) for group in range(2 * SPLIT_TERMS)], lane
+
+
+def pack_stats(maxima, totals):
+    heads = len(maxima)
+    groups, lane = lane_groups(heads)
+    is_maximum = lane < SPLIT_TERMS * heads
+    left = jnp.zeros((maxima[0].shape[0], HEAD_DIM), jnp.float32)
+    for head in range(heads):
+        here = lane == head
+        for group in range(1, 2 * SPLIT_TERMS):
+            here = here | (lane == head + group * heads)
+        left = jnp.where(here, jnp.where(is_maximum, maxima[head], totals[head]), left)
+    packed = jnp.zeros_like(left)
+    for term in range(SPLIT_TERMS):
+        rounded = left.astype(jnp.bfloat16).astype(jnp.float32)
+        packed = jnp.where(groups[term] | groups[SPLIT_TERMS + term], rounded, packed)
+        left = left - rounded
+    return packed.astype(jnp.bfloat16)
+
+
+def unpack_stats(packed, heads):
+    terms = packed.astype(jnp.float32)
+    summed = terms
+    for term in range(1, SPLIT_TERMS):
+        summed = summed + pltpu.roll(terms, HEAD_DIM - term * heads, 1)
+    return summed, pltpu.roll(summed, HEAD_DIM - SPLIT_TERMS * heads, 1)
+
+
+def attend_kernel(stale_ref, query_parts, key_value_parts, out_refs):
+    rows = query_parts[0].shape[0]
+    width = query_parts[0].shape[1]
+    patch = lax.axis_index("patch")
+    uly = lax.axis_index("uly")
+    heads = range(width // HEAD_DIM)
+
+    def refreshed(kind):
+        parts = []
+        for block, part_ref in enumerate(key_value_parts):
+            home = (patch ^ (block & 2)) * 2 + (uly ^ (block & 1))
+            stale = stale_ref[kind, pl.ds(pl.multiple_of(home * rows, rows), rows), :]
+            parts.append(refresh(stale, part_ref[kind * rows : (kind + 1) * rows, :]))
+        return jnp.concatenate(parts, axis=0)
+
+    query_rows = jnp.concatenate([part_ref[...] for part_ref in query_parts], axis=0)
+    key_rows = refreshed(0)
+    scores = [head_scores(query_rows, key_rows, head) for head in heads]
+    value_rows = refreshed(1)
+    maxima = [jnp.max(each, axis=1, keepdims=True) for each in scores]
+    weights = [jnp.exp(each - maximum) for each, maximum in zip(scores, maxima)]
+    sums = [weigh_values(weights[head], value_rows, head) for head in heads]
+    totals = [jnp.sum(each, axis=1, keepdims=True) for each in weights]
+    for head in heads:
+        result = (sums[head] / totals[head]).astype(jnp.bfloat16)
+        for block, out_ref in enumerate(out_refs):
+            out_ref[:, head * HEAD_DIM : (head + 1) * HEAD_DIM] = result[block * rows : (block + 1) * rows]
+    stats = pack_stats(maxima, totals)
+    for block, out_ref in enumerate(out_refs):
+        out_ref[:, width : width + HEAD_DIM] = stats[block * rows : (block + 1) * rows]
+
+
+def attend_partly(home, home_queries, arrived, own_stale):
+    rows, width = home_queries.shape
+
+    def body(home_ref, home_queries_ref, *refs):
+        named = dict(zip(START_ORDER, refs))
+        stale_ref, *out_refs = refs[len(START_ORDER) :]
+        query_parts = (home_queries_ref, named[1].at[pl.ds(2 * rows, rows)], named[2], named[3])
+        attend_kernel(stale_ref, query_parts, (home_ref, named[1], named[4], named[5]), out_refs)
+
+    operands = [home, home_queries, *(arrived[name] for name in START_ORDER), own_stale]
+    return kernel_call(body, [(rows, width + HEAD_DIM)] * 4, operands, [pltpu.VMEM] * len(operands))
+
+
+def merge_kernel(part_refs, mixed_hbm, mixed_ref, sems):
+    rows, packed_width = part_refs[0].shape
+    width = packed_width - HEAD_DIM
+    heads = width // HEAD_DIM
+    uly = lax.axis_index("uly")
+    stats = [unpack_stats(part_ref[:, width:], heads) for part_ref in part_refs]
+    used = lax.broadcasted_iota(jnp.int32, (1, HEAD_DIM), 1) < heads
+    shares = []
+    for near, far in ((0, 2), (1, 3)):
+        top = jnp.maximum(stats[near][0], stats[far][0])
+        near_total = stats[near][1] * jnp.exp(stats[near][0] - top)
+        far_total = stats[far][1] * jnp.exp(stats[far][0] - top)
+        share = jnp.where(used, near_total / (near_total + far_total), 0.0)
+        high = share.astype(jnp.bfloat16)
+        shares += [high, (share - high.astype(jnp.float32)).astype(jnp.bfloat16)]
+    head_of = lax.broadcasted_iota(jnp.int32, (HEAD_DIM, width), 1) // HEAD_DIM
+    spread = (lax.broadcasted_iota(jnp.int32, (HEAD_DIM, width), 0) == head_of).astype(jnp.float32).astype(jnp.bfloat16)
+    wide = jnp.dot(jnp.concatenate(shares, axis=0), spread, preferred_element_type=jnp.float32)
+    copies = []
+    for side, (near, far) in enumerate(((0, 2), (1, 3))):
+        share = wide[2 * side * rows : (2 * side + 1) * rows] + wide[(2 * side + 1) * rows : (2 * side + 2) * rows]
+        far_rows = part_refs[far][:, :width].astype(jnp.float32)
+        near_rows = part_refs[near][:, :width].astype(jnp.float32)
+        mixed_ref[side] = (far_rows + (near_rows - far_rows) * share).astype(jnp.bfloat16)
+        columns = aligned((uly if side == 0 else 1 - uly) * width, width)
+        copies.append(pltpu.make_async_copy(mixed_ref.at[side], mixed_hbm.at[:, columns], sems.at[side]))
+        copies[side].start()
+    for copy in copies:
+        copy.wait()
+
+
+def merge(parts):
+    rows, packed_width = parts[0].shape
+    width = packed_width - HEAD_DIM
+    names = (0, *RETURN_ORDER)
+
+    def body(*refs):
+        named = dict(zip(names, refs))
+        merge_kernel([named[block] for block in range(4)], *refs[4:])
+
+    (mixed,) = kernel_call(
+        body,
+        [(rows, 2 * width)],
+        [parts[name] for name in names],
+        [pltpu.VMEM] * 4,
+        [pltpu.VMEM((2, rows, width), jnp.bfloat16), pltpu.SemaphoreType.DMA((2,))],
+        out_space=pltpu.HBM,
+    )
+    return mixed
+
+
+def swap(array, distance):
+    count = lax.axis_size(BOTH)
+    return lax.ppermute(array, BOTH, [(peer, peer ^ distance) for peer in range(count)])
+
+
+def attend_paired(queries, stale_kv, codes, exps):
+    kv_rows = 2 * queries.shape[0]
+    away, home, home_queries = decode_halves(queries, codes, exps)
+    home, stale_kv = lax.optimization_barrier((home, stale_kv))
+    own_stale = jnp.swapaxes(stale_kv, 0, 1)
+    blocks = {1: away, 2: home_queries, 3: away[kv_rows:], 4: home, 5: away[:kv_rows]}
+    arrived = {distance: swap(blocks[distance], distance) for distance in START_ORDER}
+    parts = attend_partly(home, home_queries, arrived, own_stale)
+    return merge([parts[0]] + [swap(parts[distance], distance) for distance in (1, 2, 3)])
+
+
+def on_device(queries, stale_kv, codes, exps):
+    if lax.axis_size("patch") == 4 and lax.axis_size("uly") == 2:
+        return attend_paired(queries, stale_kv, codes, exps)
+    return attend_gathered(queries, stale_kv, codes, exps)
 
 
 def solution(mesh):

time: 96 us -> 23.8 us (0.25)
  local copies, waits for them, and re-layouts: 41.8 us -> 0.09 us
  blocking collectives: 28.6 us -> 0 us
  matrix products: 5.54 us -> 0 us
  starting transfers between devices: 7 us -> 12.5 us
  other arithmetic: 4.29 us -> 0 us
  Pallas kernels: 0 us -> 2.72 us
    all_gather x1 -> x0, blocking collectives: 21.3 us -> none  [on_device(): gathered = lax.all_gather(residual, 'patch', axis=0, tiled=True)]
    unnamed x17 -> x2, local copies, waits for them, and re-layouts: 16 us -> 0.01 us
    all_to_all x3 -> x0, local copies, waits for them, and re-layouts: 13.2 us -> none  [the longest x1 11.9 us: on_device(): lax.all_to_all(blocked, 'uly', split_axis=3, concat_axis=1, tiled=True)]
    ppermute x0 -> x8, starting transfers between devices: none -> 12.5 us  [swap(): lax.ppermute(array, BOTH, [(peer, peer ^ distance) for peer in range(coun...]
    reshape x1 -> x0, local copies, waits for them, and re-layouts: 10.4 us -> none  [on_device(): gathered.reshape(patch_count, residual.shape[0], 2, residual.shape[2])]
    ppermute x0 -> x8, waiting for transfers between devices: none -> 8.28 us  [swap(): lax.ppermute(array, BOTH, [(peer, peer ^ distance) for peer in range(coun...]
    all_to_all x2 -> x0, waiting for transfers between devices: 7.75 us -> none  [the longest x1 7.74 us: on_device(): lax.all_to_all(blocked, 'uly', split_axis=3, concat_axis=1, tiled=True)]
    all_to_all x1 -> x0, blocking collectives: 7.35 us -> none  [on_device(): lax.all_to_all(result, 'uly', split_axis=0, concat_axis=1, tiled=True)]
  transfers between devices with their start and end apart: 2 -> 8, of which waited for: 1 -> 5; matrix products, arithmetic and copies ran while one was open for 21% -> 0% of each run, Pallas kernels for 0% -> 0%
where the time goes in v5:
time: 23.8 us; the launch traced here: 23.6 us
  starting transfers between devices  12.5 us (53%)
  waiting for transfers between devices  8.28 us (35%)
  Pallas kernels  2.72 us (11%)
    ppermute x8, starting transfers between devices, swap(): lax.ppermute(array, BOTH, [(peer, peer ^ distance) for peer in range(coun...  12.5 us
    ppermute x8, waiting for transfers between devices, swap(): lax.ppermute(array, BOTH, [(peer, peer ^ distance) for peer in range(coun...  8.28 us
    pallas_call x3, Pallas kernels, kernel_call(): pl.pallas_call(body, out_shape=[jax.ShapeDtypeStruct(shape, jnp.bfloat16)...  2.72 us
  transfers between devices with their start and end apart: 8, of which 5 were waited for; matrix products, arithmetic and copies ran while one was open for 0% of the time, Pallas kernels for 0%

profile of v5, /device:TPU:0, one launch (start us, length us, event | category | flops | bytes accessed | tf_op | source)
XLA Modules:
  0.0 23.6 jit_solution(5708824659136246858)
XLA Ops:
  0.0 0.0 copy-start
  0.0 1.3 %shard_map.46 = (bf16[48,1536]{1,0:T(8,128)(2,1)S(1)}, bf16[32,1536]{1,0:T(8,128)(2,1)S(1)}, bf16[16,1536]{1,0:T(8,128)(2,1)S(1)}) custom-call(bf16[16,3072]{1,0:T(8,128)(2,1)} %queries_hbm.1, s32[16,2,3072]{2,1,0:T(2,128)} %codes_hbm.1, s32[16,2,24]{2,1,0:T(2,128)} %exps_hbm.1), custom_call_target="tpu_custom_call" | custom-call | tf_op jit(solution)/shard_map/pallas_call | solution.py:91
  1.3 3.0 %collective-permute-start.2 = (bf16[48,1536]{1,0:T(8,128)(2,1)S(1)}, bf16[48,1536]{1,0:T(8,128)(2,1)S(1)}, u32[]{:S(2)}, u32[]{:S(2)}) collective-permute-start(bf16[48,1536]{1,0:T(8,128)(2,1)S(1)} %get-tuple-element.17), channel_id=1, source_target_pairs={{0,4},{4,0},{8,12},{12,8},{16,20},{20,16},{24,28},{28,24},{1,5},{5... | collective-permute-start | bytes 442376 | tf_op jit(solution)/shard_map/ppermute | solution.py:282
  4.3 2.6 %collective-permute-start = (bf16[32,1536]{1,0:T(8,128)(2,1)S(1)}, bf16[32,1536]{1,0:T(8,128)(2,1)S(1)}, u32[]{:S(2)}, u32[]{:S(2)}) collective-permute-start(bf16[32,1536]{1,0:T(8,128)(2,1)S(1)} %slice.6), channel_id=1, source_target_pairs={{0,20},{4,16},{8,28},{12,24},{16,4},{20,0},{24,12},{28,8},{1,21},{... | collective-permute-start | bytes 294920 | tf_op jit(solution)/shard_map/ppermute | solution.py:282
  6.9 0.1 collective-permute-start.1
  7.0 2.7 %collective-permute-start.3 = (bf16[16,1536]{1,0:T(8,128)(2,1)S(1)}, bf16[16,1536]{1,0:T(8,128)(2,1)S(1)}, u32[]{:S(2)}, u32[]{:S(2)}) collective-permute-start(bf16[16,1536]{1,0:T(8,128)(2,1)S(1)} %slice.7), channel_id=1, source_target_pairs={{0,12},{4,8},{8,4},{12,0},{16,28},{20,24},{24,20},{28,16},{1,13},{... | collective-permute-start | bytes 147464 | tf_op jit(solution)/shard_map/ppermute | solution.py:282
  9.8 0.4 %collective-permute-start.4 = (bf16[16,1536]{1,0:T(8,128)(2,1)S(1)}, bf16[16,1536]{1,0:T(8,128)(2,1)S(1)}, u32[]{:S(2)}, u32[]{:S(2)}) collective-permute-start(bf16[16,1536]{1,0:T(8,128)(2,1)S(1)} %get-tuple-element.16.home_queries_ref), channel_id=1, source_target_pairs={{0,8},{4,12},{8,0},{12,4},{16,24},{20,28},{24,16},{28,20},{1,9},{5... | collective-permute-start | bytes 147464 | tf_op jit(solution)/shard_map/ppermute | solution.py:282
  10.2 0.0 copy-done
  10.2 0.1 copy.7
  10.3 2.1 %collective-permute-done.3.refs_3_ = bf16[16,1536]{1,0:T(8,128)(2,1)S(1)} collective-permute-done((bf16[16,1536]{1,0:T(8,128)(2,1)S(1)}, bf16[16,1536]{1,0:T(8,128)(2,1)S(1)}, u32[]{:S(2)}, u32[]{:S(2)}) %collective-permute-start.3) | collective-permute-done | bytes 49184 | tf_op jit(solution)/shard_map/ppermute | solution.py:282
  12.4 3.6 %collective-permute-done.4.refs_4_ = bf16[16,1536]{1,0:T(8,128)(2,1)S(1)} collective-permute-done((bf16[16,1536]{1,0:T(8,128)(2,1)S(1)}, bf16[16,1536]{1,0:T(8,128)(2,1)S(1)}, u32[]{:S(2)}, u32[]{:S(2)}) %collective-permute-start.4) | collective-permute-done | bytes 49184 | tf_op jit(solution)/shard_map/ppermute | solution.py:282
  16.1 0.0 collective-permute-done.refs_0_
  16.1 0.0 collective-permute-done.1.refs_1_
  16.1 0.0 collective-permute-done.2.refs_2_
  16.1 0.5 %shard_map.47 = (bf16[16,1664]{1,0:T(8,128)(2,1)S(1)}, bf16[16,1664]{1,0:T(8,128)(2,1)S(1)}, bf16[16,1664]{1,0:T(8,128)(2,1)S(1)}, bf16[16,1664]{1,0:T(8,128)(2,1)S(1)}) custom-call(bf16[32,1536]{1,0:T(8,128)(2,1)S(1)} %get-tuple-element.15.home_ref, bf16[16,1536]{1,0:T(8,128)(2,1)S(1)} %get-tuple-element.16.home_queries_ref, ...), custom_call_target="tpu_custom_call" | custom-call | tf_op jit(solution)/shard_map/pallas_call | solution.py:91
  16.6 1.4 %collective-permute-start.5 = (bf16[16,1664]{1,0:T(8,128)(2,1)S(1)}, bf16[16,1664]{1,0:T(8,128)(2,1)S(1)}, u32[]{:S(2)}, u32[]{:S(2)}) collective-permute-start(bf16[16,1664]{1,0:T(8,128)(2,1)S(1)} %get-tuple-element.20), channel_id=1, source_target_pairs={{0,12},{4,8},{8,4},{12,0},{16,28},{20,24},{24,20},{28,16},{1,13},{... | collective-permute-start | bytes 159752 | tf_op jit(solution)/shard_map/ppermute | solution.py:282
  18.0 0.6 %collective-permute-start.6 = (bf16[16,1664]{1,0:T(8,128)(2,1)S(1)}, bf16[16,1664]{1,0:T(8,128)(2,1)S(1)}, u32[]{:S(2)}, u32[]{:S(2)}) collective-permute-start(bf16[16,1664]{1,0:T(8,128)(2,1)S(1)} %get-tuple-element.21), channel_id=1, source_target_pairs={{0,4},{4,0},{8,12},{12,8},{16,20},{20,16},{24,28},{28,24},{1,5},{5... | collective-permute-start | bytes 159752 | tf_op jit(solution)/shard_map/ppermute | solution.py:282
  18.5 1.6 %collective-permute-start.7 = (bf16[16,1664]{1,0:T(8,128)(2,1)S(1)}, bf16[16,1664]{1,0:T(8,128)(2,1)S(1)}, u32[]{:S(2)}, u32[]{:S(2)}) collective-permute-start(bf16[16,1664]{1,0:T(8,128)(2,1)S(1)} %get-tuple-element.22), channel_id=1, source_target_pairs={{0,8},{4,12},{8,0},{12,4},{16,24},{20,28},{24,16},{28,20},{1,9},{5... | collective-permute-start | bytes 159752 | tf_op jit(solution)/shard_map/ppermute | solution.py:282
  20.1 1.8 %collective-permute-done.5.refs_1_ = bf16[16,1664]{1,0:T(8,128)(2,1)S(1)} collective-permute-done((bf16[16,1664]{1,0:T(8,128)(2,1)S(1)}, bf16[16,1664]{1,0:T(8,128)(2,1)S(1)}, u32[]{:S(2)}, u32[]{:S(2)}) %collective-permute-start.5) | collective-permute-done | bytes 53280 | tf_op jit(solution)/shard_map/ppermute | solution.py:282
  21.9 0.4 %collective-permute-done.6.refs_2_ = bf16[16,1664]{1,0:T(8,128)(2,1)S(1)} collective-permute-done((bf16[16,1664]{1,0:T(8,128)(2,1)S(1)}, bf16[16,1664]{1,0:T(8,128)(2,1)S(1)}, u32[]{:S(2)}, u32[]{:S(2)}) %collective-permute-start.6) | collective-permute-done | bytes 53280 | tf_op jit(solution)/shard_map/ppermute | solution.py:282
  22.3 0.4 %collective-permute-done.7.refs_3_ = bf16[16,1664]{1,0:T(8,128)(2,1)S(1)} collective-permute-done((bf16[16,1664]{1,0:T(8,128)(2,1)S(1)}, bf16[16,1664]{1,0:T(8,128)(2,1)S(1)}, u32[]{:S(2)}, u32[]{:S(2)}) %collective-permute-start.7) | collective-permute-done | bytes 53280 | tf_op jit(solution)/shard_map/ppermute | solution.py:282
  22.6 1.0 %shard_map.48 = bf16[16,3072]{1,0:T(8,128)(2,1)} custom-call(bf16[16,1664]{1,0:T(8,128)(2,1)S(1)} %get-tuple-element.19.refs_0_, bf16[16,1664]{1,0:T(8,128)(2,1)S(1)} %collective-permute-done.5.refs_1_, bf16[16,1664]{1,0:T(8,128)(2,1)S(1)} %collective-permute-done.6.refs_2_, bf16[16,1664]{1,0:T(8,128)(2,1)S(1)} %collective-permute-done.7.refs_3_), custom_call_target="tpu_custom_call" | custom-call | tf_op jit(solution)/shard_map/pallas_call | solution.py:91
  (2 shorter events, 0.0 us)
Async XLA Ops:
  0.0 10.2 %copy-start = (bf16[128,2,1536]{2,1,0:T(2,128)(2,1)S(1)}, bf16[128,2,1536]{2,1,0:T(2,128)(2,1)}, u32[]{:S(2)}) copy-start(bf16[128,2,1536]{2,1,0:T(2,128)(2,1)} %param.5) | copy-start | bytes 2359300
  1.3 14.8 %collective-permute-start.2 = (bf16[48,1536]{1,0:T(8,128)(2,1)S(1)}, bf16[48,1536]{1,0:T(8,128)(2,1)S(1)}, u32[]{:S(2)}, u32[]{:S(2)}) collective-permute-start(bf16[48,1536]{1,0:T(8,128)(2,1)S(1)} %get-tuple-element.17), channel_id=1, source_target_pairs={{0,4},{4,0},{8,12},{12,8},{16,20},{20,16},{24,28},{28,24},{1,5},{5... | collective-permute-start | bytes 442376 | tf_op jit(solution)/shard_map/ppermute | solution.py:282
  4.3 11.7 %collective-permute-start = (bf16[32,1536]{1,0:T(8,128)(2,1)S(1)}, bf16[32,1536]{1,0:T(8,128)(2,1)S(1)}, u32[]{:S(2)}, u32[]{:S(2)}) collective-permute-start(bf16[32,1536]{1,0:T(8,128)(2,1)S(1)} %slice.6), channel_id=1, source_target_pairs={{0,20},{4,16},{8,28},{12,24},{16,4},{20,0},{24,12},{28,8},{1,21},{... | collective-permute-start | bytes 294920 | tf_op jit(solution)/shard_map/ppermute | solution.py:282
  6.9 9.2 %collective-permute-start.1 = (bf16[32,1536]{1,0:T(8,128)(2,1)S(1)}, bf16[32,1536]{1,0:T(8,128)(2,1)S(1)}, u32[]{:S(2)}, u32[]{:S(2)}) collective-permute-start(bf16[32,1536]{1,0:T(8,128)(2,1)S(1)} %get-tuple-element.15.home_ref), channel_id=1, source_target_pairs={{0,16},{4,20},{8,24},{12,28},{16,0},{20,4},{24,8},{28,12},{1,17},{... | collective-permute-start | bytes 294920 | tf_op jit(solution)/shard_map/ppermute | solution.py:282
  7.0 5.4 %collective-permute-start.3 = (bf16[16,1536]{1,0:T(8,128)(2,1)S(1)}, bf16[16,1536]{1,0:T(8,128)(2,1)S(1)}, u32[]{:S(2)}, u32[]{:S(2)}) collective-permute-start(bf16[16,1536]{1,0:T(8,128)(2,1)S(1)} %slice.7), channel_id=1, source_target_pairs={{0,12},{4,8},{8,4},{12,0},{16,28},{20,24},{24,20},{28,16},{1,13},{... | collective-permute-start | bytes 147464 | tf_op jit(solution)/shard_map/ppermute | solution.py:282
  9.8 6.3 %collective-permute-start.4 = (bf16[16,1536]{1,0:T(8,128)(2,1)S(1)}, bf16[16,1536]{1,0:T(8,128)(2,1)S(1)}, u32[]{:S(2)}, u32[]{:S(2)}) collective-permute-start(bf16[16,1536]{1,0:T(8,128)(2,1)S(1)} %get-tuple-element.16.home_queries_ref), channel_id=1, source_target_pairs={{0,8},{4,12},{8,0},{12,4},{16,24},{20,28},{24,16},{28,20},{1,9},{5... | collective-permute-start | bytes 147464 | tf_op jit(solution)/shard_map/ppermute | solution.py:282
  16.6 5.4 %collective-permute-start.5 = (bf16[16,1664]{1,0:T(8,128)(2,1)S(1)}, bf16[16,1664]{1,0:T(8,128)(2,1)S(1)}, u32[]{:S(2)}, u32[]{:S(2)}) collective-permute-start(bf16[16,1664]{1,0:T(8,128)(2,1)S(1)} %get-tuple-element.20), channel_id=1, source_target_pairs={{0,12},{4,8},{8,4},{12,0},{16,28},{20,24},{24,20},{28,16},{1,13},{... | collective-permute-start | bytes 159752 | tf_op jit(solution)/shard_map/ppermute | solution.py:282
  18.0 4.3 %collective-permute-start.6 = (bf16[16,1664]{1,0:T(8,128)(2,1)S(1)}, bf16[16,1664]{1,0:T(8,128)(2,1)S(1)}, u32[]{:S(2)}, u32[]{:S(2)}) collective-permute-start(bf16[16,1664]{1,0:T(8,128)(2,1)S(1)} %get-tuple-element.21), channel_id=1, source_target_pairs={{0,4},{4,0},{8,12},{12,8},{16,20},{20,16},{24,28},{28,24},{1,5},{5... | collective-permute-start | bytes 159752 | tf_op jit(solution)/shard_map/ppermute | solution.py:282
  18.5 4.1 %collective-permute-start.7 = (bf16[16,1664]{1,0:T(8,128)(2,1)S(1)}, bf16[16,1664]{1,0:T(8,128)(2,1)S(1)}, u32[]{:S(2)}, u32[]{:S(2)}) collective-permute-start(bf16[16,1664]{1,0:T(8,128)(2,1)S(1)} %get-tuple-element.22), channel_id=1, source_target_pairs={{0,8},{4,12},{8,0},{12,4},{16,24},{20,28},{24,16},{28,20},{1,9},{5... | collective-permute-start | bytes 159752 | tf_op jit(solution)/shard_map/ppermute | solution.py:282

commit v6 on v5

--- a/solution.py
+++ b/solution.py
@@ -12,8 +12,7 @@
 SCALE_BLOCK = 128
 KERNEL_VMEM = 8 << 20
 BOTH = ("patch", "uly")
-START_ORDER = (5, 4, 1, 3, 2)
-RETURN_ORDER = (3, 1, 2)
+RETURN_ORDER = (3, 2, 1)
 SPLIT_TERMS = 3
 
 
@@ -191,7 +190,7 @@
     def refreshed(kind):
         parts = []
         for block, part_ref in enumerate(key_value_parts):
-            home = (patch ^ (block & 2)) * 2 + (uly ^ (block & 1))
+            home = (patch ^ (block >> 1)) * 2 + (uly ^ (block & 1))
             stale = stale_ref[kind, pl.ds(pl.multiple_of(home * rows, rows), rows), :]
             parts.append(refresh(stale, part_ref[kind * rows : (kind + 1) * rows, :]))
         return jnp.concatenate(parts, axis=0)
@@ -213,16 +212,20 @@
         out_ref[:, width : width + HEAD_DIM] = stats[block * rows : (block + 1) * rows]
 
 
-def attend_partly(home, home_queries, arrived, own_stale):
+def attend_partly(home, home_queries, beside, near, far_queries, own_stale):
     rows, width = home_queries.shape
 
-    def body(home_ref, home_queries_ref, *refs):
-        named = dict(zip(START_ORDER, refs))
-        stale_ref, *out_refs = refs[len(START_ORDER) :]
-        query_parts = (home_queries_ref, named[1].at[pl.ds(2 * rows, rows)], named[2], named[3])
-        attend_kernel(stale_ref, query_parts, (home_ref, named[1], named[4], named[5]), out_refs)
-
-    operands = [home, home_queries, *(arrived[name] for name in START_ORDER), own_stale]
+    def body(home_ref, home_queries_ref, beside_ref, same_ref, diagonal_ref, far_ref, far_beside_ref, stale_ref, *out_refs):
+        own_columns = aligned(lax.axis_index("uly") * width, width)
+        query_parts = (
+            home_queries_ref,
+            beside_ref.at[pl.ds(2 * rows, rows)],
+            far_ref.at[:, own_columns],
+            far_beside_ref,
+        )
+        attend_kernel(stale_ref, query_parts, (home_ref, beside_ref, same_ref, diagonal_ref), out_refs)
+
+    operands = [home, home_queries, beside, *near, *far_queries, own_stale]
     return kernel_call(body, [(rows, width + HEAD_DIM)] * 4, operands, [pltpu.VMEM] * len(operands))
 
 
@@ -284,13 +287,17 @@
 
 def attend_paired(queries, stale_kv, codes, exps):
     kv_rows = 2 * queries.shape[0]
+    half = stale_kv.shape[2]
+    far = swap(queries, 4)
     away, home, home_queries = decode_halves(queries, codes, exps)
     home, stale_kv = lax.optimization_barrier((home, stale_kv))
     own_stale = jnp.swapaxes(stale_kv, 0, 1)
-    blocks = {1: away, 2: home_queries, 3: away[kv_rows:], 4: home, 5: away[:kv_rows]}
-    arrived = {distance: swap(blocks[distance], distance) for distance in START_ORDER}
-    parts = attend_partly(home, home_queries, arrived, own_stale)
-    return merge([parts[0]] + [swap(parts[distance], distance) for distance in (1, 2, 3)])
+    beside = swap(away, 1)
+    near = [swap(home, 2), swap(away[:kv_rows], 3)]
+    handed = lax.dynamic_slice(far, (0, (1 - lax.axis_index("uly")) * half), (far.shape[0], half))
+    far_queries = [far, swap(handed, 1)]
+    parts = attend_partly(home, home_queries, beside, near, far_queries, own_stale)
+    return merge([parts[0]] + [swap(part, distance) for part, distance in zip(parts[1:], (1, 4, 5))])
 
 
 def on_device(queries, stale_kv, codes, exps):

time: 23.8 us -> 23.5 us (0.987)
  waiting for transfers between devices: 8.28 us -> 6.87 us
  starting transfers between devices: 12.5 us -> 13.7 us
    ppermute x8, waiting for transfers between devices: 8.28 us -> 6.87 us  [swap(): lax.ppermute(array, BOTH, [(peer, peer ^ distance) for peer in range(coun...]
    ppermute x8, starting transfers between devices: 12.5 us -> 13.7 us  [swap(): lax.ppermute(array, BOTH, [(peer, peer ^ distance) for peer in range(coun...]
  transfers between devices with their start and end apart: 8 -> 8, of which waited for: 5 -> 6; matrix products, arithmetic and copies ran while one was open for 0% -> 0% of each run, Pallas kernels for 0% -> 5%
where the time goes in v6:
time: 23.5 us; the launch traced here: 23.3 us
  starting transfers between devices  13.7 us (58%)
  waiting for transfers between devices  6.87 us (29%)
  Pallas kernels  2.63 us (11%)
    ppermute x8, starting transfers between devices, swap(): lax.ppermute(array, BOTH, [(peer, peer ^ distance) for peer in range(coun...  13.7 us
    ppermute x8, waiting for transfers between devices, swap(): lax.ppermute(array, BOTH, [(peer, peer ^ distance) for peer in range(coun...  6.87 us
    pallas_call x3, Pallas kernels, kernel_call(): pl.pallas_call(body, out_shape=[jax.ShapeDtypeStruct(shape, jnp.bfloat16)...  2.63 us
  transfers between devices with their start and end apart: 8, of which 6 were waited for; matrix products, arithmetic and copies ran while one was open for 0% of the time, Pallas kernels for 5%

profile of v6, /device:TPU:0, one launch (start us, length us, event | category | flops | bytes accessed | tf_op | source)
XLA Modules:
  0.0 23.3 jit_solution(103062308230006776)
XLA Ops:
  0.0 0.0 copy-start
  0.0 4.0 %collective-permute-start.3 = (bf16[16,3072]{1,0:T(8,128)(2,1)}, bf16[16,3072]{1,0:T(8,128)(2,1)S(1)}, u32[]{:S(2)}, u32[]{:S(2)}) collective-permute-start(bf16[16,3072]{1,0:T(8,128)(2,1)} %queries_hbm.1), channel_id=1, source_target_pairs={{0,16},{4,20},{8,24},{12,28},{16,0},{20,4},{24,8},{28,12},{1,17},{... | collective-permute-start | bytes 294920 | tf_op jit(solution)/shard_map/ppermute | solution.py:285
  4.0 1.2 %shard_map.46 = (bf16[48,1536]{1,0:T(8,128)(2,1)S(1)}, bf16[32,1536]{1,0:T(8,128)(2,1)S(1)}, bf16[16,1536]{1,0:T(8,128)(2,1)S(1)}) custom-call(bf16[16,3072]{1,0:T(8,128)(2,1)} %queries_hbm.1, s32[16,2,3072]{2,1,0:T(2,128)} %codes_hbm.1, s32[16,2,24]{2,1,0:T(2,128)} %exps_hbm.1), custom_call_target="tpu_custom_call" | custom-call | tf_op jit(solution)/shard_map/pallas_call | solution.py:90
  5.2 1.6 %collective-permute-start = (bf16[48,1536]{1,0:T(8,128)(2,1)S(1)}, bf16[48,1536]{1,0:T(8,128)(2,1)S(1)}, u32[]{:S(2)}, u32[]{:S(2)}) collective-permute-start(bf16[48,1536]{1,0:T(8,128)(2,1)S(1)} %get-tuple-element.17), channel_id=1, source_target_pairs={{0,4},{4,0},{8,12},{12,8},{16,20},{20,16},{24,28},{28,24},{1,5},{5... | collective-permute-start | bytes 442376 | tf_op jit(solution)/shard_map/ppermute | solution.py:285
  6.8 1.6 %collective-permute-start.2 = (bf16[32,1536]{1,0:T(8,128)(2,1)S(1)}, bf16[32,1536]{1,0:T(8,128)(2,1)S(1)}, u32[]{:S(2)}, u32[]{:S(2)}) collective-permute-start(bf16[32,1536]{1,0:T(8,128)(2,1)S(1)} %slice.3), channel_id=1, source_target_pairs={{0,12},{4,8},{8,4},{12,0},{16,28},{20,24},{24,20},{28,16},{1,13},{... | collective-permute-start | bytes 294920 | tf_op jit(solution)/shard_map/ppermute | solution.py:285
  8.4 0.4 %collective-permute-start.1 = (bf16[32,1536]{1,0:T(8,128)(2,1)S(1)}, bf16[32,1536]{1,0:T(8,128)(2,1)S(1)}, u32[]{:S(2)}, u32[]{:S(2)}) collective-permute-start(bf16[32,1536]{1,0:T(8,128)(2,1)S(1)} %get-tuple-element.15.home_ref), channel_id=1, source_target_pairs={{0,8},{4,12},{8,0},{12,4},{16,24},{20,28},{24,16},{28,20},{1,9},{5... | collective-permute-start | bytes 294920 | tf_op jit(solution)/shard_map/ppermute | solution.py:285
  8.9 0.3 %collective-permute-done.3.far_ref = bf16[16,3072]{1,0:T(8,128)(2,1)S(1)} collective-permute-done((bf16[16,3072]{1,0:T(8,128)(2,1)}, bf16[16,3072]{1,0:T(8,128)(2,1)S(1)}, u32[]{:S(2)}, u32[]{:S(2)}) %collective-permute-start.3) | collective-permute-done | bytes 98336 | tf_op jit(solution)/shard_map/ppermute | solution.py:285
  9.2 1.6 %collective-permute-start.4 = (bf16[16,1536]{1,0:T(8,128)(2,1)S(1)}, bf16[16,1536]{1,0:T(8,128)(2,1)S(1)}, u32[]{:S(2)}, u32[]{:S(2)}) collective-permute-start(bf16[16,1536]{1,0:T(8,128)(2,1)S(1)} %constant_dynamic-slice_fusion), channel_id=1, source_target_pairs={{0,4},{4,0},{8,12},{12,8},{16,20},{20,16},{24,28},{28,24},{1,5},{5... | collective-permute-start | bytes 147464 | tf_op jit(solution)/shard_map/ppermute | solution.py:285
  10.8 0.0 copy-done
  10.8 0.1 copy.7
  10.9 2.5 %collective-permute-done.2.diagonal_ref = bf16[32,1536]{1,0:T(8,128)(2,1)S(1)} collective-permute-done((bf16[32,1536]{1,0:T(8,128)(2,1)S(1)}, bf16[32,1536]{1,0:T(8,128)(2,1)S(1)}, u32[]{:S(2)}, u32[]{:S(2)}) %collective-permute-start.2) | collective-permute-done | bytes 98336 | tf_op jit(solution)/shard_map/ppermute | solution.py:285
  13.4 0.0 collective-permute-done.1.same_ref
  13.4 0.4 %collective-permute-done.4.far_beside_ref = bf16[16,1536]{1,0:T(8,128)(2,1)S(1)} collective-permute-done((bf16[16,1536]{1,0:T(8,128)(2,1)S(1)}, bf16[16,1536]{1,0:T(8,128)(2,1)S(1)}, u32[]{:S(2)}, u32[]{:S(2)}) %collective-permute-start.4) | collective-permute-done | bytes 49184 | tf_op jit(solution)/shard_map/ppermute | solution.py:285
  13.8 0.0 collective-permute-done.beside_ref
  13.8 0.5 %shard_map.47 = (bf16[16,1664]{1,0:T(8,128)(2,1)S(1)}, bf16[16,1664]{1,0:T(8,128)(2,1)S(1)}, bf16[16,1664]{1,0:T(8,128)(2,1)S(1)}, bf16[16,1664]{1,0:T(8,128)(2,1)S(1)}) custom-call(bf16[32,1536]{1,0:T(8,128)(2,1)S(1)} %get-tuple-element.15.home_ref, bf16[16,1536]{1,0:T(8,128)(2,1)S(1)} %get-tuple-element.16.home_queries_ref, ...), custom_call_target="tpu_custom_call" | custom-call | tf_op jit(solution)/shard_map/pallas_call | solution.py:90
  14.2 1.7 %collective-permute-start.5 = (bf16[16,1664]{1,0:T(8,128)(2,1)S(1)}, bf16[16,1664]{1,0:T(8,128)(2,1)S(1)}, u32[]{:S(2)}, u32[]{:S(2)}) collective-permute-start(bf16[16,1664]{1,0:T(8,128)(2,1)S(1)} %get-tuple-element.20), channel_id=1, source_target_pairs={{0,20},{4,16},{8,28},{12,24},{16,4},{20,0},{24,12},{28,8},{1,21},{... | collective-permute-start | bytes 159752 | tf_op jit(solution)/shard_map/ppermute | solution.py:285
  15.9 2.3 %collective-permute-start.6 = (bf16[16,1664]{1,0:T(8,128)(2,1)S(1)}, bf16[16,1664]{1,0:T(8,128)(2,1)S(1)}, u32[]{:S(2)}, u32[]{:S(2)}) collective-permute-start(bf16[16,1664]{1,0:T(8,128)(2,1)S(1)} %get-tuple-element.21), channel_id=1, source_target_pairs={{0,16},{4,20},{8,24},{12,28},{16,0},{20,4},{24,8},{28,12},{1,17},{... | collective-permute-start | bytes 159752 | tf_op jit(solution)/shard_map/ppermute | solution.py:285
  18.2 0.5 %collective-permute-start.7 = (bf16[16,1664]{1,0:T(8,128)(2,1)S(1)}, bf16[16,1664]{1,0:T(8,128)(2,1)S(1)}, u32[]{:S(2)}, u32[]{:S(2)}) collective-permute-start(bf16[16,1664]{1,0:T(8,128)(2,1)S(1)} %get-tuple-element.22), channel_id=1, source_target_pairs={{0,4},{4,0},{8,12},{12,8},{16,20},{20,16},{24,28},{28,24},{1,5},{5... | collective-permute-start | bytes 159752 | tf_op jit(solution)/shard_map/ppermute | solution.py:285
  18.7 1.7 %collective-permute-done.5.refs_1_ = bf16[16,1664]{1,0:T(8,128)(2,1)S(1)} collective-permute-done((bf16[16,1664]{1,0:T(8,128)(2,1)S(1)}, bf16[16,1664]{1,0:T(8,128)(2,1)S(1)}, u32[]{:S(2)}, u32[]{:S(2)}) %collective-permute-start.5) | collective-permute-done | bytes 53280 | tf_op jit(solution)/shard_map/ppermute | solution.py:285
  20.4 1.7 %collective-permute-done.6.refs_2_ = bf16[16,1664]{1,0:T(8,128)(2,1)S(1)} collective-permute-done((bf16[16,1664]{1,0:T(8,128)(2,1)S(1)}, bf16[16,1664]{1,0:T(8,128)(2,1)S(1)}, u32[]{:S(2)}, u32[]{:S(2)}) %collective-permute-start.6) | collective-permute-done | bytes 53280 | tf_op jit(solution)/shard_map/ppermute | solution.py:285
  22.1 0.2 collective-permute-done.7.refs_3_
  22.3 1.0 %shard_map.48 = bf16[16,3072]{1,0:T(8,128)(2,1)} custom-call(bf16[16,1664]{1,0:T(8,128)(2,1)S(1)} %get-tuple-element.19.refs_0_, bf16[16,1664]{1,0:T(8,128)(2,1)S(1)} %collective-permute-done.5.refs_1_, bf16[16,1664]{1,0:T(8,128)(2,1)S(1)} %collective-permute-done.6.refs_2_, bf16[16,1664]{1,0:T(8,128)(2,1)S(1)} %collective-permute-done.7.refs_3_), custom_call_target="tpu_custom_call" | custom-call | tf_op jit(solution)/shard_map/pallas_call | solution.py:90
  (2 shorter events, 0.0 us)
Async XLA Ops:
  0.0 10.8 %copy-start = (bf16[128,2,1536]{2,1,0:T(2,128)(2,1)S(1)}, bf16[128,2,1536]{2,1,0:T(2,128)(2,1)}, u32[]{:S(2)}) copy-start(bf16[128,2,1536]{2,1,0:T(2,128)(2,1)} %param.5) | copy-start | bytes 2359300
  0.0 9.2 %collective-permute-start.3 = (bf16[16,3072]{1,0:T(8,128)(2,1)}, bf16[16,3072]{1,0:T(8,128)(2,1)S(1)}, u32[]{:S(2)}, u32[]{:S(2)}) collective-permute-start(bf16[16,3072]{1,0:T(8,128)(2,1)} %queries_hbm.1), channel_id=1, source_target_pairs={{0,16},{4,20},{8,24},{12,28},{16,0},{20,4},{24,8},{28,12},{1,17},{... | collective-permute-start | bytes 294920 | tf_op jit(solution)/shard_map/ppermute | solution.py:285
  5.2 8.5 %collective-permute-start = (bf16[48,1536]{1,0:T(8,128)(2,1)S(1)}, bf16[48,1536]{1,0:T(8,128)(2,1)S(1)}, u32[]{:S(2)}, u32[]{:S(2)}) collective-permute-start(bf16[48,1536]{1,0:T(8,128)(2,1)S(1)} %get-tuple-element.17), channel_id=1, source_target_pairs={{0,4},{4,0},{8,12},{12,8},{16,20},{20,16},{24,28},{28,24},{1,5},{5... | collective-permute-start | bytes 442376 | tf_op jit(solution)/shard_map/ppermute | solution.py:285
  6.8 6.6 %collective-permute-start.2 = (bf16[32,1536]{1,0:T(8,128)(2,1)S(1)}, bf16[32,1536]{1,0:T(8,128)(2,1)S(1)}, u32[]{:S(2)}, u32[]{:S(2)}) collective-permute-start(bf16[32,1536]{1,0:T(8,128)(2,1)S(1)} %slice.3), channel_id=1, source_target_pairs={{0,12},{4,8},{8,4},{12,0},{16,28},{20,24},{24,20},{28,16},{1,13},{... | collective-permute-start | bytes 294920 | tf_op jit(solution)/shard_map/ppermute | solution.py:285
  8.4 5.0 %collective-permute-start.1 = (bf16[32,1536]{1,0:T(8,128)(2,1)S(1)}, bf16[32,1536]{1,0:T(8,128)(2,1)S(1)}, u32[]{:S(2)}, u32[]{:S(2)}) collective-permute-start(bf16[32,1536]{1,0:T(8,128)(2,1)S(1)} %get-tuple-element.15.home_ref), channel_id=1, source_target_pairs={{0,8},{4,12},{8,0},{12,4},{16,24},{20,28},{24,16},{28,20},{1,9},{5... | collective-permute-start | bytes 294920 | tf_op jit(solution)/shard_map/ppermute | solution.py:285
  9.2 4.6 %collective-permute-start.4 = (bf16[16,1536]{1,0:T(8,128)(2,1)S(1)}, bf16[16,1536]{1,0:T(8,128)(2,1)S(1)}, u32[]{:S(2)}, u32[]{:S(2)}) collective-permute-start(bf16[16,1536]{1,0:T(8,128)(2,1)S(1)} %constant_dynamic-slice_fusion), channel_id=1, source_target_pairs={{0,4},{4,0},{8,12},{12,8},{16,20},{20,16},{24,28},{28,24},{1,5},{5... | collective-permute-start | bytes 147464 | tf_op jit(solution)/shard_map/ppermute | solution.py:285
  14.2 6.2 %collective-permute-start.5 = (bf16[16,1664]{1,0:T(8,128)(2,1)S(1)}, bf16[16,1664]{1,0:T(8,128)(2,1)S(1)}, u32[]{:S(2)}, u32[]{:S(2)}) collective-permute-start(bf16[16,1664]{1,0:T(8,128)(2,1)S(1)} %get-tuple-element.20), channel_id=1, source_target_pairs={{0,20},{4,16},{8,28},{12,24},{16,4},{20,0},{24,12},{28,8},{1,21},{... | collective-permute-start | bytes 159752 | tf_op jit(solution)/shard_map/ppermute | solution.py:285
  15.9 6.2 %collective-permute-start.6 = (bf16[16,1664]{1,0:T(8,128)(2,1)S(1)}, bf16[16,1664]{1,0:T(8,128)(2,1)S(1)}, u32[]{:S(2)}, u32[]{:S(2)}) collective-permute-start(bf16[16,1664]{1,0:T(8,128)(2,1)S(1)} %get-tuple-element.21), channel_id=1, source_target_pairs={{0,16},{4,20},{8,24},{12,28},{16,0},{20,4},{24,8},{28,12},{1,17},{... | collective-permute-start | bytes 159752 | tf_op jit(solution)/shard_map/ppermute | solution.py:285
  18.2 4.1 %collective-permute-start.7 = (bf16[16,1664]{1,0:T(8,128)(2,1)S(1)}, bf16[16,1664]{1,0:T(8,128)(2,1)S(1)}, u32[]{:S(2)}, u32[]{:S(2)}) collective-permute-start(bf16[16,1664]{1,0:T(8,128)(2,1)S(1)} %get-tuple-element.22), channel_id=1, source_target_pairs={{0,4},{4,0},{8,12},{12,8},{16,20},{20,16},{24,28},{28,24},{1,5},{5... | collective-permute-start | bytes 159752 | tf_op jit(solution)/shard_map/ppermute | solution.py:285

commit v7 on v6

--- a/solution.py
+++ b/solution.py
@@ -12,8 +12,10 @@
 SCALE_BLOCK = 128
 KERNEL_VMEM = 8 << 20
 BOTH = ("patch", "uly")
-RETURN_ORDER = (3, 2, 1)
+RETURN_ORDER = (3, 1, 2)
 SPLIT_TERMS = 3
+KEY, QUERY = 0, 1
+FAR_QUERY_PARITY = 1
 
 
 def decode(codes, exps):
@@ -185,12 +187,14 @@
     width = query_parts[0].shape[1]
     patch = lax.axis_index("patch")
     uly = lax.axis_index("uly")
+    odd = lax.rem(lax.axis_index("rep"), 2)
+    key_step = steps_of(0)[KEY] + odd * (steps_of(1)[KEY] - steps_of(0)[KEY])
     heads = range(width // HEAD_DIM)
 
     def refreshed(kind):
         parts = []
         for block, part_ref in enumerate(key_value_parts):
-            home = (patch ^ (block >> 1)) * 2 + (uly ^ (block & 1))
+            home = (patch ^ ((block >> 1) * key_step)) * 2 + (uly ^ (block & 1))
             stale = stale_ref[kind, pl.ds(pl.multiple_of(home * rows, rows), rows), :]
             parts.append(refresh(stale, part_ref[kind * rows : (kind + 1) * rows, :]))
         return jnp.concatenate(parts, axis=0)
@@ -280,24 +284,34 @@
     return mixed
 
 
-def swap(array, distance):
-    count = lax.axis_size(BOTH)
-    return lax.ppermute(array, BOTH, [(peer, peer ^ distance) for peer in range(count)])
+def steps_of(rep):
+    return (1, 2) if rep % 2 == FAR_QUERY_PARITY else (2, 1)
+
+
+def swap(array, role, uly):
+    peers = lax.axis_size(BOTH)
+    pairs = []
+    reps = lax.axis_size("rep")
+    for rep in range(reps):
+        step = 0 if role is None else steps_of(rep)[role]
+        pairs += [(peer * reps + rep, (peer ^ (2 * step + uly)) * reps + rep) for peer in range(peers)]
+    return lax.ppermute(array, (*BOTH, "rep"), pairs)
 
 
 def attend_paired(queries, stale_kv, codes, exps):
     kv_rows = 2 * queries.shape[0]
     half = stale_kv.shape[2]
-    far = swap(queries, 4)
+    far = swap(queries, QUERY, 0)
     away, home, home_queries = decode_halves(queries, codes, exps)
     home, stale_kv = lax.optimization_barrier((home, stale_kv))
     own_stale = jnp.swapaxes(stale_kv, 0, 1)
-    beside = swap(away, 1)
-    near = [swap(home, 2), swap(away[:kv_rows], 3)]
+    beside = swap(away, None, 1)
+    near = [swap(home, KEY, 0), swap(away[:kv_rows], KEY, 1)]
     handed = lax.dynamic_slice(far, (0, (1 - lax.axis_index("uly")) * half), (far.shape[0], half))
-    far_queries = [far, swap(handed, 1)]
+    far_queries = [far, swap(handed, None, 1)]
     parts = attend_partly(home, home_queries, beside, near, far_queries, own_stale)
-    return merge([parts[0]] + [swap(part, distance) for part, distance in zip(parts[1:], (1, 4, 5))])
+    homes = ((None, 1), (QUERY, 0), (QUERY, 1))
+    return merge([parts[0]] + [swap(part, *home) for part, home in zip(parts[1:], homes)])
 
 
 def on_device(queries, stale_kv, codes, exps):

time: 23.5 us -> 22.9 us (0.974)
  starting transfers between devices: 13.7 us -> 12.7 us
  waiting for transfers between devices: 6.87 us -> 7.3 us
    ppermute x8, starting transfers between devices: 13.7 us -> 12.7 us  [swap(): return lax.ppermute(array, (*BOTH, 'rep'), pairs)]
    ppermute x8, waiting for transfers between devices: 6.87 us -> 7.3 us  [swap(): return lax.ppermute(array, (*BOTH, 'rep'), pairs)]
  transfers between devices with their start and end apart: 8 -> 8, of which waited for: 6 -> 4; matrix products, arithmetic and copies ran while one was open for 0% -> 0% of each run, Pallas kernels for 5% -> 5%
where the time goes in v7:
time: 22.9 us; the launch traced here: 22.7 us
  starting transfers between devices  12.7 us (55%)
  waiting for transfers between devices  7.3 us (32%)
  Pallas kernels  2.64 us (12%)
    ppermute x8, starting transfers between devices, swap(): return lax.ppermute(array, (*BOTH, 'rep'), pairs)  12.7 us
    ppermute x8, waiting for transfers between devices, swap(): return lax.ppermute(array, (*BOTH, 'rep'), pairs)  7.3 us
    pallas_call x3, Pallas kernels, kernel_call(): pl.pallas_call(body, out_shape=[jax.ShapeDtypeStruct(shape, jnp.bfloat16)...  2.64 us
  transfers between devices with their start and end apart: 8, of which 4 were waited for; matrix products, arithmetic and copies ran while one was open for 0% of the time, Pallas kernels for 5%

profile of v7, /device:TPU:0, one launch (start us, length us, event | category | flops | bytes accessed | tf_op | source)
XLA Modules:
  0.0 22.7 jit_solution(18430640959182864129)
XLA Ops:
  0.0 0.0 copy-start
  0.0 3.0 %collective-permute-start.3 = (bf16[16,3072]{1,0:T(8,128)(2,1)}, bf16[16,3072]{1,0:T(8,128)(2,1)S(1)}, u32[]{:S(2)}, u32[]{:S(2)}) collective-permute-start(bf16[16,3072]{1,0:T(8,128)(2,1)} %queries_hbm.1), channel_id=1, source_target_pairs={{0,8},{4,12},{8,0},{12,4},{16,24},{20,28},{24,16},{28,20},{1,17},{... | collective-permute-start | bytes 294920 | tf_op jit(solution)/shard_map/ppermute | solution.py:298
  3.0 1.2 %shard_map.46 = (bf16[48,1536]{1,0:T(8,128)(2,1)S(1)}, bf16[32,1536]{1,0:T(8,128)(2,1)S(1)}, bf16[16,1536]{1,0:T(8,128)(2,1)S(1)}) custom-call(bf16[16,3072]{1,0:T(8,128)(2,1)} %queries_hbm.1, s32[16,2,3072]{2,1,0:T(2,128)} %codes_hbm.1, s32[16,2,24]{2,1,0:T(2,128)} %exps_hbm.1), custom_call_target="tpu_custom_call" | custom-call | tf_op jit(solution)/shard_map/pallas_call | solution.py:92
  4.2 1.6 %collective-permute-start = (bf16[48,1536]{1,0:T(8,128)(2,1)S(1)}, bf16[48,1536]{1,0:T(8,128)(2,1)S(1)}, u32[]{:S(2)}, u32[]{:S(2)}) collective-permute-start(bf16[48,1536]{1,0:T(8,128)(2,1)S(1)} %get-tuple-element.17), channel_id=1, source_target_pairs={{0,4},{4,0},{8,12},{12,8},{16,20},{20,16},{24,28},{28,24},{1,5},{5... | collective-permute-start | bytes 442376 | tf_op jit(solution)/shard_map/ppermute | solution.py:298
  5.8 2.6 %collective-permute-start.2 = (bf16[32,1536]{1,0:T(8,128)(2,1)S(1)}, bf16[32,1536]{1,0:T(8,128)(2,1)S(1)}, u32[]{:S(2)}, u32[]{:S(2)}) collective-permute-start(bf16[32,1536]{1,0:T(8,128)(2,1)S(1)} %slice.3), channel_id=1, source_target_pairs={{0,20},{4,16},{8,28},{12,24},{16,4},{20,0},{24,12},{28,8},{1,13},{... | collective-permute-start | bytes 294920 | tf_op jit(solution)/shard_map/ppermute | solution.py:298
  8.4 0.3 %collective-permute-start.1 = (bf16[32,1536]{1,0:T(8,128)(2,1)S(1)}, bf16[32,1536]{1,0:T(8,128)(2,1)S(1)}, u32[]{:S(2)}, u32[]{:S(2)}) collective-permute-start(bf16[32,1536]{1,0:T(8,128)(2,1)S(1)} %get-tuple-element.15.home_ref), channel_id=1, source_target_pairs={{0,16},{4,20},{8,24},{12,28},{16,0},{20,4},{24,8},{28,12},{1,9},{5... | collective-permute-start | bytes 294920 | tf_op jit(solution)/shard_map/ppermute | solution.py:298
  8.7 0.0 collective-permute-done.3.far_ref
  8.8 1.6 %collective-permute-start.4 = (bf16[16,1536]{1,0:T(8,128)(2,1)S(1)}, bf16[16,1536]{1,0:T(8,128)(2,1)S(1)}, u32[]{:S(2)}, u32[]{:S(2)}) collective-permute-start(bf16[16,1536]{1,0:T(8,128)(2,1)S(1)} %constant_dynamic-slice_fusion), channel_id=1, source_target_pairs={{0,4},{4,0},{8,12},{12,8},{16,20},{20,16},{24,28},{28,24},{1,5},{5... | collective-permute-start | bytes 147464 | tf_op jit(solution)/shard_map/ppermute | solution.py:298
  10.3 0.0 copy-done
  10.3 0.1 copy.7
  10.4 2.9 %collective-permute-done.2.diagonal_ref = bf16[32,1536]{1,0:T(8,128)(2,1)S(1)} collective-permute-done((bf16[32,1536]{1,0:T(8,128)(2,1)S(1)}, bf16[32,1536]{1,0:T(8,128)(2,1)S(1)}, u32[]{:S(2)}, u32[]{:S(2)}) %collective-permute-start.2) | collective-permute-done | bytes 98336 | tf_op jit(solution)/shard_map/ppermute | solution.py:298
  13.3 1.5 %collective-permute-done.1.same_ref = bf16[32,1536]{1,0:T(8,128)(2,1)S(1)} collective-permute-done((bf16[32,1536]{1,0:T(8,128)(2,1)S(1)}, bf16[32,1536]{1,0:T(8,128)(2,1)S(1)}, u32[]{:S(2)}, u32[]{:S(2)}) %collective-permute-start.1) | collective-permute-done | bytes 98336 | tf_op jit(solution)/shard_map/ppermute | solution.py:298
  14.9 0.0 collective-permute-done.4.far_beside_ref
  14.9 0.0 collective-permute-done.beside_ref
  14.9 0.5 %shard_map.47 = (bf16[16,1664]{1,0:T(8,128)(2,1)S(1)}, bf16[16,1664]{1,0:T(8,128)(2,1)S(1)}, bf16[16,1664]{1,0:T(8,128)(2,1)S(1)}, bf16[16,1664]{1,0:T(8,128)(2,1)S(1)}) custom-call(bf16[32,1536]{1,0:T(8,128)(2,1)S(1)} %get-tuple-element.15.home_ref, bf16[16,1536]{1,0:T(8,128)(2,1)S(1)} %get-tuple-element.16.home_queries_ref, ...), custom_call_target="tpu_custom_call" | custom-call | tf_op jit(solution)/shard_map/pallas_call | solution.py:92
  15.3 0.6 %collective-permute-start.5 = (bf16[16,1664]{1,0:T(8,128)(2,1)S(1)}, bf16[16,1664]{1,0:T(8,128)(2,1)S(1)}, u32[]{:S(2)}, u32[]{:S(2)}) collective-permute-start(bf16[16,1664]{1,0:T(8,128)(2,1)S(1)} %get-tuple-element.20), channel_id=1, source_target_pairs={{0,12},{4,8},{8,4},{12,0},{16,28},{20,24},{24,20},{28,16},{1,21},{... | collective-permute-start | bytes 159752 | tf_op jit(solution)/shard_map/ppermute | solution.py:298
  16.0 1.0 %collective-permute-start.6 = (bf16[16,1664]{1,0:T(8,128)(2,1)S(1)}, bf16[16,1664]{1,0:T(8,128)(2,1)S(1)}, u32[]{:S(2)}, u32[]{:S(2)}) collective-permute-start(bf16[16,1664]{1,0:T(8,128)(2,1)S(1)} %get-tuple-element.21), channel_id=1, source_target_pairs={{0,4},{4,0},{8,12},{12,8},{16,20},{20,16},{24,28},{28,24},{1,5},{5... | collective-permute-start | bytes 159752 | tf_op jit(solution)/shard_map/ppermute | solution.py:298
  17.0 1.9 %collective-permute-start.7 = (bf16[16,1664]{1,0:T(8,128)(2,1)S(1)}, bf16[16,1664]{1,0:T(8,128)(2,1)S(1)}, u32[]{:S(2)}, u32[]{:S(2)}) collective-permute-start(bf16[16,1664]{1,0:T(8,128)(2,1)S(1)} %get-tuple-element.22), channel_id=1, source_target_pairs={{0,8},{4,12},{8,0},{12,4},{16,24},{20,28},{24,16},{28,20},{1,17},{... | collective-permute-start | bytes 159752 | tf_op jit(solution)/shard_map/ppermute | solution.py:298
  18.9 2.0 %collective-permute-done.5.refs_1_ = bf16[16,1664]{1,0:T(8,128)(2,1)S(1)} collective-permute-done((bf16[16,1664]{1,0:T(8,128)(2,1)S(1)}, bf16[16,1664]{1,0:T(8,128)(2,1)S(1)}, u32[]{:S(2)}, u32[]{:S(2)}) %collective-permute-start.5) | collective-permute-done | bytes 53280 | tf_op jit(solution)/shard_map/ppermute | solution.py:298
  20.9 0.0 collective-permute-done.6.refs_2_
  20.9 0.9 %collective-permute-done.7.refs_3_ = bf16[16,1664]{1,0:T(8,128)(2,1)S(1)} collective-permute-done((bf16[16,1664]{1,0:T(8,128)(2,1)S(1)}, bf16[16,1664]{1,0:T(8,128)(2,1)S(1)}, u32[]{:S(2)}, u32[]{:S(2)}) %collective-permute-start.7) | collective-permute-done | bytes 53280 | tf_op jit(solution)/shard_map/ppermute | solution.py:298
  21.8 1.0 %shard_map.48 = bf16[16,3072]{1,0:T(8,128)(2,1)} custom-call(bf16[16,1664]{1,0:T(8,128)(2,1)S(1)} %get-tuple-element.19.refs_0_, bf16[16,1664]{1,0:T(8,128)(2,1)S(1)} %collective-permute-done.5.refs_1_, bf16[16,1664]{1,0:T(8,128)(2,1)S(1)} %collective-permute-done.6.refs_2_, bf16[16,1664]{1,0:T(8,128)(2,1)S(1)} %collective-permute-done.7.refs_3_), custom_call_target="tpu_custom_call" | custom-call | tf_op jit(solution)/shard_map/pallas_call | solution.py:92
  (2 shorter events, 0.0 us)
Async XLA Ops:
  0.0 10.3 %copy-start = (bf16[128,2,1536]{2,1,0:T(2,128)(2,1)S(1)}, bf16[128,2,1536]{2,1,0:T(2,128)(2,1)}, u32[]{:S(2)}) copy-start(bf16[128,2,1536]{2,1,0:T(2,128)(2,1)} %param.5) | copy-start | bytes 2359300
  0.0 8.7 %collective-permute-start.3 = (bf16[16,3072]{1,0:T(8,128)(2,1)}, bf16[16,3072]{1,0:T(8,128)(2,1)S(1)}, u32[]{:S(2)}, u32[]{:S(2)}) collective-permute-start(bf16[16,3072]{1,0:T(8,128)(2,1)} %queries_hbm.1), channel_id=1, source_target_pairs={{0,8},{4,12},{8,0},{12,4},{16,24},{20,28},{24,16},{28,20},{1,17},{... | collective-permute-start | bytes 294920 | tf_op jit(solution)/shard_map/ppermute | solution.py:298
  4.2 10.6 %collective-permute-start = (bf16[48,1536]{1,0:T(8,128)(2,1)S(1)}, bf16[48,1536]{1,0:T(8,128)(2,1)S(1)}, u32[]{:S(2)}, u32[]{:S(2)}) collective-permute-start(bf16[48,1536]{1,0:T(8,128)(2,1)S(1)} %get-tuple-element.17), channel_id=1, source_target_pairs={{0,4},{4,0},{8,12},{12,8},{16,20},{20,16},{24,28},{28,24},{1,5},{5... | collective-permute-start | bytes 442376 | tf_op jit(solution)/shard_map/ppermute | solution.py:298
  5.8 7.5 %collective-permute-start.2 = (bf16[32,1536]{1,0:T(8,128)(2,1)S(1)}, bf16[32,1536]{1,0:T(8,128)(2,1)S(1)}, u32[]{:S(2)}, u32[]{:S(2)}) collective-permute-start(bf16[32,1536]{1,0:T(8,128)(2,1)S(1)} %slice.3), channel_id=1, source_target_pairs={{0,20},{4,16},{8,28},{12,24},{16,4},{20,0},{24,12},{28,8},{1,13},{... | collective-permute-start | bytes 294920 | tf_op jit(solution)/shard_map/ppermute | solution.py:298
  8.4 6.5 %collective-permute-start.1 = (bf16[32,1536]{1,0:T(8,128)(2,1)S(1)}, bf16[32,1536]{1,0:T(8,128)(2,1)S(1)}, u32[]{:S(2)}, u32[]{:S(2)}) collective-permute-start(bf16[32,1536]{1,0:T(8,128)(2,1)S(1)} %get-tuple-element.15.home_ref), channel_id=1, source_target_pairs={{0,16},{4,20},{8,24},{12,28},{16,0},{20,4},{24,8},{28,12},{1,9},{5... | collective-permute-start | bytes 294920 | tf_op jit(solution)/shard_map/ppermute | solution.py:298
  8.8 6.1 %collective-permute-start.4 = (bf16[16,1536]{1,0:T(8,128)(2,1)S(1)}, bf16[16,1536]{1,0:T(8,128)(2,1)S(1)}, u32[]{:S(2)}, u32[]{:S(2)}) collective-permute-start(bf16[16,1536]{1,0:T(8,128)(2,1)S(1)} %constant_dynamic-slice_fusion), channel_id=1, source_target_pairs={{0,4},{4,0},{8,12},{12,8},{16,20},{20,16},{24,28},{28,24},{1,5},{5... | collective-permute-start | bytes 147464 | tf_op jit(solution)/shard_map/ppermute | solution.py:298
  15.3 5.5 %collective-permute-start.5 = (bf16[16,1664]{1,0:T(8,128)(2,1)S(1)}, bf16[16,1664]{1,0:T(8,128)(2,1)S(1)}, u32[]{:S(2)}, u32[]{:S(2)}) collective-permute-start(bf16[16,1664]{1,0:T(8,128)(2,1)S(1)} %get-tuple-element.20), channel_id=1, source_target_pairs={{0,12},{4,8},{8,4},{12,0},{16,28},{20,24},{24,20},{28,16},{1,21},{... | collective-permute-start | bytes 159752 | tf_op jit(solution)/shard_map/ppermute | solution.py:298
  16.0 4.9 %collective-permute-start.6 = (bf16[16,1664]{1,0:T(8,128)(2,1)S(1)}, bf16[16,1664]{1,0:T(8,128)(2,1)S(1)}, u32[]{:S(2)}, u32[]{:S(2)}) collective-permute-start(bf16[16,1664]{1,0:T(8,128)(2,1)S(1)} %get-tuple-element.21), channel_id=1, source_target_pairs={{0,4},{4,0},{8,12},{12,8},{16,20},{20,16},{24,28},{28,24},{1,5},{5... | collective-permute-start | bytes 159752 | tf_op jit(solution)/shard_map/ppermute | solution.py:298
  17.0 4.7 %collective-permute-start.7 = (bf16[16,1664]{1,0:T(8,128)(2,1)S(1)}, bf16[16,1664]{1,0:T(8,128)(2,1)S(1)}, u32[]{:S(2)}, u32[]{:S(2)}) collective-permute-start(bf16[16,1664]{1,0:T(8,128)(2,1)S(1)} %get-tuple-element.22), channel_id=1, source_target_pairs={{0,8},{4,12},{8,0},{12,4},{16,24},{20,28},{24,16},{28,20},{1,17},{... | collective-permute-start | bytes 159752 | tf_op jit(solution)/shard_map/ppermute | solution.py:298

commit v8 on v7

--- a/solution.py
+++ b/solution.py
@@ -14,6 +14,7 @@
 BOTH = ("patch", "uly")
 RETURN_ORDER = (3, 1, 2)
 SPLIT_TERMS = 3
+KEY_VALUE_ORDER = (2, 3, 1)
 KEY, QUERY = 0, 1
 FAR_QUERY_PARITY = 1
 
@@ -99,7 +100,9 @@
     )(*operands)
 
 
-def decode_kernel(queries_hbm, codes_hbm, exps_hbm, away_ref, home_ref, home_queries_ref, codes_ref, exps_ref, sems):
+def decode_kernel(
+    queries_hbm, codes_hbm, exps_hbm, away_ref, home_ref, away_queries_ref, home_queries_ref, codes_ref, exps_ref, sems
+):
     rows, half = home_queries_ref.shape
     uly = lax.axis_index("uly")
     starts = ((1 - uly) * half, uly * half)
@@ -114,7 +117,7 @@
             )
             fetch_codes[slot].start()
     fetch_queries = []
-    for side, target in enumerate((away_ref.at[pl.ds(2 * rows, rows)], home_queries_ref)):
+    for side, target in enumerate((away_queries_ref, home_queries_ref)):
         fetch_queries.append(pltpu.make_async_copy(queries_hbm.at[:, aligned(starts[side], half)], target, sems.at[5 + side]))
         fetch_queries[side].start()
     blocks = exps_ref.shape[2]
@@ -140,7 +143,7 @@
     half = model_width // lax.axis_size("uly")
     return kernel_call(
         decode_kernel,
-        [(3 * rows, half), (2 * rows, half), (rows, half)],
+        [(2 * rows, half)] * 2 + [(rows, half)] * 2,
         [queries, codes, exps],
         [pltpu.HBM] * 3,
         [
@@ -216,20 +219,17 @@
         out_ref[:, width : width + HEAD_DIM] = stats[block * rows : (block + 1) * rows]
 
 
-def attend_partly(home, home_queries, beside, near, far_queries, own_stale):
+def attend_partly(home, home_queries, key_values, other_queries, handed, own_stale):
     rows, width = home_queries.shape
 
-    def body(home_ref, home_queries_ref, beside_ref, same_ref, diagonal_ref, far_ref, far_beside_ref, stale_ref, *out_refs):
+    def body(home_ref, home_queries_ref, *refs):
+        named = dict(zip(KEY_VALUE_ORDER, refs))
+        other_ref, handed_ref, stale_ref, *out_refs = refs[len(KEY_VALUE_ORDER) :]
         own_columns = aligned(lax.axis_index("uly") * width, width)
-        query_parts = (
-            home_queries_ref,
-            beside_ref.at[pl.ds(2 * rows, rows)],
-            far_ref.at[:, own_columns],
-            far_beside_ref,
-        )
-        attend_kernel(stale_ref, query_parts, (home_ref, beside_ref, same_ref, diagonal_ref), out_refs)
-
-    operands = [home, home_queries, beside, *near, *far_queries, own_stale]
+        query_parts = (home_queries_ref, handed_ref.at[0], other_ref.at[:, own_columns], handed_ref.at[1])
+        attend_kernel(stale_ref, query_parts, (home_ref, *(named[block] for block in (1, 2, 3))), out_refs)
+
+    operands = [home, home_queries, *(key_values[block] for block in KEY_VALUE_ORDER), other_queries, handed, own_stale]
     return kernel_call(body, [(rows, width + HEAD_DIM)] * 4, operands, [pltpu.VMEM] * len(operands))
 
 
@@ -299,17 +299,15 @@
 
 
 def attend_paired(queries, stale_kv, codes, exps):
-    kv_rows = 2 * queries.shape[0]
     half = stale_kv.shape[2]
-    far = swap(queries, QUERY, 0)
-    away, home, home_queries = decode_halves(queries, codes, exps)
+    other = swap(queries, QUERY, 0)
+    away, home, away_queries, home_queries = decode_halves(queries, codes, exps)
     home, stale_kv = lax.optimization_barrier((home, stale_kv))
     own_stale = jnp.swapaxes(stale_kv, 0, 1)
-    beside = swap(away, None, 1)
-    near = [swap(home, KEY, 0), swap(away[:kv_rows], KEY, 1)]
-    handed = lax.dynamic_slice(far, (0, (1 - lax.axis_index("uly")) * half), (far.shape[0], half))
-    far_queries = [far, swap(handed, None, 1)]
-    parts = attend_partly(home, home_queries, beside, near, far_queries, own_stale)
+    key_values = {1: swap(away, None, 1), 2: swap(home, KEY, 0), 3: swap(away, KEY, 1)}
+    other_away = lax.dynamic_slice(other, (0, (1 - lax.axis_index("uly")) * half), (other.shape[0], half))
+    handed = swap(jnp.stack([away_queries, other_away]), None, 1)
+    parts = attend_partly(home, home_queries, key_values, other, handed, own_stale)
     homes = ((None, 1), (QUERY, 0), (QUERY, 1))
     return merge([parts[0]] + [swap(part, *home) for part, home in zip(parts[1:], homes)])
 

time: 22.9 us -> 22.6 us (0.987)
  no operation moved by 1% of the time
where the time goes in v8:
time: 22.6 us; the launch traced here: 22.5 us
  starting transfers between devices  12.6 us (56%)
  waiting for transfers between devices  7.1 us (31%)
  Pallas kernels  2.65 us (12%)
    ppermute x8, starting transfers between devices, swap(): return lax.ppermute(array, (*BOTH, 'rep'), pairs)  12.6 us
    ppermute x8, waiting for transfers between devices, swap(): return lax.ppermute(array, (*BOTH, 'rep'), pairs)  7.1 us
    pallas_call x3, Pallas kernels, kernel_call(): pl.pallas_call(body, out_shape=[jax.ShapeDtypeStruct(shape, jnp.bfloat16)...  2.65 us
  transfers between devices with their start and end apart: 8, of which 4 were waited for; matrix products, arithmetic and copies ran while one was open for 0% of the time, Pallas kernels for 5%

profile of v8, /device:TPU:0, one launch (start us, length us, event | category | flops | bytes accessed | tf_op | source)
XLA Modules:
  0.0 22.5 jit_solution(12882192000484930352)
XLA Ops:
  0.0 0.0 copy-start
  0.0 3.0 %collective-permute-start.3 = (bf16[16,3072]{1,0:T(8,128)(2,1)}, bf16[16,3072]{1,0:T(8,128)(2,1)S(1)}, u32[]{:S(2)}, u32[]{:S(2)}) collective-permute-start(bf16[16,3072]{1,0:T(8,128)(2,1)} %queries_hbm.1), channel_id=1, source_target_pairs={{0,8},{4,12},{8,0},{12,4},{16,24},{20,28},{24,16},{28,20},{1,17},{... | collective-permute-start | bytes 294920 | tf_op jit(solution)/shard_map/ppermute | solution.py:298
  3.0 1.2 %shard_map.46 = (bf16[32,1536]{1,0:T(8,128)(2,1)S(1)}, bf16[32,1536]{1,0:T(8,128)(2,1)S(1)}, bf16[16,1536]{1,0:T(8,128)(2,1)S(1)}, bf16[16,1536]{1,0:T(8,128)(2,1)S(1)}) custom-call(bf16[16,3072]{1,0:T(8,128)(2,1)} %queries_hbm.1, s32[16,2,3072]{2,1,0:T(2,128)} %codes_hbm.1, s32[16,2,24]{2,1,0:T(2,128)} %exps_hbm.1), custom_call_target="tpu_custom_call" | custom-call | tf_op jit(solution)/shard_map/pallas_call | solution.py:93
  4.2 1.6 %collective-permute-start.2 = (bf16[32,1536]{1,0:T(8,128)(2,1)S(1)}, bf16[32,1536]{1,0:T(8,128)(2,1)S(1)}, u32[]{:S(2)}, u32[]{:S(2)}) collective-permute-start(bf16[32,1536]{1,0:T(8,128)(2,1)S(1)} %get-tuple-element.18), channel_id=1, source_target_pairs={{0,4},{4,0},{8,12},{12,8},{16,20},{20,16},{24,28},{28,24},{1,5},{5... | collective-permute-start | bytes 294920 | tf_op jit(solution)/shard_map/ppermute | solution.py:298
  5.8 2.5 %collective-permute-start.1 = (bf16[32,1536]{1,0:T(8,128)(2,1)S(1)}, bf16[32,1536]{1,0:T(8,128)(2,1)S(1)}, u32[]{:S(2)}, u32[]{:S(2)}) collective-permute-start(bf16[32,1536]{1,0:T(8,128)(2,1)S(1)} %get-tuple-element.18), channel_id=1, source_target_pairs={{0,20},{4,16},{8,28},{12,24},{16,4},{20,0},{24,12},{28,8},{1,13},{... | collective-permute-start | bytes 294920 | tf_op jit(solution)/shard_map/ppermute | solution.py:298
  8.3 0.3 %collective-permute-start = (bf16[32,1536]{1,0:T(8,128)(2,1)S(1)}, bf16[32,1536]{1,0:T(8,128)(2,1)S(1)}, u32[]{:S(2)}, u32[]{:S(2)}) collective-permute-start(bf16[32,1536]{1,0:T(8,128)(2,1)S(1)} %get-tuple-element.16.home_ref), channel_id=1, source_target_pairs={{0,16},{4,20},{8,24},{12,28},{16,0},{20,4},{24,8},{28,12},{1,9},{5... | collective-permute-start | bytes 294920 | tf_op jit(solution)/shard_map/ppermute | solution.py:298
  8.7 0.0 collective-permute-done.3.refs_3_
  8.7 1.6 %collective-permute-start.4 = (bf16[2,16,1536]{2,1,0:T(8,128)(2,1)S(1)}, bf16[2,16,1536]{2,1,0:T(8,128)(2,1)S(1)}, u32[]{:S(2)}, u32[]{:S(2)}) collective-permute-start(bf16[2,16,1536]{2,1,0:T(8,128)(2,1)S(1)} %pad_maximum_fusion), channel_id=1, source_target_pairs={{0,4},{4,0},{8,12},{12,8},{16,20},{20,16},{24,28},{28,24},{1,5},{5... | collective-permute-start | bytes 294920 | tf_op jit(solution)/shard_map/ppermute | solution.py:298
  10.3 0.0 copy-done
  10.3 0.1 copy.7
  10.4 4.4 %collective-permute-done.refs_0_ = bf16[32,1536]{1,0:T(8,128)(2,1)S(1)} collective-permute-done((bf16[32,1536]{1,0:T(8,128)(2,1)S(1)}, bf16[32,1536]{1,0:T(8,128)(2,1)S(1)}, u32[]{:S(2)}, u32[]{:S(2)}) %collective-permute-start) | collective-permute-done | bytes 98336 | tf_op jit(solution)/shard_map/ppermute | solution.py:298
  14.8 0.0 collective-permute-done.2.refs_2_
  14.8 0.0 collective-permute-done.1.refs_1_
  14.8 0.0 collective-permute-done.4.refs_4_
  14.8 0.5 %shard_map.47 = (bf16[16,1664]{1,0:T(8,128)(2,1)S(1)}, bf16[16,1664]{1,0:T(8,128)(2,1)S(1)}, bf16[16,1664]{1,0:T(8,128)(2,1)S(1)}, bf16[16,1664]{1,0:T(8,128)(2,1)S(1)}) custom-call(bf16[32,1536]{1,0:T(8,128)(2,1)S(1)} %get-tuple-element.16.home_ref, bf16[16,1536]{1,0:T(8,128)(2,1)S(1)} %get-tuple-element.17.home_queries_ref, ...), custom_call_target="tpu_custom_call" | custom-call | tf_op jit(solution)/shard_map/pallas_call | solution.py:93
  15.3 0.8 %collective-permute-start.5 = (bf16[16,1664]{1,0:T(8,128)(2,1)S(1)}, bf16[16,1664]{1,0:T(8,128)(2,1)S(1)}, u32[]{:S(2)}, u32[]{:S(2)}) collective-permute-start(bf16[16,1664]{1,0:T(8,128)(2,1)S(1)} %get-tuple-element.22), channel_id=1, source_target_pairs={{0,12},{4,8},{8,4},{12,0},{16,28},{20,24},{24,20},{28,16},{1,21},{... | collective-permute-start | bytes 159752 | tf_op jit(solution)/shard_map/ppermute | solution.py:298
  16.1 1.3 %collective-permute-start.6 = (bf16[16,1664]{1,0:T(8,128)(2,1)S(1)}, bf16[16,1664]{1,0:T(8,128)(2,1)S(1)}, u32[]{:S(2)}, u32[]{:S(2)}) collective-permute-start(bf16[16,1664]{1,0:T(8,128)(2,1)S(1)} %get-tuple-element.23), channel_id=1, source_target_pairs={{0,4},{4,0},{8,12},{12,8},{16,20},{20,16},{24,28},{28,24},{1,5},{5... | collective-permute-start | bytes 159752 | tf_op jit(solution)/shard_map/ppermute | solution.py:298
  17.4 1.5 %collective-permute-start.7 = (bf16[16,1664]{1,0:T(8,128)(2,1)S(1)}, bf16[16,1664]{1,0:T(8,128)(2,1)S(1)}, u32[]{:S(2)}, u32[]{:S(2)}) collective-permute-start(bf16[16,1664]{1,0:T(8,128)(2,1)S(1)} %get-tuple-element.24), channel_id=1, source_target_pairs={{0,8},{4,12},{8,0},{12,4},{16,24},{20,28},{24,16},{28,20},{1,17},{... | collective-permute-start | bytes 159752 | tf_op jit(solution)/shard_map/ppermute | solution.py:298
  18.8 1.7 %collective-permute-done.5.refs_1_ = bf16[16,1664]{1,0:T(8,128)(2,1)S(1)} collective-permute-done((bf16[16,1664]{1,0:T(8,128)(2,1)S(1)}, bf16[16,1664]{1,0:T(8,128)(2,1)S(1)}, u32[]{:S(2)}, u32[]{:S(2)}) %collective-permute-start.5) | collective-permute-done | bytes 53280 | tf_op jit(solution)/shard_map/ppermute | solution.py:298
  20.6 0.2 %collective-permute-done.6.refs_2_ = bf16[16,1664]{1,0:T(8,128)(2,1)S(1)} collective-permute-done((bf16[16,1664]{1,0:T(8,128)(2,1)S(1)}, bf16[16,1664]{1,0:T(8,128)(2,1)S(1)}, u32[]{:S(2)}, u32[]{:S(2)}) %collective-permute-start.6) | collective-permute-done | bytes 53280 | tf_op jit(solution)/shard_map/ppermute | solution.py:298
  20.8 0.7 %collective-permute-done.7.refs_3_ = bf16[16,1664]{1,0:T(8,128)(2,1)S(1)} collective-permute-done((bf16[16,1664]{1,0:T(8,128)(2,1)S(1)}, bf16[16,1664]{1,0:T(8,128)(2,1)S(1)}, u32[]{:S(2)}, u32[]{:S(2)}) %collective-permute-start.7) | collective-permute-done | bytes 53280 | tf_op jit(solution)/shard_map/ppermute | solution.py:298
  21.5 1.0 %shard_map.48 = bf16[16,3072]{1,0:T(8,128)(2,1)} custom-call(bf16[16,1664]{1,0:T(8,128)(2,1)S(1)} %get-tuple-element.21.refs_0_, bf16[16,1664]{1,0:T(8,128)(2,1)S(1)} %collective-permute-done.5.refs_1_, bf16[16,1664]{1,0:T(8,128)(2,1)S(1)} %collective-permute-done.6.refs_2_, bf16[16,1664]{1,0:T(8,128)(2,1)S(1)} %collective-permute-done.7.refs_3_), custom_call_target="tpu_custom_call" | custom-call | tf_op jit(solution)/shard_map/pallas_call | solution.py:93
  (2 shorter events, 0.0 us)
Async XLA Ops:
  0.0 10.3 %copy-start = (bf16[128,2,1536]{2,1,0:T(2,128)(2,1)S(1)}, bf16[128,2,1536]{2,1,0:T(2,128)(2,1)}, u32[]{:S(2)}) copy-start(bf16[128,2,1536]{2,1,0:T(2,128)(2,1)} %param.5) | copy-start | bytes 2359300
  0.0 8.7 %collective-permute-start.3 = (bf16[16,3072]{1,0:T(8,128)(2,1)}, bf16[16,3072]{1,0:T(8,128)(2,1)S(1)}, u32[]{:S(2)}, u32[]{:S(2)}) collective-permute-start(bf16[16,3072]{1,0:T(8,128)(2,1)} %queries_hbm.1), channel_id=1, source_target_pairs={{0,8},{4,12},{8,0},{12,4},{16,24},{20,28},{24,16},{28,20},{1,17},{... | collective-permute-start | bytes 294920 | tf_op jit(solution)/shard_map/ppermute | solution.py:298
  4.2 10.6 %collective-permute-start.2 = (bf16[32,1536]{1,0:T(8,128)(2,1)S(1)}, bf16[32,1536]{1,0:T(8,128)(2,1)S(1)}, u32[]{:S(2)}, u32[]{:S(2)}) collective-permute-start(bf16[32,1536]{1,0:T(8,128)(2,1)S(1)} %get-tuple-element.18), channel_id=1, source_target_pairs={{0,4},{4,0},{8,12},{12,8},{16,20},{20,16},{24,28},{28,24},{1,5},{5... | collective-permute-start | bytes 294920 | tf_op jit(solution)/shard_map/ppermute | solution.py:298
  5.8 9.0 %collective-permute-start.1 = (bf16[32,1536]{1,0:T(8,128)(2,1)S(1)}, bf16[32,1536]{1,0:T(8,128)(2,1)S(1)}, u32[]{:S(2)}, u32[]{:S(2)}) collective-permute-start(bf16[32,1536]{1,0:T(8,128)(2,1)S(1)} %get-tuple-element.18), channel_id=1, source_target_pairs={{0,20},{4,16},{8,28},{12,24},{16,4},{20,0},{24,12},{28,8},{1,13},{... | collective-permute-start | bytes 294920 | tf_op jit(solution)/shard_map/ppermute | solution.py:298
  8.3 6.5 %collective-permute-start = (bf16[32,1536]{1,0:T(8,128)(2,1)S(1)}, bf16[32,1536]{1,0:T(8,128)(2,1)S(1)}, u32[]{:S(2)}, u32[]{:S(2)}) collective-permute-start(bf16[32,1536]{1,0:T(8,128)(2,1)S(1)} %get-tuple-element.16.home_ref), channel_id=1, source_target_pairs={{0,16},{4,20},{8,24},{12,28},{16,0},{20,4},{24,8},{28,12},{1,9},{5... | collective-permute-start | bytes 294920 | tf_op jit(solution)/shard_map/ppermute | solution.py:298
  8.7 6.1 %collective-permute-start.4 = (bf16[2,16,1536]{2,1,0:T(8,128)(2,1)S(1)}, bf16[2,16,1536]{2,1,0:T(8,128)(2,1)S(1)}, u32[]{:S(2)}, u32[]{:S(2)}) collective-permute-start(bf16[2,16,1536]{2,1,0:T(8,128)(2,1)S(1)} %pad_maximum_fusion), channel_id=1, source_target_pairs={{0,4},{4,0},{8,12},{12,8},{16,20},{20,16},{24,28},{28,24},{1,5},{5... | collective-permute-start | bytes 294920 | tf_op jit(solution)/shard_map/ppermute | solution.py:298
  15.3 5.3 %collective-permute-start.5 = (bf16[16,1664]{1,0:T(8,128)(2,1)S(1)}, bf16[16,1664]{1,0:T(8,128)(2,1)S(1)}, u32[]{:S(2)}, u32[]{:S(2)}) collective-permute-start(bf16[16,1664]{1,0:T(8,128)(2,1)S(1)} %get-tuple-element.22), channel_id=1, source_target_pairs={{0,12},{4,8},{8,4},{12,0},{16,28},{20,24},{24,20},{28,16},{1,21},{... | collective-permute-start | bytes 159752 | tf_op jit(solution)/shard_map/ppermute | solution.py:298
  16.1 4.7 %collective-permute-start.6 = (bf16[16,1664]{1,0:T(8,128)(2,1)S(1)}, bf16[16,1664]{1,0:T(8,128)(2,1)S(1)}, u32[]{:S(2)}, u32[]{:S(2)}) collective-permute-start(bf16[16,1664]{1,0:T(8,128)(2,1)S(1)} %get-tuple-element.23), channel_id=1, source_target_pairs={{0,4},{4,0},{8,12},{12,8},{16,20},{20,16},{24,28},{28,24},{1,5},{5... | collective-permute-start | bytes 159752 | tf_op jit(solution)/shard_map/ppermute | solution.py:298
  17.4 4.1 %collective-permute-start.7 = (bf16[16,1664]{1,0:T(8,128)(2,1)S(1)}, bf16[16,1664]{1,0:T(8,128)(2,1)S(1)}, u32[]{:S(2)}, u32[]{:S(2)}) collective-permute-start(bf16[16,1664]{1,0:T(8,128)(2,1)S(1)} %get-tuple-element.24), channel_id=1, source_target_pairs={{0,8},{4,12},{8,0},{12,4},{16,24},{20,28},{24,16},{28,20},{1,17},{... | collective-permute-start | bytes 159752 | tf_op jit(solution)/shard_map/ppermute | solution.py:298

commit v9 on v8

--- a/solution.py
+++ b/solution.py
@@ -12,9 +12,8 @@
 SCALE_BLOCK = 128
 KERNEL_VMEM = 8 << 20
 BOTH = ("patch", "uly")
-RETURN_ORDER = (3, 1, 2)
 SPLIT_TERMS = 3
-KEY_VALUE_ORDER = (2, 3, 1)
+KEY_VALUE_ORDER = (3, 2, 1)
 KEY, QUERY = 0, 1
 FAR_QUERY_PARITY = 1
 
@@ -179,10 +178,8 @@
 
 def unpack_stats(packed, heads):
     terms = packed.astype(jnp.float32)
-    summed = terms
-    for term in range(1, SPLIT_TERMS):
-        summed = summed + pltpu.roll(terms, HEAD_DIM - term * heads, 1)
-    return summed, pltpu.roll(summed, HEAD_DIM - SPLIT_TERMS * heads, 1)
+    shifted = [terms] + [pltpu.roll(terms, HEAD_DIM - group * heads, 1) for group in range(1, 2 * SPLIT_TERMS)]
+    return sum(shifted[1:SPLIT_TERMS], shifted[0]), sum(shifted[SPLIT_TERMS + 1 :], shifted[SPLIT_TERMS])
 
 
 def attend_kernel(stale_ref, query_parts, key_value_parts, out_refs):
@@ -233,59 +230,55 @@
     return kernel_call(body, [(rows, width + HEAD_DIM)] * 4, operands, [pltpu.VMEM] * len(operands))
 
 
-def merge_kernel(part_refs, mixed_hbm, mixed_ref, sems):
-    rows, packed_width = part_refs[0].shape
-    width = packed_width - HEAD_DIM
+def merge_side(near_ref, far_ref, out_ref):
+    width = near_ref.shape[1] - HEAD_DIM
     heads = width // HEAD_DIM
-    uly = lax.axis_index("uly")
-    stats = [unpack_stats(part_ref[:, width:], heads) for part_ref in part_refs]
-    used = lax.broadcasted_iota(jnp.int32, (1, HEAD_DIM), 1) < heads
-    shares = []
-    for near, far in ((0, 2), (1, 3)):
-        top = jnp.maximum(stats[near][0], stats[far][0])
-        near_total = stats[near][1] * jnp.exp(stats[near][0] - top)
-        far_total = stats[far][1] * jnp.exp(stats[far][0] - top)
-        share = jnp.where(used, near_total / (near_total + far_total), 0.0)
-        high = share.astype(jnp.bfloat16)
-        shares += [high, (share - high.astype(jnp.float32)).astype(jnp.bfloat16)]
-    head_of = lax.broadcasted_iota(jnp.int32, (HEAD_DIM, width), 1) // HEAD_DIM
-    spread = (lax.broadcasted_iota(jnp.int32, (HEAD_DIM, width), 0) == head_of).astype(jnp.float32).astype(jnp.bfloat16)
-    wide = jnp.dot(jnp.concatenate(shares, axis=0), spread, preferred_element_type=jnp.float32)
-    copies = []
-    for side, (near, far) in enumerate(((0, 2), (1, 3))):
-        share = wide[2 * side * rows : (2 * side + 1) * rows] + wide[(2 * side + 1) * rows : (2 * side + 2) * rows]
-        far_rows = part_refs[far][:, :width].astype(jnp.float32)
-        near_rows = part_refs[near][:, :width].astype(jnp.float32)
-        mixed_ref[side] = (far_rows + (near_rows - far_rows) * share).astype(jnp.bfloat16)
-        columns = aligned((uly if side == 0 else 1 - uly) * width, width)
-        copies.append(pltpu.make_async_copy(mixed_ref.at[side], mixed_hbm.at[:, columns], sems.at[side]))
-        copies[side].start()
-    for copy in copies:
-        copy.wait()
+    near_stats, far_stats = (unpack_stats(ref[:, width:], heads) for ref in (near_ref, far_ref))
+    top = jnp.maximum(near_stats[0], far_stats[0])
+    near_total = near_stats[1] * jnp.exp(near_stats[0] - top)
+    far_total = far_stats[1] * jnp.exp(far_stats[0] - top)
+    share = near_total / (near_total + far_total)
+    for head in range(heads):
+        columns = slice(head * HEAD_DIM, (head + 1) * HEAD_DIM)
+        near_rows = near_ref[:, columns].astype(jnp.float32)
+        far_rows = far_ref[:, columns].astype(jnp.float32)
+        out_ref[:, columns] = (far_rows + (near_rows - far_rows) * share[:, head : head + 1]).astype(jnp.bfloat16)
 
 
 def merge(parts):
     rows, packed_width = parts[0].shape
     width = packed_width - HEAD_DIM
-    names = (0, *RETURN_ORDER)
-
-    def body(*refs):
-        named = dict(zip(names, refs))
-        merge_kernel([named[block] for block in range(4)], *refs[4:])
+
+    def beside_body(far_ref, near_ref, out_ref):
+        merge_side(near_ref, far_ref, out_ref)
+
+    (beside,) = kernel_call(beside_body, [(rows, width)], [parts[3], parts[1]], [pltpu.VMEM] * 2)
+
+    def body(beside_ref, near_ref, far_ref, mixed_hbm, own_ref, sems):
+        uly = lax.axis_index("uly")
+        copies = [
+            pltpu.make_async_copy(beside_ref, mixed_hbm.at[:, aligned((1 - uly) * width, width)], sems.at[0]),
+            pltpu.make_async_copy(own_ref, mixed_hbm.at[:, aligned(uly * width, width)], sems.at[1]),
+        ]
+        copies[0].start()
+        merge_side(near_ref, far_ref, own_ref)
+        copies[1].start()
+        for copy in copies:
+            copy.wait()
 
     (mixed,) = kernel_call(
         body,
         [(rows, 2 * width)],
-        [parts[name] for name in names],
-        [pltpu.VMEM] * 4,
-        [pltpu.VMEM((2, rows, width), jnp.bfloat16), pltpu.SemaphoreType.DMA((2,))],
+        [beside, parts[0], parts[2]],
+        [pltpu.VMEM] * 3,
+        [pltpu.VMEM((rows, width), jnp.bfloat16), pltpu.SemaphoreType.DMA((2,))],
         out_space=pltpu.HBM,
     )
     return mixed
 
 
 def steps_of(rep):
-    return (1, 2) if rep % 2 == FAR_QUERY_PARITY else (2, 1)
+    return (1, 2) if rep % 2 == FAR_QUERY_PARITY else (3, 1)
 
 
 def swap(array, role, uly):

time: 22.6 us -> 22.3 us (0.987)
  waiting for transfers between devices: 7.1 us -> 5.8 us
  starting transfers between devices: 12.6 us -> 13.5 us
    ppermute x8, waiting for transfers between devices: 7.1 us -> 5.8 us  [swap(): return lax.ppermute(array, (*BOTH, 'rep'), pairs)]
    ppermute x8, starting transfers between devices: 12.6 us -> 13.5 us  [swap(): return lax.ppermute(array, (*BOTH, 'rep'), pairs)]
    pallas_call x3 -> x4, Pallas kernels: 2.65 us -> 2.71 us  [kernel_call(): pl.pallas_call(body, out_shape=[jax.ShapeDtypeStruct(shape, jnp.bfloat16)...]
  transfers between devices with their start and end apart: 8 -> 8, of which waited for: 4 -> 3; matrix products, arithmetic and copies ran while one was open for 0% -> 0% of each run, Pallas kernels for 5% -> 6%
where the time goes in v9:
time: 22.3 us; the launch traced here: 22.2 us
  starting transfers between devices  13.5 us (61%)
  waiting for transfers between devices  5.8 us (26%)
  Pallas kernels  2.71 us (12%)
    ppermute x8, starting transfers between devices, swap(): return lax.ppermute(array, (*BOTH, 'rep'), pairs)  13.5 us
    ppermute x8, waiting for transfers between devices, swap(): return lax.ppermute(array, (*BOTH, 'rep'), pairs)  5.8 us
    pallas_call x4, Pallas kernels, kernel_call(): pl.pallas_call(body, out_shape=[jax.ShapeDtypeStruct(shape, jnp.bfloat16)...  2.71 us
  transfers between devices with their start and end apart: 8, of which 3 were waited for; matrix products, arithmetic and copies ran while one was open for 0% of the time, Pallas kernels for 6%

profile of v9, /device:TPU:0, one launch (start us, length us, event | category | flops | bytes accessed | tf_op | source)
XLA Modules:
  0.0 22.2 jit_solution(6995234584817353110)
XLA Ops:
  0.0 0.0 copy-start
  0.0 3.0 %collective-permute-start.3 = (bf16[16,3072]{1,0:T(8,128)(2,1)}, bf16[16,3072]{1,0:T(8,128)(2,1)S(1)}, u32[]{:S(2)}, u32[]{:S(2)}) collective-permute-start(bf16[16,3072]{1,0:T(8,128)(2,1)} %queries_hbm.1), channel_id=1, source_target_pairs={{0,8},{4,12},{8,0},{12,4},{16,24},{20,28},{24,16},{28,20},{1,17},{... | collective-permute-start | bytes 294920 | tf_op jit(solution)/shard_map/ppermute | solution.py:291
  3.0 1.2 %shard_map.46 = (bf16[32,1536]{1,0:T(8,128)(2,1)S(1)}, bf16[32,1536]{1,0:T(8,128)(2,1)S(1)}, bf16[16,1536]{1,0:T(8,128)(2,1)S(1)}, bf16[16,1536]{1,0:T(8,128)(2,1)S(1)}) custom-call(bf16[16,3072]{1,0:T(8,128)(2,1)} %queries_hbm.1, s32[16,2,3072]{2,1,0:T(2,128)} %codes_hbm.1, s32[16,2,24]{2,1,0:T(2,128)} %exps_hbm.1), custom_call_target="tpu_custom_call" | custom-call | tf_op jit(solution)/shard_map/pallas_call | solution.py:92
  4.2 1.6 %collective-permute-start.2 = (bf16[32,1536]{1,0:T(8,128)(2,1)S(1)}, bf16[32,1536]{1,0:T(8,128)(2,1)S(1)}, u32[]{:S(2)}, u32[]{:S(2)}) collective-permute-start(bf16[32,1536]{1,0:T(8,128)(2,1)S(1)} %get-tuple-element.18), channel_id=1, source_target_pairs={{0,4},{4,0},{8,12},{12,8},{16,20},{20,16},{24,28},{28,24},{1,5},{5... | collective-permute-start | bytes 294920 | tf_op jit(solution)/shard_map/ppermute | solution.py:291
  5.8 2.4 %collective-permute-start = (bf16[32,1536]{1,0:T(8,128)(2,1)S(1)}, bf16[32,1536]{1,0:T(8,128)(2,1)S(1)}, u32[]{:S(2)}, u32[]{:S(2)}) collective-permute-start(bf16[32,1536]{1,0:T(8,128)(2,1)S(1)} %get-tuple-element.18), channel_id=1, source_target_pairs={{0,28},{4,24},{8,20},{12,16},{16,12},{20,8},{24,4},{28,0},{1,13},{... | collective-permute-start | bytes 294920 | tf_op jit(solution)/shard_map/ppermute | solution.py:291
  8.2 1.3 %collective-permute-start.1 = (bf16[32,1536]{1,0:T(8,128)(2,1)S(1)}, bf16[32,1536]{1,0:T(8,128)(2,1)S(1)}, u32[]{:S(2)}, u32[]{:S(2)}) collective-permute-start(bf16[32,1536]{1,0:T(8,128)(2,1)S(1)} %get-tuple-element.16.home_ref), channel_id=1, source_target_pairs={{0,24},{4,28},{8,16},{12,20},{16,8},{20,12},{24,0},{28,4},{1,9},{5... | collective-permute-start | bytes 294920 | tf_op jit(solution)/shard_map/ppermute | solution.py:291
  9.6 0.0 collective-permute-done.3.refs_3_
  9.6 1.6 %collective-permute-start.4 = (bf16[2,16,1536]{2,1,0:T(8,128)(2,1)S(1)}, bf16[2,16,1536]{2,1,0:T(8,128)(2,1)S(1)}, u32[]{:S(2)}, u32[]{:S(2)}) collective-permute-start(bf16[2,16,1536]{2,1,0:T(8,128)(2,1)S(1)} %pad_maximum_fusion), channel_id=1, source_target_pairs={{0,4},{4,0},{8,12},{12,8},{16,20},{20,16},{24,28},{28,24},{1,5},{5... | collective-permute-start | bytes 294920 | tf_op jit(solution)/shard_map/ppermute | solution.py:291
  11.2 0.0 copy-done
  11.2 0.1 copy.7
  11.3 3.4 %collective-permute-done.1.refs_1_ = bf16[32,1536]{1,0:T(8,128)(2,1)S(1)} collective-permute-done((bf16[32,1536]{1,0:T(8,128)(2,1)S(1)}, bf16[32,1536]{1,0:T(8,128)(2,1)S(1)}, u32[]{:S(2)}, u32[]{:S(2)}) %collective-permute-start.1) | collective-permute-done | bytes 98336 | tf_op jit(solution)/shard_map/ppermute | solution.py:291
  14.6 0.0 collective-permute-done.2.refs_2_
  14.6 0.0 collective-permute-done.refs_0_
  14.7 0.0 collective-permute-done.4.refs_4_
  14.7 0.5 %shard_map.47 = (bf16[16,1664]{1,0:T(8,128)(2,1)S(1)}, bf16[16,1664]{1,0:T(8,128)(2,1)S(1)}, bf16[16,1664]{1,0:T(8,128)(2,1)S(1)}, bf16[16,1664]{1,0:T(8,128)(2,1)S(1)}) custom-call(bf16[32,1536]{1,0:T(8,128)(2,1)S(1)} %get-tuple-element.16.home_ref, bf16[16,1536]{1,0:T(8,128)(2,1)S(1)} %get-tuple-element.17.home_queries_ref, ...), custom_call_target="tpu_custom_call" | custom-call | tf_op jit(solution)/shard_map/pallas_call | solution.py:92
  15.1 1.0 %collective-permute-start.5 = (bf16[16,1664]{1,0:T(8,128)(2,1)S(1)}, bf16[16,1664]{1,0:T(8,128)(2,1)S(1)}, u32[]{:S(2)}, u32[]{:S(2)}) collective-permute-start(bf16[16,1664]{1,0:T(8,128)(2,1)S(1)} %get-tuple-element.21), channel_id=1, source_target_pairs={{0,12},{4,8},{8,4},{12,0},{16,28},{20,24},{24,20},{28,16},{1,21},{... | collective-permute-start | bytes 159752 | tf_op jit(solution)/shard_map/ppermute | solution.py:291
  16.1 0.8 %collective-permute-start.6 = (bf16[16,1664]{1,0:T(8,128)(2,1)S(1)}, bf16[16,1664]{1,0:T(8,128)(2,1)S(1)}, u32[]{:S(2)}, u32[]{:S(2)}) collective-permute-start(bf16[16,1664]{1,0:T(8,128)(2,1)S(1)} %get-tuple-element.22), channel_id=1, source_target_pairs={{0,4},{4,0},{8,12},{12,8},{16,20},{20,16},{24,28},{28,24},{1,5},{5... | collective-permute-start | bytes 159752 | tf_op jit(solution)/shard_map/ppermute | solution.py:291
  16.9 1.8 %collective-permute-start.7 = (bf16[16,1664]{1,0:T(8,128)(2,1)S(1)}, bf16[16,1664]{1,0:T(8,128)(2,1)S(1)}, u32[]{:S(2)}, u32[]{:S(2)}) collective-permute-start(bf16[16,1664]{1,0:T(8,128)(2,1)S(1)} %get-tuple-element.24), channel_id=1, source_target_pairs={{0,8},{4,12},{8,0},{12,4},{16,24},{20,28},{24,16},{28,20},{1,17},{... | collective-permute-start | bytes 159752 | tf_op jit(solution)/shard_map/ppermute | solution.py:291
  18.7 2.1 %collective-permute-done.5.far_ref = bf16[16,1664]{1,0:T(8,128)(2,1)S(1)} collective-permute-done((bf16[16,1664]{1,0:T(8,128)(2,1)S(1)}, bf16[16,1664]{1,0:T(8,128)(2,1)S(1)}, u32[]{:S(2)}, u32[]{:S(2)}) %collective-permute-start.5) | collective-permute-done | bytes 53280 | tf_op jit(solution)/shard_map/ppermute | solution.py:291
  20.8 0.0 collective-permute-done.6.near_ref
  20.8 0.2 shard_map.48.beside_ref
  21.0 0.3 %collective-permute-done.7.far_ref = bf16[16,1664]{1,0:T(8,128)(2,1)S(1)} collective-permute-done((bf16[16,1664]{1,0:T(8,128)(2,1)S(1)}, bf16[16,1664]{1,0:T(8,128)(2,1)S(1)}, u32[]{:S(2)}, u32[]{:S(2)}) %collective-permute-start.7) | collective-permute-done | bytes 53280 | tf_op jit(solution)/shard_map/ppermute | solution.py:291
  21.3 0.8 %shard_map.49 = bf16[16,3072]{1,0:T(8,128)(2,1)} custom-call(bf16[16,1536]{1,0:T(8,128)(2,1)S(1)} %shard_map.48.beside_ref, bf16[16,1664]{1,0:T(8,128)(2,1)S(1)} %get-tuple-element.23.near_ref, bf16[16,1664]{1,0:T(8,128)(2,1)S(1)} %collective-permute-done.7.far_ref), custom_call_target="tpu_custom_call" | custom-call | tf_op jit(solution)/shard_map/pallas_call | solution.py:92
  (2 shorter events, 0.0 us)
Async XLA Ops:
  0.0 11.2 %copy-start = (bf16[128,2,1536]{2,1,0:T(2,128)(2,1)S(1)}, bf16[128,2,1536]{2,1,0:T(2,128)(2,1)}, u32[]{:S(2)}) copy-start(bf16[128,2,1536]{2,1,0:T(2,128)(2,1)} %param.5) | copy-start | bytes 2359300
  0.0 9.6 %collective-permute-start.3 = (bf16[16,3072]{1,0:T(8,128)(2,1)}, bf16[16,3072]{1,0:T(8,128)(2,1)S(1)}, u32[]{:S(2)}, u32[]{:S(2)}) collective-permute-start(bf16[16,3072]{1,0:T(8,128)(2,1)} %queries_hbm.1), channel_id=1, source_target_pairs={{0,8},{4,12},{8,0},{12,4},{16,24},{20,28},{24,16},{28,20},{1,17},{... | collective-permute-start | bytes 294920 | tf_op jit(solution)/shard_map/ppermute | solution.py:291
  4.2 10.4 %collective-permute-start.2 = (bf16[32,1536]{1,0:T(8,128)(2,1)S(1)}, bf16[32,1536]{1,0:T(8,128)(2,1)S(1)}, u32[]{:S(2)}, u32[]{:S(2)}) collective-permute-start(bf16[32,1536]{1,0:T(8,128)(2,1)S(1)} %get-tuple-element.18), channel_id=1, source_target_pairs={{0,4},{4,0},{8,12},{12,8},{16,20},{20,16},{24,28},{28,24},{1,5},{5... | collective-permute-start | bytes 294920 | tf_op jit(solution)/shard_map/ppermute | solution.py:291
  5.8 8.8 %collective-permute-start = (bf16[32,1536]{1,0:T(8,128)(2,1)S(1)}, bf16[32,1536]{1,0:T(8,128)(2,1)S(1)}, u32[]{:S(2)}, u32[]{:S(2)}) collective-permute-start(bf16[32,1536]{1,0:T(8,128)(2,1)S(1)} %get-tuple-element.18), channel_id=1, source_target_pairs={{0,28},{4,24},{8,20},{12,16},{16,12},{20,8},{24,4},{28,0},{1,13},{... | collective-permute-start | bytes 294920 | tf_op jit(solution)/shard_map/ppermute | solution.py:291
  8.2 6.4 %collective-permute-start.1 = (bf16[32,1536]{1,0:T(8,128)(2,1)S(1)}, bf16[32,1536]{1,0:T(8,128)(2,1)S(1)}, u32[]{:S(2)}, u32[]{:S(2)}) collective-permute-start(bf16[32,1536]{1,0:T(8,128)(2,1)S(1)} %get-tuple-element.16.home_ref), channel_id=1, source_target_pairs={{0,24},{4,28},{8,16},{12,20},{16,8},{20,12},{24,0},{28,4},{1,9},{5... | collective-permute-start | bytes 294920 | tf_op jit(solution)/shard_map/ppermute | solution.py:291
  9.6 5.1 %collective-permute-start.4 = (bf16[2,16,1536]{2,1,0:T(8,128)(2,1)S(1)}, bf16[2,16,1536]{2,1,0:T(8,128)(2,1)S(1)}, u32[]{:S(2)}, u32[]{:S(2)}) collective-permute-start(bf16[2,16,1536]{2,1,0:T(8,128)(2,1)S(1)} %pad_maximum_fusion), channel_id=1, source_target_pairs={{0,4},{4,0},{8,12},{12,8},{16,20},{20,16},{24,28},{28,24},{1,5},{5... | collective-permute-start | bytes 294920 | tf_op jit(solution)/shard_map/ppermute | solution.py:291
  15.1 5.7 %collective-permute-start.5 = (bf16[16,1664]{1,0:T(8,128)(2,1)S(1)}, bf16[16,1664]{1,0:T(8,128)(2,1)S(1)}, u32[]{:S(2)}, u32[]{:S(2)}) collective-permute-start(bf16[16,1664]{1,0:T(8,128)(2,1)S(1)} %get-tuple-element.21), channel_id=1, source_target_pairs={{0,12},{4,8},{8,4},{12,0},{16,28},{20,24},{24,20},{28,16},{1,21},{... | collective-permute-start | bytes 159752 | tf_op jit(solution)/shard_map/ppermute | solution.py:291
  16.1 4.7 %collective-permute-start.6 = (bf16[16,1664]{1,0:T(8,128)(2,1)S(1)}, bf16[16,1664]{1,0:T(8,128)(2,1)S(1)}, u32[]{:S(2)}, u32[]{:S(2)}) collective-permute-start(bf16[16,1664]{1,0:T(8,128)(2,1)S(1)} %get-tuple-element.22), channel_id=1, source_target_pairs={{0,4},{4,0},{8,12},{12,8},{16,20},{20,16},{24,28},{28,24},{1,5},{5... | collective-permute-start | bytes 159752 | tf_op jit(solution)/shard_map/ppermute | solution.py:291
  16.9 4.4 %collective-permute-start.7 = (bf16[16,1664]{1,0:T(8,128)(2,1)S(1)}, bf16[16,1664]{1,0:T(8,128)(2,1)S(1)}, u32[]{:S(2)}, u32[]{:S(2)}) collective-permute-start(bf16[16,1664]{1,0:T(8,128)(2,1)S(1)} %get-tuple-element.24), channel_id=1, source_target_pairs={{0,8},{4,12},{8,0},{12,4},{16,24},{20,28},{24,16},{28,20},{1,17},{... | collective-permute-start | bytes 159752 | tf_op jit(solution)/shard_map/ppermute | solution.py:291

commit v10 on v9

--- a/solution.py
+++ b/solution.py
@@ -205,10 +205,14 @@
     value_rows = refreshed(1)
     maxima = [jnp.max(each, axis=1, keepdims=True) for each in scores]
     weights = [jnp.exp(each - maximum) for each, maximum in zip(scores, maxima)]
-    sums = [weigh_values(weights[head], value_rows, head) for head in heads]
-    totals = [jnp.sum(each, axis=1, keepdims=True) for each in weights]
+    ones = jnp.ones((value_rows.shape[0], HEAD_DIM), jnp.bfloat16)
+    products = []
     for head in heads:
-        result = (sums[head] / totals[head]).astype(jnp.bfloat16)
+        with_ones = jnp.concatenate([column_block(value_rows, head), ones], axis=1)
+        products.append(jnp.dot(weights[head].astype(jnp.bfloat16), with_ones, preferred_element_type=jnp.float32))
+    totals = [column_block(each, 1) for each in products]
+    for head in heads:
+        result = (column_block(products[head], 0) / totals[head]).astype(jnp.bfloat16)
         for block, out_ref in enumerate(out_refs):
             out_ref[:, head * HEAD_DIM : (head + 1) * HEAD_DIM] = result[block * rows : (block + 1) * rows]
     stats = pack_stats(maxima, totals)

time: 22.3 us -> 22.3 us (level)
  no operation moved by 1% of the time
where the time goes in v10:
time: 22.3 us; the launch traced here: 22.2 us
  starting transfers between devices  13.5 us (61%)
  waiting for transfers between devices  5.8 us (26%)
  Pallas kernels  2.73 us (12%)
    ppermute x8, starting transfers between devices, swap(): return lax.ppermute(array, (*BOTH, 'rep'), pairs)  13.5 us
    ppermute x8, waiting for transfers between devices, swap(): return lax.ppermute(array, (*BOTH, 'rep'), pairs)  5.8 us
    pallas_call x4, Pallas kernels, kernel_call(): pl.pallas_call(body, out_shape=[jax.ShapeDtypeStruct(shape, jnp.bfloat16)...  2.73 us
  transfers between devices with their start and end apart: 8, of which 3 were waited for; matrix products, arithmetic and copies ran while one was open for 0% of the time, Pallas kernels for 6%

profile of v10, /device:TPU:0, one launch (start us, length us, event | category | flops | bytes accessed | tf_op | source)
XLA Modules:
  0.0 22.2 jit_solution(9338748584463297948)
XLA Ops:
  0.0 0.0 copy-start
  0.0 3.0 %collective-permute-start.3 = (bf16[16,3072]{1,0:T(8,128)(2,1)}, bf16[16,3072]{1,0:T(8,128)(2,1)S(1)}, u32[]{:S(2)}, u32[]{:S(2)}) collective-permute-start(bf16[16,3072]{1,0:T(8,128)(2,1)} %queries_hbm.1), channel_id=1, source_target_pairs={{0,8},{4,12},{8,0},{12,4},{16,24},{20,28},{24,16},{28,20},{1,17},{... | collective-permute-start | bytes 294920 | tf_op jit(solution)/shard_map/ppermute | solution.py:295
  3.0 1.2 %shard_map.46 = (bf16[32,1536]{1,0:T(8,128)(2,1)S(1)}, bf16[32,1536]{1,0:T(8,128)(2,1)S(1)}, bf16[16,1536]{1,0:T(8,128)(2,1)S(1)}, bf16[16,1536]{1,0:T(8,128)(2,1)S(1)}) custom-call(bf16[16,3072]{1,0:T(8,128)(2,1)} %queries_hbm.1, s32[16,2,3072]{2,1,0:T(2,128)} %codes_hbm.1, s32[16,2,24]{2,1,0:T(2,128)} %exps_hbm.1), custom_call_target="tpu_custom_call" | custom-call | tf_op jit(solution)/shard_map/pallas_call | solution.py:92
  4.2 1.6 %collective-permute-start.2 = (bf16[32,1536]{1,0:T(8,128)(2,1)S(1)}, bf16[32,1536]{1,0:T(8,128)(2,1)S(1)}, u32[]{:S(2)}, u32[]{:S(2)}) collective-permute-start(bf16[32,1536]{1,0:T(8,128)(2,1)S(1)} %get-tuple-element.18), channel_id=1, source_target_pairs={{0,4},{4,0},{8,12},{12,8},{16,20},{20,16},{24,28},{28,24},{1,5},{5... | collective-permute-start | bytes 294920 | tf_op jit(solution)/shard_map/ppermute | solution.py:295
  5.8 2.4 %collective-permute-start = (bf16[32,1536]{1,0:T(8,128)(2,1)S(1)}, bf16[32,1536]{1,0:T(8,128)(2,1)S(1)}, u32[]{:S(2)}, u32[]{:S(2)}) collective-permute-start(bf16[32,1536]{1,0:T(8,128)(2,1)S(1)} %get-tuple-element.18), channel_id=1, source_target_pairs={{0,28},{4,24},{8,20},{12,16},{16,12},{20,8},{24,4},{28,0},{1,13},{... | collective-permute-start | bytes 294920 | tf_op jit(solution)/shard_map/ppermute | solution.py:295
  8.2 1.3 %collective-permute-start.1 = (bf16[32,1536]{1,0:T(8,128)(2,1)S(1)}, bf16[32,1536]{1,0:T(8,128)(2,1)S(1)}, u32[]{:S(2)}, u32[]{:S(2)}) collective-permute-start(bf16[32,1536]{1,0:T(8,128)(2,1)S(1)} %get-tuple-element.16.home_ref), channel_id=1, source_target_pairs={{0,24},{4,28},{8,16},{12,20},{16,8},{20,12},{24,0},{28,4},{1,9},{5... | collective-permute-start | bytes 294920 | tf_op jit(solution)/shard_map/ppermute | solution.py:295
  9.6 0.0 collective-permute-done.3.refs_3_
  9.6 1.6 %collective-permute-start.4 = (bf16[2,16,1536]{2,1,0:T(8,128)(2,1)S(1)}, bf16[2,16,1536]{2,1,0:T(8,128)(2,1)S(1)}, u32[]{:S(2)}, u32[]{:S(2)}) collective-permute-start(bf16[2,16,1536]{2,1,0:T(8,128)(2,1)S(1)} %pad_maximum_fusion), channel_id=1, source_target_pairs={{0,4},{4,0},{8,12},{12,8},{16,20},{20,16},{24,28},{28,24},{1,5},{5... | collective-permute-start | bytes 294920 | tf_op jit(solution)/shard_map/ppermute | solution.py:295
  11.2 0.0 copy-done
  11.2 0.1 copy.7
  11.3 3.4 %collective-permute-done.1.refs_1_ = bf16[32,1536]{1,0:T(8,128)(2,1)S(1)} collective-permute-done((bf16[32,1536]{1,0:T(8,128)(2,1)S(1)}, bf16[32,1536]{1,0:T(8,128)(2,1)S(1)}, u32[]{:S(2)}, u32[]{:S(2)}) %collective-permute-start.1) | collective-permute-done | bytes 98336 | tf_op jit(solution)/shard_map/ppermute | solution.py:295
  14.6 0.0 collective-permute-done.2.refs_2_
  14.6 0.0 collective-permute-done.refs_0_
  14.7 0.0 collective-permute-done.4.refs_4_
  14.7 0.5 %shard_map.47 = (bf16[16,1664]{1,0:T(8,128)(2,1)S(1)}, bf16[16,1664]{1,0:T(8,128)(2,1)S(1)}, bf16[16,1664]{1,0:T(8,128)(2,1)S(1)}, bf16[16,1664]{1,0:T(8,128)(2,1)S(1)}) custom-call(bf16[32,1536]{1,0:T(8,128)(2,1)S(1)} %get-tuple-element.16.home_ref, bf16[16,1536]{1,0:T(8,128)(2,1)S(1)} %get-tuple-element.17.home_queries_ref, ...), custom_call_target="tpu_custom_call" | custom-call | tf_op jit(solution)/shard_map/pallas_call | solution.py:92
  15.2 1.0 %collective-permute-start.5 = (bf16[16,1664]{1,0:T(8,128)(2,1)S(1)}, bf16[16,1664]{1,0:T(8,128)(2,1)S(1)}, u32[]{:S(2)}, u32[]{:S(2)}) collective-permute-start(bf16[16,1664]{1,0:T(8,128)(2,1)S(1)} %get-tuple-element.21), channel_id=1, source_target_pairs={{0,12},{4,8},{8,4},{12,0},{16,28},{20,24},{24,20},{28,16},{1,21},{... | collective-permute-start | bytes 159752 | tf_op jit(solution)/shard_map/ppermute | solution.py:295
  16.1 0.8 %collective-permute-start.6 = (bf16[16,1664]{1,0:T(8,128)(2,1)S(1)}, bf16[16,1664]{1,0:T(8,128)(2,1)S(1)}, u32[]{:S(2)}, u32[]{:S(2)}) collective-permute-start(bf16[16,1664]{1,0:T(8,128)(2,1)S(1)} %get-tuple-element.22), channel_id=1, source_target_pairs={{0,4},{4,0},{8,12},{12,8},{16,20},{20,16},{24,28},{28,24},{1,5},{5... | collective-permute-start | bytes 159752 | tf_op jit(solution)/shard_map/ppermute | solution.py:295
  17.0 1.8 %collective-permute-start.7 = (bf16[16,1664]{1,0:T(8,128)(2,1)S(1)}, bf16[16,1664]{1,0:T(8,128)(2,1)S(1)}, u32[]{:S(2)}, u32[]{:S(2)}) collective-permute-start(bf16[16,1664]{1,0:T(8,128)(2,1)S(1)} %get-tuple-element.24), channel_id=1, source_target_pairs={{0,8},{4,12},{8,0},{12,4},{16,24},{20,28},{24,16},{28,20},{1,17},{... | collective-permute-start | bytes 159752 | tf_op jit(solution)/shard_map/ppermute | solution.py:295
  18.7 2.1 %collective-permute-done.5.far_ref = bf16[16,1664]{1,0:T(8,128)(2,1)S(1)} collective-permute-done((bf16[16,1664]{1,0:T(8,128)(2,1)S(1)}, bf16[16,1664]{1,0:T(8,128)(2,1)S(1)}, u32[]{:S(2)}, u32[]{:S(2)}) %collective-permute-start.5) | collective-permute-done | bytes 53280 | tf_op jit(solution)/shard_map/ppermute | solution.py:295
  20.8 0.0 collective-permute-done.6.near_ref
  20.8 0.2 shard_map.48.beside_ref
  21.0 0.3 %collective-permute-done.7.far_ref = bf16[16,1664]{1,0:T(8,128)(2,1)S(1)} collective-permute-done((bf16[16,1664]{1,0:T(8,128)(2,1)S(1)}, bf16[16,1664]{1,0:T(8,128)(2,1)S(1)}, u32[]{:S(2)}, u32[]{:S(2)}) %collective-permute-start.7) | collective-permute-done | bytes 53280 | tf_op jit(solution)/shard_map/ppermute | solution.py:295
  21.3 0.8 %shard_map.49 = bf16[16,3072]{1,0:T(8,128)(2,1)} custom-call(bf16[16,1536]{1,0:T(8,128)(2,1)S(1)} %shard_map.48.beside_ref, bf16[16,1664]{1,0:T(8,128)(2,1)S(1)} %get-tuple-element.23.near_ref, bf16[16,1664]{1,0:T(8,128)(2,1)S(1)} %collective-permute-done.7.far_ref), custom_call_target="tpu_custom_call" | custom-call | tf_op jit(solution)/shard_map/pallas_call | solution.py:92
  (2 shorter events, 0.0 us)
Async XLA Ops:
  0.0 11.2 %copy-start = (bf16[128,2,1536]{2,1,0:T(2,128)(2,1)S(1)}, bf16[128,2,1536]{2,1,0:T(2,128)(2,1)}, u32[]{:S(2)}) copy-start(bf16[128,2,1536]{2,1,0:T(2,128)(2,1)} %param.5) | copy-start | bytes 2359300
  0.0 9.6 %collective-permute-start.3 = (bf16[16,3072]{1,0:T(8,128)(2,1)}, bf16[16,3072]{1,0:T(8,128)(2,1)S(1)}, u32[]{:S(2)}, u32[]{:S(2)}) collective-permute-start(bf16[16,3072]{1,0:T(8,128)(2,1)} %queries_hbm.1), channel_id=1, source_target_pairs={{0,8},{4,12},{8,0},{12,4},{16,24},{20,28},{24,16},{28,20},{1,17},{... | collective-permute-start | bytes 294920 | tf_op jit(solution)/shard_map/ppermute | solution.py:295
  4.2 10.4 %collective-permute-start.2 = (bf16[32,1536]{1,0:T(8,128)(2,1)S(1)}, bf16[32,1536]{1,0:T(8,128)(2,1)S(1)}, u32[]{:S(2)}, u32[]{:S(2)}) collective-permute-start(bf16[32,1536]{1,0:T(8,128)(2,1)S(1)} %get-tuple-element.18), channel_id=1, source_target_pairs={{0,4},{4,0},{8,12},{12,8},{16,20},{20,16},{24,28},{28,24},{1,5},{5... | collective-permute-start | bytes 294920 | tf_op jit(solution)/shard_map/ppermute | solution.py:295
  5.8 8.8 %collective-permute-start = (bf16[32,1536]{1,0:T(8,128)(2,1)S(1)}, bf16[32,1536]{1,0:T(8,128)(2,1)S(1)}, u32[]{:S(2)}, u32[]{:S(2)}) collective-permute-start(bf16[32,1536]{1,0:T(8,128)(2,1)S(1)} %get-tuple-element.18), channel_id=1, source_target_pairs={{0,28},{4,24},{8,20},{12,16},{16,12},{20,8},{24,4},{28,0},{1,13},{... | collective-permute-start | bytes 294920 | tf_op jit(solution)/shard_map/ppermute | solution.py:295
  8.2 6.4 %collective-permute-start.1 = (bf16[32,1536]{1,0:T(8,128)(2,1)S(1)}, bf16[32,1536]{1,0:T(8,128)(2,1)S(1)}, u32[]{:S(2)}, u32[]{:S(2)}) collective-permute-start(bf16[32,1536]{1,0:T(8,128)(2,1)S(1)} %get-tuple-element.16.home_ref), channel_id=1, source_target_pairs={{0,24},{4,28},{8,16},{12,20},{16,8},{20,12},{24,0},{28,4},{1,9},{5... | collective-permute-start | bytes 294920 | tf_op jit(solution)/shard_map/ppermute | solution.py:295
  9.6 5.1 %collective-permute-start.4 = (bf16[2,16,1536]{2,1,0:T(8,128)(2,1)S(1)}, bf16[2,16,1536]{2,1,0:T(8,128)(2,1)S(1)}, u32[]{:S(2)}, u32[]{:S(2)}) collective-permute-start(bf16[2,16,1536]{2,1,0:T(8,128)(2,1)S(1)} %pad_maximum_fusion), channel_id=1, source_target_pairs={{0,4},{4,0},{8,12},{12,8},{16,20},{20,16},{24,28},{28,24},{1,5},{5... | collective-permute-start | bytes 294920 | tf_op jit(solution)/shard_map/ppermute | solution.py:295
  15.2 5.7 %collective-permute-start.5 = (bf16[16,1664]{1,0:T(8,128)(2,1)S(1)}, bf16[16,1664]{1,0:T(8,128)(2,1)S(1)}, u32[]{:S(2)}, u32[]{:S(2)}) collective-permute-start(bf16[16,1664]{1,0:T(8,128)(2,1)S(1)} %get-tuple-element.21), channel_id=1, source_target_pairs={{0,12},{4,8},{8,4},{12,0},{16,28},{20,24},{24,20},{28,16},{1,21},{... | collective-permute-start | bytes 159752 | tf_op jit(solution)/shard_map/ppermute | solution.py:295
  16.1 4.7 %collective-permute-start.6 = (bf16[16,1664]{1,0:T(8,128)(2,1)S(1)}, bf16[16,1664]{1,0:T(8,128)(2,1)S(1)}, u32[]{:S(2)}, u32[]{:S(2)}) collective-permute-start(bf16[16,1664]{1,0:T(8,128)(2,1)S(1)} %get-tuple-element.22), channel_id=1, source_target_pairs={{0,4},{4,0},{8,12},{12,8},{16,20},{20,16},{24,28},{28,24},{1,5},{5... | collective-permute-start | bytes 159752 | tf_op jit(solution)/shard_map/ppermute | solution.py:295
  17.0 4.4 %collective-permute-start.7 = (bf16[16,1664]{1,0:T(8,128)(2,1)S(1)}, bf16[16,1664]{1,0:T(8,128)(2,1)S(1)}, u32[]{:S(2)}, u32[]{:S(2)}) collective-permute-start(bf16[16,1664]{1,0:T(8,128)(2,1)S(1)} %get-tuple-element.24), channel_id=1, source_target_pairs={{0,8},{4,12},{8,0},{12,4},{16,24},{20,28},{24,16},{28,20},{1,17},{... | collective-permute-start | bytes 159752 | tf_op jit(solution)/shard_map/ppermute | solution.py:295

commit v11 on v10

--- a/solution.py
+++ b/solution.py
@@ -108,13 +108,9 @@
     fetch_exps = pltpu.make_async_copy(exps_hbm, exps_ref, sems.at[0])
     fetch_exps.start()
     fetch_codes = []
-    for start in starts:
-        for kind in range(2):
-            slot = len(fetch_codes)
-            fetch_codes.append(
-                pltpu.make_async_copy(codes_hbm.at[:, kind, aligned(start, half)], codes_ref.at[slot], sems.at[1 + slot])
-            )
-            fetch_codes[slot].start()
+    for kind in range(2):
+        fetch_codes.append(pltpu.make_async_copy(codes_hbm.at[:, kind, :], codes_ref.at[kind], sems.at[1 + kind]))
+        fetch_codes[kind].start()
     fetch_queries = []
     for side, target in enumerate((away_queries_ref, home_queries_ref)):
         fetch_queries.append(pltpu.make_async_copy(queries_hbm.at[:, aligned(starts[side], half)], target, sems.at[5 + side]))
@@ -127,11 +123,11 @@
     scales = scales.astype(jnp.bfloat16)
     spreads = [(row_of == block_of + start // SCALE_BLOCK).astype(jnp.float32).astype(jnp.bfloat16) for start in starts]
     wide_scales = [jnp.dot(scales, spread, preferred_element_type=jnp.float32) for spread in spreads]
-    for side, out_ref in enumerate((away_ref, home_ref)):
-        for kind in range(2):
-            fetch_codes[2 * side + kind].wait()
-            own_rows = slice(kind * rows, (kind + 1) * rows)
-            decoded = codes_ref[2 * side + kind].astype(jnp.float32) * wide_scales[side][own_rows]
+    for kind in range(2):
+        fetch_codes[kind].wait()
+        own_rows = slice(kind * rows, (kind + 1) * rows)
+        for start, wide_scale, out_ref in zip(starts, wide_scales, (away_ref, home_ref)):
+            decoded = codes_ref[kind, :, aligned(start, half)].astype(jnp.float32) * wide_scale[own_rows]
             out_ref[own_rows, :] = decoded.astype(jnp.bfloat16)
     for fetch in fetch_queries:
         fetch.wait()
@@ -146,7 +142,7 @@
         [queries, codes, exps],
         [pltpu.HBM] * 3,
         [
-            pltpu.VMEM((4, rows, half), codes.dtype),
+            pltpu.VMEM((2, rows, model_width), codes.dtype),
             pltpu.VMEM(exps.shape, exps.dtype),
             pltpu.SemaphoreType.DMA((7,)),
         ],

time: 22.3 us -> 22.3 us (level)
  no operation moved by 1% of the time
where the time goes in v11:
time: 22.3 us; the launch traced here: 22.2 us
  starting transfers between devices  13.5 us (61%)
  waiting for transfers between devices  5.8 us (26%)
  Pallas kernels  2.72 us (12%)
    ppermute x8, starting transfers between devices, swap(): return lax.ppermute(array, (*BOTH, 'rep'), pairs)  13.5 us
    ppermute x8, waiting for transfers between devices, swap(): return lax.ppermute(array, (*BOTH, 'rep'), pairs)  5.8 us
    pallas_call x4, Pallas kernels, kernel_call(): pl.pallas_call(body, out_shape=[jax.ShapeDtypeStruct(shape, jnp.bfloat16)...  2.72 us
  transfers between devices with their start and end apart: 8, of which 3 were waited for; matrix products, arithmetic and copies ran while one was open for 0% of the time, Pallas kernels for 6%

profile of v11, /device:TPU:0, one launch (start us, length us, event | category | flops | bytes accessed | tf_op | source)
XLA Modules:
  0.0 22.2 jit_solution(6389011210285060299)
XLA Ops:
  0.0 0.0 copy-start
  0.0 3.0 %collective-permute-start.3 = (bf16[16,3072]{1,0:T(8,128)(2,1)}, bf16[16,3072]{1,0:T(8,128)(2,1)S(1)}, u32[]{:S(2)}, u32[]{:S(2)}) collective-permute-start(bf16[16,3072]{1,0:T(8,128)(2,1)} %queries_hbm.1), channel_id=1, source_target_pairs={{0,8},{4,12},{8,0},{12,4},{16,24},{20,28},{24,16},{28,20},{1,17},{... | collective-permute-start | bytes 294920 | tf_op jit(solution)/shard_map/ppermute | solution.py:291
  3.0 1.2 %shard_map.46 = (bf16[32,1536]{1,0:T(8,128)(2,1)S(1)}, bf16[32,1536]{1,0:T(8,128)(2,1)S(1)}, bf16[16,1536]{1,0:T(8,128)(2,1)S(1)}, bf16[16,1536]{1,0:T(8,128)(2,1)S(1)}) custom-call(bf16[16,3072]{1,0:T(8,128)(2,1)} %queries_hbm.1, s32[16,2,3072]{2,1,0:T(2,128)} %codes_hbm.1, s32[16,2,24]{2,1,0:T(2,128)} %exps_hbm.1), custom_call_target="tpu_custom_call" | custom-call | tf_op jit(solution)/shard_map/pallas_call | solution.py:92
  4.2 1.6 %collective-permute-start.2 = (bf16[32,1536]{1,0:T(8,128)(2,1)S(1)}, bf16[32,1536]{1,0:T(8,128)(2,1)S(1)}, u32[]{:S(2)}, u32[]{:S(2)}) collective-permute-start(bf16[32,1536]{1,0:T(8,128)(2,1)S(1)} %get-tuple-element.18), channel_id=1, source_target_pairs={{0,4},{4,0},{8,12},{12,8},{16,20},{20,16},{24,28},{28,24},{1,5},{5... | collective-permute-start | bytes 294920 | tf_op jit(solution)/shard_map/ppermute | solution.py:291
  5.8 2.4 %collective-permute-start = (bf16[32,1536]{1,0:T(8,128)(2,1)S(1)}, bf16[32,1536]{1,0:T(8,128)(2,1)S(1)}, u32[]{:S(2)}, u32[]{:S(2)}) collective-permute-start(bf16[32,1536]{1,0:T(8,128)(2,1)S(1)} %get-tuple-element.18), channel_id=1, source_target_pairs={{0,28},{4,24},{8,20},{12,16},{16,12},{20,8},{24,4},{28,0},{1,13},{... | collective-permute-start | bytes 294920 | tf_op jit(solution)/shard_map/ppermute | solution.py:291
  8.2 1.3 %collective-permute-start.1 = (bf16[32,1536]{1,0:T(8,128)(2,1)S(1)}, bf16[32,1536]{1,0:T(8,128)(2,1)S(1)}, u32[]{:S(2)}, u32[]{:S(2)}) collective-permute-start(bf16[32,1536]{1,0:T(8,128)(2,1)S(1)} %get-tuple-element.16.home_ref), channel_id=1, source_target_pairs={{0,24},{4,28},{8,16},{12,20},{16,8},{20,12},{24,0},{28,4},{1,9},{5... | collective-permute-start | bytes 294920 | tf_op jit(solution)/shard_map/ppermute | solution.py:291
  9.6 0.0 collective-permute-done.3.refs_3_
  9.6 1.6 %collective-permute-start.4 = (bf16[2,16,1536]{2,1,0:T(8,128)(2,1)S(1)}, bf16[2,16,1536]{2,1,0:T(8,128)(2,1)S(1)}, u32[]{:S(2)}, u32[]{:S(2)}) collective-permute-start(bf16[2,16,1536]{2,1,0:T(8,128)(2,1)S(1)} %pad_maximum_fusion), channel_id=1, source_target_pairs={{0,4},{4,0},{8,12},{12,8},{16,20},{20,16},{24,28},{28,24},{1,5},{5... | collective-permute-start | bytes 294920 | tf_op jit(solution)/shard_map/ppermute | solution.py:291
  11.2 0.0 copy-done
  11.2 0.1 copy.7
  11.3 3.4 %collective-permute-done.1.refs_1_ = bf16[32,1536]{1,0:T(8,128)(2,1)S(1)} collective-permute-done((bf16[32,1536]{1,0:T(8,128)(2,1)S(1)}, bf16[32,1536]{1,0:T(8,128)(2,1)S(1)}, u32[]{:S(2)}, u32[]{:S(2)}) %collective-permute-start.1) | collective-permute-done | bytes 98336 | tf_op jit(solution)/shard_map/ppermute | solution.py:291
  14.6 0.0 collective-permute-done.2.refs_2_
  14.6 0.0 collective-permute-done.refs_0_
  14.6 0.0 collective-permute-done.4.refs_4_
  14.6 0.5 %shard_map.47 = (bf16[16,1664]{1,0:T(8,128)(2,1)S(1)}, bf16[16,1664]{1,0:T(8,128)(2,1)S(1)}, bf16[16,1664]{1,0:T(8,128)(2,1)S(1)}, bf16[16,1664]{1,0:T(8,128)(2,1)S(1)}) custom-call(bf16[32,1536]{1,0:T(8,128)(2,1)S(1)} %get-tuple-element.16.home_ref, bf16[16,1536]{1,0:T(8,128)(2,1)S(1)} %get-tuple-element.17.home_queries_ref, ...), custom_call_target="tpu_custom_call" | custom-call | tf_op jit(solution)/shard_map/pallas_call | solution.py:92
  15.1 1.0 %collective-permute-start.5 = (bf16[16,1664]{1,0:T(8,128)(2,1)S(1)}, bf16[16,1664]{1,0:T(8,128)(2,1)S(1)}, u32[]{:S(2)}, u32[]{:S(2)}) collective-permute-start(bf16[16,1664]{1,0:T(8,128)(2,1)S(1)} %get-tuple-element.21), channel_id=1, source_target_pairs={{0,12},{4,8},{8,4},{12,0},{16,28},{20,24},{24,20},{28,16},{1,21},{... | collective-permute-start | bytes 159752 | tf_op jit(solution)/shard_map/ppermute | solution.py:291
  16.1 0.8 %collective-permute-start.6 = (bf16[16,1664]{1,0:T(8,128)(2,1)S(1)}, bf16[16,1664]{1,0:T(8,128)(2,1)S(1)}, u32[]{:S(2)}, u32[]{:S(2)}) collective-permute-start(bf16[16,1664]{1,0:T(8,128)(2,1)S(1)} %get-tuple-element.22), channel_id=1, source_target_pairs={{0,4},{4,0},{8,12},{12,8},{16,20},{20,16},{24,28},{28,24},{1,5},{5... | collective-permute-start | bytes 159752 | tf_op jit(solution)/shard_map/ppermute | solution.py:291
  16.9 1.8 %collective-permute-start.7 = (bf16[16,1664]{1,0:T(8,128)(2,1)S(1)}, bf16[16,1664]{1,0:T(8,128)(2,1)S(1)}, u32[]{:S(2)}, u32[]{:S(2)}) collective-permute-start(bf16[16,1664]{1,0:T(8,128)(2,1)S(1)} %get-tuple-element.24), channel_id=1, source_target_pairs={{0,8},{4,12},{8,0},{12,4},{16,24},{20,28},{24,16},{28,20},{1,17},{... | collective-permute-start | bytes 159752 | tf_op jit(solution)/shard_map/ppermute | solution.py:291
  18.7 2.1 %collective-permute-done.5.far_ref = bf16[16,1664]{1,0:T(8,128)(2,1)S(1)} collective-permute-done((bf16[16,1664]{1,0:T(8,128)(2,1)S(1)}, bf16[16,1664]{1,0:T(8,128)(2,1)S(1)}, u32[]{:S(2)}, u32[]{:S(2)}) %collective-permute-start.5) | collective-permute-done | bytes 53280 | tf_op jit(solution)/shard_map/ppermute | solution.py:291
  20.8 0.0 collective-permute-done.6.near_ref
  20.8 0.2 shard_map.48.beside_ref
  21.0 0.3 %collective-permute-done.7.far_ref = bf16[16,1664]{1,0:T(8,128)(2,1)S(1)} collective-permute-done((bf16[16,1664]{1,0:T(8,128)(2,1)S(1)}, bf16[16,1664]{1,0:T(8,128)(2,1)S(1)}, u32[]{:S(2)}, u32[]{:S(2)}) %collective-permute-start.7) | collective-permute-done | bytes 53280 | tf_op jit(solution)/shard_map/ppermute | solution.py:291
  21.3 0.8 %shard_map.49 = bf16[16,3072]{1,0:T(8,128)(2,1)} custom-call(bf16[16,1536]{1,0:T(8,128)(2,1)S(1)} %shard_map.48.beside_ref, bf16[16,1664]{1,0:T(8,128)(2,1)S(1)} %get-tuple-element.23.near_ref, bf16[16,1664]{1,0:T(8,128)(2,1)S(1)} %collective-permute-done.7.far_ref), custom_call_target="tpu_custom_call" | custom-call | tf_op jit(solution)/shard_map/pallas_call | solution.py:92
  (2 shorter events, 0.0 us)
Async XLA Ops:
  0.0 11.2 %copy-start = (bf16[128,2,1536]{2,1,0:T(2,128)(2,1)S(1)}, bf16[128,2,1536]{2,1,0:T(2,128)(2,1)}, u32[]{:S(2)}) copy-start(bf16[128,2,1536]{2,1,0:T(2,128)(2,1)} %param.5) | copy-start | bytes 2359300
  0.0 9.6 %collective-permute-start.3 = (bf16[16,3072]{1,0:T(8,128)(2,1)}, bf16[16,3072]{1,0:T(8,128)(2,1)S(1)}, u32[]{:S(2)}, u32[]{:S(2)}) collective-permute-start(bf16[16,3072]{1,0:T(8,128)(2,1)} %queries_hbm.1), channel_id=1, source_target_pairs={{0,8},{4,12},{8,0},{12,4},{16,24},{20,28},{24,16},{28,20},{1,17},{... | collective-permute-start | bytes 294920 | tf_op jit(solution)/shard_map/ppermute | solution.py:291
  4.2 10.4 %collective-permute-start.2 = (bf16[32,1536]{1,0:T(8,128)(2,1)S(1)}, bf16[32,1536]{1,0:T(8,128)(2,1)S(1)}, u32[]{:S(2)}, u32[]{:S(2)}) collective-permute-start(bf16[32,1536]{1,0:T(8,128)(2,1)S(1)} %get-tuple-element.18), channel_id=1, source_target_pairs={{0,4},{4,0},{8,12},{12,8},{16,20},{20,16},{24,28},{28,24},{1,5},{5... | collective-permute-start | bytes 294920 | tf_op jit(solution)/shard_map/ppermute | solution.py:291
  5.8 8.8 %collective-permute-start = (bf16[32,1536]{1,0:T(8,128)(2,1)S(1)}, bf16[32,1536]{1,0:T(8,128)(2,1)S(1)}, u32[]{:S(2)}, u32[]{:S(2)}) collective-permute-start(bf16[32,1536]{1,0:T(8,128)(2,1)S(1)} %get-tuple-element.18), channel_id=1, source_target_pairs={{0,28},{4,24},{8,20},{12,16},{16,12},{20,8},{24,4},{28,0},{1,13},{... | collective-permute-start | bytes 294920 | tf_op jit(solution)/shard_map/ppermute | solution.py:291
  8.2 6.4 %collective-permute-start.1 = (bf16[32,1536]{1,0:T(8,128)(2,1)S(1)}, bf16[32,1536]{1,0:T(8,128)(2,1)S(1)}, u32[]{:S(2)}, u32[]{:S(2)}) collective-permute-start(bf16[32,1536]{1,0:T(8,128)(2,1)S(1)} %get-tuple-element.16.home_ref), channel_id=1, source_target_pairs={{0,24},{4,28},{8,16},{12,20},{16,8},{20,12},{24,0},{28,4},{1,9},{5... | collective-permute-start | bytes 294920 | tf_op jit(solution)/shard_map/ppermute | solution.py:291
  9.6 5.1 %collective-permute-start.4 = (bf16[2,16,1536]{2,1,0:T(8,128)(2,1)S(1)}, bf16[2,16,1536]{2,1,0:T(8,128)(2,1)S(1)}, u32[]{:S(2)}, u32[]{:S(2)}) collective-permute-start(bf16[2,16,1536]{2,1,0:T(8,128)(2,1)S(1)} %pad_maximum_fusion), channel_id=1, source_target_pairs={{0,4},{4,0},{8,12},{12,8},{16,20},{20,16},{24,28},{28,24},{1,5},{5... | collective-permute-start | bytes 294920 | tf_op jit(solution)/shard_map/ppermute | solution.py:291
  15.1 5.7 %collective-permute-start.5 = (bf16[16,1664]{1,0:T(8,128)(2,1)S(1)}, bf16[16,1664]{1,0:T(8,128)(2,1)S(1)}, u32[]{:S(2)}, u32[]{:S(2)}) collective-permute-start(bf16[16,1664]{1,0:T(8,128)(2,1)S(1)} %get-tuple-element.21), channel_id=1, source_target_pairs={{0,12},{4,8},{8,4},{12,0},{16,28},{20,24},{24,20},{28,16},{1,21},{... | collective-permute-start | bytes 159752 | tf_op jit(solution)/shard_map/ppermute | solution.py:291
  16.1 4.7 %collective-permute-start.6 = (bf16[16,1664]{1,0:T(8,128)(2,1)S(1)}, bf16[16,1664]{1,0:T(8,128)(2,1)S(1)}, u32[]{:S(2)}, u32[]{:S(2)}) collective-permute-start(bf16[16,1664]{1,0:T(8,128)(2,1)S(1)} %get-tuple-element.22), channel_id=1, source_target_pairs={{0,4},{4,0},{8,12},{12,8},{16,20},{20,16},{24,28},{28,24},{1,5},{5... | collective-permute-start | bytes 159752 | tf_op jit(solution)/shard_map/ppermute | solution.py:291
  16.9 4.4 %collective-permute-start.7 = (bf16[16,1664]{1,0:T(8,128)(2,1)S(1)}, bf16[16,1664]{1,0:T(8,128)(2,1)S(1)}, u32[]{:S(2)}, u32[]{:S(2)}) collective-permute-start(bf16[16,1664]{1,0:T(8,128)(2,1)S(1)} %get-tuple-element.24), channel_id=1, source_target_pairs={{0,8},{4,12},{8,0},{12,4},{16,24},{20,28},{24,16},{28,20},{1,17},{... | collective-permute-start | bytes 159752 | tf_op jit(solution)/shard_map/ppermute | solution.py:291

commit v12 on v9

--- a/solution.py
+++ b/solution.py
@@ -13,7 +13,7 @@
 KERNEL_VMEM = 8 << 20
 BOTH = ("patch", "uly")
 SPLIT_TERMS = 3
-KEY_VALUE_ORDER = (3, 2, 1)
+KEY_VALUE_ORDER = (3, 1, 2)
 KEY, QUERY = 0, 1
 FAR_QUERY_PARITY = 1
 

time: 22.3 us -> 22.3 us (level)
  no operation moved by 1% of the time
where the time goes in v12:
time: 22.3 us; the launch traced here: 22.2 us
  starting transfers between devices  13.5 us (61%)
  waiting for transfers between devices  5.8 us (26%)
  Pallas kernels  2.71 us (12%)
    ppermute x8, starting transfers between devices, swap(): return lax.ppermute(array, (*BOTH, 'rep'), pairs)  13.5 us
    ppermute x8, waiting for transfers between devices, swap(): return lax.ppermute(array, (*BOTH, 'rep'), pairs)  5.8 us
    pallas_call x4, Pallas kernels, kernel_call(): pl.pallas_call(body, out_shape=[jax.ShapeDtypeStruct(shape, jnp.bfloat16)...  2.71 us
  transfers between devices with their start and end apart: 8, of which 3 were waited for; matrix products, arithmetic and copies ran while one was open for 0% of the time, Pallas kernels for 6%

profile of v12, /device:TPU:0, one launch (start us, length us, event | category | flops | bytes accessed | tf_op | source)
XLA Modules:
  0.0 22.2 jit_solution(3776893330502719235)
XLA Ops:
  0.0 0.0 copy-start
  0.0 3.0 %collective-permute-start.3 = (bf16[16,3072]{1,0:T(8,128)(2,1)}, bf16[16,3072]{1,0:T(8,128)(2,1)S(1)}, u32[]{:S(2)}, u32[]{:S(2)}) collective-permute-start(bf16[16,3072]{1,0:T(8,128)(2,1)} %queries_hbm.1), channel_id=1, source_target_pairs={{0,8},{4,12},{8,0},{12,4},{16,24},{20,28},{24,16},{28,20},{1,17},{... | collective-permute-start | bytes 294920 | tf_op jit(solution)/shard_map/ppermute | solution.py:291
  3.0 1.2 %shard_map.46 = (bf16[32,1536]{1,0:T(8,128)(2,1)S(1)}, bf16[32,1536]{1,0:T(8,128)(2,1)S(1)}, bf16[16,1536]{1,0:T(8,128)(2,1)S(1)}, bf16[16,1536]{1,0:T(8,128)(2,1)S(1)}) custom-call(bf16[16,3072]{1,0:T(8,128)(2,1)} %queries_hbm.1, s32[16,2,3072]{2,1,0:T(2,128)} %codes_hbm.1, s32[16,2,24]{2,1,0:T(2,128)} %exps_hbm.1), custom_call_target="tpu_custom_call" | custom-call | tf_op jit(solution)/shard_map/pallas_call | solution.py:92
  4.2 1.6 %collective-permute-start.1 = (bf16[32,1536]{1,0:T(8,128)(2,1)S(1)}, bf16[32,1536]{1,0:T(8,128)(2,1)S(1)}, u32[]{:S(2)}, u32[]{:S(2)}) collective-permute-start(bf16[32,1536]{1,0:T(8,128)(2,1)S(1)} %get-tuple-element.18), channel_id=1, source_target_pairs={{0,4},{4,0},{8,12},{12,8},{16,20},{20,16},{24,28},{28,24},{1,5},{5... | collective-permute-start | bytes 294920 | tf_op jit(solution)/shard_map/ppermute | solution.py:291
  5.8 2.4 %collective-permute-start = (bf16[32,1536]{1,0:T(8,128)(2,1)S(1)}, bf16[32,1536]{1,0:T(8,128)(2,1)S(1)}, u32[]{:S(2)}, u32[]{:S(2)}) collective-permute-start(bf16[32,1536]{1,0:T(8,128)(2,1)S(1)} %get-tuple-element.18), channel_id=1, source_target_pairs={{0,28},{4,24},{8,20},{12,16},{16,12},{20,8},{24,4},{28,0},{1,13},{... | collective-permute-start | bytes 294920 | tf_op jit(solution)/shard_map/ppermute | solution.py:291
  8.2 1.3 %collective-permute-start.2 = (bf16[32,1536]{1,0:T(8,128)(2,1)S(1)}, bf16[32,1536]{1,0:T(8,128)(2,1)S(1)}, u32[]{:S(2)}, u32[]{:S(2)}) collective-permute-start(bf16[32,1536]{1,0:T(8,128)(2,1)S(1)} %get-tuple-element.16.home_ref), channel_id=1, source_target_pairs={{0,24},{4,28},{8,16},{12,20},{16,8},{20,12},{24,0},{28,4},{1,9},{5... | collective-permute-start | bytes 294920 | tf_op jit(solution)/shard_map/ppermute | solution.py:291
  9.6 0.0 collective-permute-done.3.refs_3_
  9.6 1.6 %collective-permute-start.4 = (bf16[2,16,1536]{2,1,0:T(8,128)(2,1)S(1)}, bf16[2,16,1536]{2,1,0:T(8,128)(2,1)S(1)}, u32[]{:S(2)}, u32[]{:S(2)}) collective-permute-start(bf16[2,16,1536]{2,1,0:T(8,128)(2,1)S(1)} %pad_maximum_fusion), channel_id=1, source_target_pairs={{0,4},{4,0},{8,12},{12,8},{16,20},{20,16},{24,28},{28,24},{1,5},{5... | collective-permute-start | bytes 294920 | tf_op jit(solution)/shard_map/ppermute | solution.py:291
  11.2 0.0 copy-done
  11.2 0.1 copy.7
  11.3 3.4 %collective-permute-done.2.refs_2_ = bf16[32,1536]{1,0:T(8,128)(2,1)S(1)} collective-permute-done((bf16[32,1536]{1,0:T(8,128)(2,1)S(1)}, bf16[32,1536]{1,0:T(8,128)(2,1)S(1)}, u32[]{:S(2)}, u32[]{:S(2)}) %collective-permute-start.2) | collective-permute-done | bytes 98336 | tf_op jit(solution)/shard_map/ppermute | solution.py:291
  14.6 0.0 collective-permute-done.1.refs_1_
  14.6 0.0 collective-permute-done.refs_0_
  14.7 0.0 collective-permute-done.4.refs_4_
  14.7 0.5 %shard_map.47 = (bf16[16,1664]{1,0:T(8,128)(2,1)S(1)}, bf16[16,1664]{1,0:T(8,128)(2,1)S(1)}, bf16[16,1664]{1,0:T(8,128)(2,1)S(1)}, bf16[16,1664]{1,0:T(8,128)(2,1)S(1)}) custom-call(bf16[32,1536]{1,0:T(8,128)(2,1)S(1)} %get-tuple-element.16.home_ref, bf16[16,1536]{1,0:T(8,128)(2,1)S(1)} %get-tuple-element.17.home_queries_ref, ...), custom_call_target="tpu_custom_call" | custom-call | tf_op jit(solution)/shard_map/pallas_call | solution.py:92
  15.1 1.0 %collective-permute-start.5 = (bf16[16,1664]{1,0:T(8,128)(2,1)S(1)}, bf16[16,1664]{1,0:T(8,128)(2,1)S(1)}, u32[]{:S(2)}, u32[]{:S(2)}) collective-permute-start(bf16[16,1664]{1,0:T(8,128)(2,1)S(1)} %get-tuple-element.21), channel_id=1, source_target_pairs={{0,12},{4,8},{8,4},{12,0},{16,28},{20,24},{24,20},{28,16},{1,21},{... | collective-permute-start | bytes 159752 | tf_op jit(solution)/shard_map/ppermute | solution.py:291
  16.1 0.8 %collective-permute-start.6 = (bf16[16,1664]{1,0:T(8,128)(2,1)S(1)}, bf16[16,1664]{1,0:T(8,128)(2,1)S(1)}, u32[]{:S(2)}, u32[]{:S(2)}) collective-permute-start(bf16[16,1664]{1,0:T(8,128)(2,1)S(1)} %get-tuple-element.22), channel_id=1, source_target_pairs={{0,4},{4,0},{8,12},{12,8},{16,20},{20,16},{24,28},{28,24},{1,5},{5... | collective-permute-start | bytes 159752 | tf_op jit(solution)/shard_map/ppermute | solution.py:291
  16.9 1.8 %collective-permute-start.7 = (bf16[16,1664]{1,0:T(8,128)(2,1)S(1)}, bf16[16,1664]{1,0:T(8,128)(2,1)S(1)}, u32[]{:S(2)}, u32[]{:S(2)}) collective-permute-start(bf16[16,1664]{1,0:T(8,128)(2,1)S(1)} %get-tuple-element.24), channel_id=1, source_target_pairs={{0,8},{4,12},{8,0},{12,4},{16,24},{20,28},{24,16},{28,20},{1,17},{... | collective-permute-start | bytes 159752 | tf_op jit(solution)/shard_map/ppermute | solution.py:291
  18.7 2.1 %collective-permute-done.5.far_ref = bf16[16,1664]{1,0:T(8,128)(2,1)S(1)} collective-permute-done((bf16[16,1664]{1,0:T(8,128)(2,1)S(1)}, bf16[16,1664]{1,0:T(8,128)(2,1)S(1)}, u32[]{:S(2)}, u32[]{:S(2)}) %collective-permute-start.5) | collective-permute-done | bytes 53280 | tf_op jit(solution)/shard_map/ppermute | solution.py:291
  20.8 0.0 collective-permute-done.6.near_ref
  20.8 0.2 shard_map.48.beside_ref
  21.0 0.3 %collective-permute-done.7.far_ref = bf16[16,1664]{1,0:T(8,128)(2,1)S(1)} collective-permute-done((bf16[16,1664]{1,0:T(8,128)(2,1)S(1)}, bf16[16,1664]{1,0:T(8,128)(2,1)S(1)}, u32[]{:S(2)}, u32[]{:S(2)}) %collective-permute-start.7) | collective-permute-done | bytes 53280 | tf_op jit(solution)/shard_map/ppermute | solution.py:291
  21.3 0.8 %shard_map.49 = bf16[16,3072]{1,0:T(8,128)(2,1)} custom-call(bf16[16,1536]{1,0:T(8,128)(2,1)S(1)} %shard_map.48.beside_ref, bf16[16,1664]{1,0:T(8,128)(2,1)S(1)} %get-tuple-element.23.near_ref, bf16[16,1664]{1,0:T(8,128)(2,1)S(1)} %collective-permute-done.7.far_ref), custom_call_target="tpu_custom_call" | custom-call | tf_op jit(solution)/shard_map/pallas_call | solution.py:92
  (2 shorter events, 0.0 us)
Async XLA Ops:
  0.0 11.2 %copy-start = (bf16[128,2,1536]{2,1,0:T(2,128)(2,1)S(1)}, bf16[128,2,1536]{2,1,0:T(2,128)(2,1)}, u32[]{:S(2)}) copy-start(bf16[128,2,1536]{2,1,0:T(2,128)(2,1)} %param.5) | copy-start | bytes 2359300
  0.0 9.6 %collective-permute-start.3 = (bf16[16,3072]{1,0:T(8,128)(2,1)}, bf16[16,3072]{1,0:T(8,128)(2,1)S(1)}, u32[]{:S(2)}, u32[]{:S(2)}) collective-permute-start(bf16[16,3072]{1,0:T(8,128)(2,1)} %queries_hbm.1), channel_id=1, source_target_pairs={{0,8},{4,12},{8,0},{12,4},{16,24},{20,28},{24,16},{28,20},{1,17},{... | collective-permute-start | bytes 294920 | tf_op jit(solution)/shard_map/ppermute | solution.py:291
  4.2 10.4 %collective-permute-start.1 = (bf16[32,1536]{1,0:T(8,128)(2,1)S(1)}, bf16[32,1536]{1,0:T(8,128)(2,1)S(1)}, u32[]{:S(2)}, u32[]{:S(2)}) collective-permute-start(bf16[32,1536]{1,0:T(8,128)(2,1)S(1)} %get-tuple-element.18), channel_id=1, source_target_pairs={{0,4},{4,0},{8,12},{12,8},{16,20},{20,16},{24,28},{28,24},{1,5},{5... | collective-permute-start | bytes 294920 | tf_op jit(solution)/shard_map/ppermute | solution.py:291
  5.8 8.8 %collective-permute-start = (bf16[32,1536]{1,0:T(8,128)(2,1)S(1)}, bf16[32,1536]{1,0:T(8,128)(2,1)S(1)}, u32[]{:S(2)}, u32[]{:S(2)}) collective-permute-start(bf16[32,1536]{1,0:T(8,128)(2,1)S(1)} %get-tuple-element.18), channel_id=1, source_target_pairs={{0,28},{4,24},{8,20},{12,16},{16,12},{20,8},{24,4},{28,0},{1,13},{... | collective-permute-start | bytes 294920 | tf_op jit(solution)/shard_map/ppermute | solution.py:291
  8.2 6.4 %collective-permute-start.2 = (bf16[32,1536]{1,0:T(8,128)(2,1)S(1)}, bf16[32,1536]{1,0:T(8,128)(2,1)S(1)}, u32[]{:S(2)}, u32[]{:S(2)}) collective-permute-start(bf16[32,1536]{1,0:T(8,128)(2,1)S(1)} %get-tuple-element.16.home_ref), channel_id=1, source_target_pairs={{0,24},{4,28},{8,16},{12,20},{16,8},{20,12},{24,0},{28,4},{1,9},{5... | collective-permute-start | bytes 294920 | tf_op jit(solution)/shard_map/ppermute | solution.py:291
  9.6 5.1 %collective-permute-start.4 = (bf16[2,16,1536]{2,1,0:T(8,128)(2,1)S(1)}, bf16[2,16,1536]{2,1,0:T(8,128)(2,1)S(1)}, u32[]{:S(2)}, u32[]{:S(2)}) collective-permute-start(bf16[2,16,1536]{2,1,0:T(8,128)(2,1)S(1)} %pad_maximum_fusion), channel_id=1, source_target_pairs={{0,4},{4,0},{8,12},{12,8},{16,20},{20,16},{24,28},{28,24},{1,5},{5... | collective-permute-start | bytes 294920 | tf_op jit(solution)/shard_map/ppermute | solution.py:291
  15.1 5.7 %collective-permute-start.5 = (bf16[16,1664]{1,0:T(8,128)(2,1)S(1)}, bf16[16,1664]{1,0:T(8,128)(2,1)S(1)}, u32[]{:S(2)}, u32[]{:S(2)}) collective-permute-start(bf16[16,1664]{1,0:T(8,128)(2,1)S(1)} %get-tuple-element.21), channel_id=1, source_target_pairs={{0,12},{4,8},{8,4},{12,0},{16,28},{20,24},{24,20},{28,16},{1,21},{... | collective-permute-start | bytes 159752 | tf_op jit(solution)/shard_map/ppermute | solution.py:291
  16.1 4.7 %collective-permute-start.6 = (bf16[16,1664]{1,0:T(8,128)(2,1)S(1)}, bf16[16,1664]{1,0:T(8,128)(2,1)S(1)}, u32[]{:S(2)}, u32[]{:S(2)}) collective-permute-start(bf16[16,1664]{1,0:T(8,128)(2,1)S(1)} %get-tuple-element.22), channel_id=1, source_target_pairs={{0,4},{4,0},{8,12},{12,8},{16,20},{20,16},{24,28},{28,24},{1,5},{5... | collective-permute-start | bytes 159752 | tf_op jit(solution)/shard_map/ppermute | solution.py:291
  16.9 4.4 %collective-permute-start.7 = (bf16[16,1664]{1,0:T(8,128)(2,1)S(1)}, bf16[16,1664]{1,0:T(8,128)(2,1)S(1)}, u32[]{:S(2)}, u32[]{:S(2)}) collective-permute-start(bf16[16,1664]{1,0:T(8,128)(2,1)S(1)} %get-tuple-element.24), channel_id=1, source_target_pairs={{0,8},{4,12},{8,0},{12,4},{16,24},{20,28},{24,16},{28,20},{1,17},{... | collective-permute-start | bytes 159752 | tf_op jit(solution)/shard_map/ppermute | solution.py:291
